TPU v7x, 32 devices: a whole 2x2x4 slice. The times are simulated.
32 devices in a mesh: seq: 4 (over z), mp: 4 (over y, x), req: 2 (over core).
Axes of the slice: x: 2, y: 2, z: 4, core: 2. Of those that a mesh axis runs over, the one named last changes fastest.
Arguments:
- hidden: bfloat16 [2, 1024, 3072], P('req', 'seq', 'mp'), may hold values from -6 to 6
- norm_gain: bfloat16 [3072], replicated, may hold values from 0.5 to 1.5
- w_query: bfloat16 [3072, 1024], P(None, 'mp'), may hold values from -0.109375 to 0.109375
- w_keyval: bfloat16 [3072, 512], P(None, 'mp'), may hold values from -0.109375 to 0.109375
- w_attn_out: bfloat16 [1024, 3072], P('mp'), may hold values from -1.5 to 1.5
- w_inner: bfloat16 [3072, 2, 1536], P(None, None, 'mp'), may hold values from -0.109375 to 0.109375
- w_bc: bfloat16 [3072, 512], P(None, 'mp'), may hold values from -0.109375 to 0.109375
- w_dt: bfloat16 [3072, 12], P(None, 'mp'), may hold values from -0.109375 to 0.109375
- dt_bias: float32 [12], P('mp'), may hold values from -4 to 0
- a_log: float32 [12], P('mp'), may hold values from -12 to 0
- d_skip: float32 [12], P('mp'), may hold values from 0.1 to 10
- conv_x: bfloat16 [4, 1536], P(None, 'mp'), may hold values from -3 to 3
- conv_bc: bfloat16 [4, 512], replicated, may hold values from -3 to 3
- mamba_gain: bfloat16 [1536], P('mp'), may hold values from 0.5 to 1.5
- w_mamba_out: bfloat16 [1536, 3072], P('mp'), may hold values from -0.15625 to 0.15625
- cache: bfloat16 [2, 1024, 512], P('req', 'seq', 'mp'), may hold values from -70 to 70, as said below
- cache_len: int32 [2], P('req'), may hold values from 256 to 1024
- tail_x: bfloat16 [2, 3, 1536], P('req', None, 'mp'), may hold values from -6 to 6
- tail_bc: bfloat16 [2, 3, 512], P('req'), may hold values from -6 to 6
- ssm_init: float32 [2, 12, 128, 256], P('req', 'mp'), may hold values from -6 to 6
Outputs:
- layer_out: bfloat16 [2, 1024, 3072], P('req', 'seq', 'mp')
- new_keyval: bfloat16 [2, 1024, 512], P('req', 'seq', 'mp')
- block_states: float32 [2, 4, 12, 128, 256], P('req', 'seq', 'mp')
Inputs may be any that keep to these rules, and one draw needn't show every extreme that they name: Rows of the cache at or past cache_len are unused.
All inputs are finite; a program needn't handle non-finite values.
Results may differ from a plain program's by a relative error of at most 0.0097.
Values may be sent and summed in bfloat16 or wider, within the bound.
No kernel may reach another device: no remote copies, remote signals or barrier semaphores. Data moves between devices by JAX's collectives and lax.ppermute only.
A program may use at most 192 MiB of HBM per device.

v0:
```python
import jax
import jax.numpy as jnp
from jax import lax
from jax.sharding import PartitionSpec as P

HD = 128
QH = 8
KVH = 2
NS = 256
CONV = 4


epsilon = 1e-05
rope_base = 100000000000.0
negative = -1e30


def shifted(block, axis, distance):
    devices = range(lax.axis_size(axis))
    route = [(i - distance, i) for i in devices if i - distance in devices]
    return lax.ppermute(block, axis, route)


def prefix(part, axis, combine, identity):
    place = lax.axis_index(axis)
    gathered = jax.tree.map(lambda a: lax.all_gather(a, axis), part)
    state = jax.tree.map(lambda a, e: jnp.zeros_like(a) + jnp.asarray(e, a.dtype), part, identity)

    def one(turn, state):
        return combine(
            state, jax.tree.map(lambda a: lax.dynamic_index_in_dim(a, turn, 0, False), gathered)
        )

    return lax.fori_loop(0, place, one, state)


def rotate(values, positions):
    half = HD // 2
    freqs = rope_base ** (-jnp.arange(half, dtype=jnp.float32) * 2.0 / HD)
    angles = positions.astype(jnp.float32)[:, None] * freqs[None, :]
    cosine = jnp.cos(angles)[:, None, :]
    sine = jnp.sin(angles)[:, None, :]
    first = values[..., :half]
    second = values[..., half:]
    return jnp.concatenate(
        [first * cosine - second * sine, second * cosine + first * sine], axis=-1
    )


def rms_scale(values):
    mean_sq = jnp.mean(values * values, axis=-1, keepdims=True)
    return values * lax.rsqrt(mean_sq + epsilon)


def causal_conv(tail, inputs, taps):
    padded = jnp.concatenate([tail, inputs], axis=0).astype(jnp.float32)
    count = inputs.shape[0]
    total = jnp.zeros(inputs.shape, jnp.float32)
    for offset in range(CONV):
        total = total + taps[offset].astype(jnp.float32)[None, :] * padded[offset : offset + count]
    return jax.nn.silu(total)


def join_states(earlier, later):
    return (earlier[0] * later[0], later[0][:, None, None] * earlier[1] + later[1])


def shards(
    hidden,
    norm_gain,
    w_query,
    w_keyval,
    w_attn_out,
    w_inner,
    w_bc,
    w_dt,
    dt_bias,
    a_log,
    d_skip,
    conv_x,
    conv_bc,
    mamba_gain,
    w_mamba_out,
    cache,
    cache_len,
    tail_x,
    tail_bc,
    ssm_init,
):
    high = lax.Precision.HIGHEST
    own_rows = hidden[0]
    tokens = own_rows.shape[0]
    seq_pos = lax.axis_index("seq")
    mp_pos = lax.axis_index("mp")
    length = cache_len[0]
    whole = lax.all_gather(own_rows, "mp", axis=1, tiled=True)
    normed = (rms_scale(whole.astype(jnp.float32)) * norm_gain.astype(jnp.float32)).astype(
        jnp.bfloat16
    )
    positions = length + seq_pos * tokens + jnp.arange(tokens, dtype=jnp.int32)
    local_heads = w_query.shape[1] // HD
    query = rotate(
        jnp.dot(normed, w_query, preferred_element_type=jnp.float32).reshape(
            tokens, local_heads, HD
        ),
        positions,
    ).astype(jnp.bfloat16)
    projected = jnp.dot(normed, w_keyval, preferred_element_type=jnp.float32)
    roped = rotate(projected[:, None, :], positions)[:, 0, :]
    kv_block = jnp.where(mp_pos % 2 == 0, roped, projected).astype(jnp.bfloat16)
    bc_block = jnp.dot(normed, w_bc, preferred_element_type=jnp.float32).astype(jnp.bfloat16)
    kv_all, bc_all, cache_all = (
        lax.all_gather(kv_block, "mp", axis=1, tiled=True),
        lax.all_gather(bc_block, "mp", axis=1, tiled=True),
        lax.all_gather(cache[0], "mp", axis=1, tiled=True),
    )
    inner = jnp.einsum("td,dkc->tkc", normed, w_inner, preferred_element_type=jnp.float32).astype(
        jnp.bfloat16
    )
    rim = CONV - 1
    prev_x, prev_bc = shifted((inner[tokens - rim :, 1], bc_all[tokens - rim :]), "seq", 1)
    first_block = seq_pos == 0
    prev_x = jnp.where(first_block, tail_x[0], prev_x)
    prev_bc = jnp.where(first_block, tail_bc[0], prev_bc)
    mamba_heads = dt_bias.shape[0]
    x_conv = causal_conv(prev_x, inner[:, 1], conv_x).reshape(tokens, mamba_heads, HD)
    bc_conv = causal_conv(prev_bc, bc_all, conv_bc)
    b_mat = bc_conv[:, :NS]
    c_mat = bc_conv[:, NS:]
    step_size = jax.nn.softplus(jnp.dot(normed, w_dt, preferred_element_type=jnp.float32) + dt_bias)
    log_decay = -step_size * jnp.exp(a_log)[None, :]
    cumulative = jnp.cumsum(log_decay, axis=0)
    pairs = jnp.dot(c_mat, b_mat.T, precision=high)
    gap = cumulative[:, None, :] - cumulative[None, :, :]
    token_ids = jnp.arange(tokens)
    lower = (token_ids[:, None] >= token_ids[None, :])[:, :, None]
    decay = jnp.where(lower, jnp.exp(jnp.where(lower, gap, 0.0)), 0.0)
    mixing = decay * pairs[:, :, None] * step_size[None, :, :]
    inner_out = jnp.einsum("tsh,shp->thp", mixing, x_conv, precision=high)
    to_end = jnp.exp(cumulative[-1][None, :] - cumulative) * step_size
    own_state = jnp.einsum("sh,shp,sn->hpn", to_end, x_conv, b_mat, precision=high)
    block_decay = jnp.exp(cumulative[-1])
    prior_decay, prior_state = prefix(
        (block_decay, own_state),
        "seq",
        join_states,
        (jnp.ones_like(block_decay), jnp.zeros_like(own_state)),
    )
    incoming = prior_state + prior_decay[:, None, None] * ssm_init[0]
    carried = jnp.exp(cumulative)[:, :, None] * jnp.einsum(
        "tn,hpn->thp", c_mat, incoming, precision=high
    )
    mamba_y = inner_out + carried + d_skip[None, :, None] * x_conv
    state_after = block_decay[:, None, None] * incoming + own_state
    gated = mamba_y * jax.nn.silu(inner[:, 0].astype(jnp.float32).reshape(tokens, mamba_heads, HD))
    mixed = (
        rms_scale(gated).reshape(tokens, mamba_heads * HD) * mamba_gain.astype(jnp.float32)
    ).astype(jnp.bfloat16)
    cache_rows = cache_all.shape[0]
    shard_rows = cache_rows + tokens
    local_rows = jnp.concatenate([cache_all, kv_all], axis=0)
    group = mp_pos * local_heads // (QH // KVH)
    query_index = seq_pos * tokens + jnp.arange(tokens, dtype=jnp.int32)
    scale = 1.0 / float(HD) ** 0.5
    piece = lax.all_gather(local_rows, "seq", axis=0, tiled=True)
    top = jnp.full((local_heads, tokens), negative, jnp.float32)
    piece = lax.dynamic_slice_in_dim(piece, group * 2 * HD, 2 * HD, 1)
    count = piece.shape[0]
    index = jnp.arange(count, dtype=jnp.int32)
    owner = index // shard_rows
    offset = index % shard_rows
    in_cache = offset < cache_rows
    slot_ok = in_cache & (owner * cache_rows + offset < length)
    new_index = owner * tokens + offset - cache_rows
    valid = slot_ok[None, :] | (~in_cache)[None, :] & (new_index[None, :] <= query_index[:, None])
    scores = (
        jnp.einsum("qhd,kd->hqk", query, piece[:, :HD], preferred_element_type=jnp.float32) * scale
    )
    masked = jnp.where(valid[None], scores, negative)
    new_top = jnp.maximum(top, jnp.max(masked, axis=-1))
    weights = jnp.where(valid[None], jnp.exp(masked - new_top[:, :, None]), 0.0)
    total = jnp.sum(weights, axis=-1)
    accum = jnp.einsum(
        "hqk,kd->hqd",
        weights.astype(jnp.bfloat16),
        piece[:, HD : 2 * HD],
        preferred_element_type=jnp.float32,
    )
    top, total, accum = (new_top, total, accum)
    attended = jnp.transpose(accum / total[:, :, None], (1, 0, 2)).reshape(tokens, local_heads * HD)
    attended = attended.astype(jnp.bfloat16)
    term = jnp.dot(attended, w_attn_out, preferred_element_type=jnp.float32)
    term = term + jnp.dot(mixed, w_mamba_out, preferred_element_type=jnp.float32)
    summed = lax.psum_scatter(term, "mp", scatter_dimension=1, tiled=True)
    layer = (summed + own_rows.astype(jnp.float32)).astype(jnp.bfloat16)
    return (layer[None], kv_block[None], state_after[None, None])


def solution(mesh):
    placed = (
        P("req", "seq", "mp"),
        P(),
        P(None, "mp"),
        P(None, "mp"),
        P("mp", None),
        P(None, None, "mp"),
        P(None, "mp"),
        P(None, "mp"),
        P("mp"),
        P("mp"),
        P("mp"),
        P(None, "mp"),
        P(),
        P("mp"),
        P("mp", None),
        P("req", "seq", "mp"),
        P("req"),
        P("req", None, "mp"),
        P("req", None, None),
        P("req", "mp", None, None),
    )
    return jax.shard_map(
        shards,
        mesh=mesh,
        in_specs=placed,
        out_specs=(P("req", "seq", "mp"), P("req", "seq", "mp"), P("req", "seq", "mp", None, None)),
        check_vma=False,
    )
```

profile of v0, /device:TPU:0, one launch (start us, length us, event | category | flops | bytes accessed | tf_op | source)
XLA Modules:
  0.0 219.0 jit_solution(850070632366076051)
XLA Ops:
  12.2 12.1 %all-gather = bf16[1,256,512]{1,2,0:T(8,128)(2,1)} all-gather(bf16[1,256,128]{1,2,0:T(8,128)(2,1)S(1)} %copy.48), channel_id=2, replica_groups=mesh['seq'=4,'mp'=4,'req'=2] {'mp'}, dimensions={2}, use_global_device_ids=true | all-gather | bytes 327680 | tf_op jit(solution)/shard_map/all_gather | solution.py:115
  28.4 15.8 %all-gather.10.cloned.1.call-done = bf16[1,256,3072]{2,1,0:T(8,128)(2,1)} async-done(((bf16[1,256,768]{2,1,0:T(8,128)(2,1)}), bf16[1,256,3072]{2,1,0:T(8,128)(2,1)}) %all-gather.10.cloned.1.call-update) | async-done | bytes 1572880 | tf_op jit(solution)/shard_map/all_gather | solution.py:96
  44.2 1.9 fusion.3
  46.1 1.9 fusion.5
  53.0 3.4 %collective-permute-start = (bf16[3,384]{1,0:T(4,128)(2,1)S(1)}, bf16[3,384]{1,0:T(4,128)(2,1)S(1)}, u32[]{:S(2)}, u32[]{:S(2)}) collective-permute-start(bf16[3,384]{1,0:T(4,128)(2,1)S(1)} %slice_bitcast_fusion.1), channel_id=1, source_target_pairs={{0,8},{8,16},{16,24},{1,9},{9,17},{17,25},{2,10},{10,18},{18,26},{... | collective-permute-start | bytes 6920 | tf_op jit(solution)/shard_map/ppermute | solution.py:21
  56.4 2.0 convolution_convert_fusion
  58.4 9.1 %all_gather.29 = bf16[256,512]{1,0:T(8,128)(2,1)S(1)} all-gather(bf16[256,128]{1,0:T(8,128)(2,1)S(1)} %convolution_convert_fusion), channel_id=1, replica_groups=mesh['seq'=4,'mp'=4,'req'=2] {'mp'}, dimensions={1}, use_global_device_ids=true | all-gather | bytes 327680 | tf_op jit(solution)/shard_map/all_gather | solution.py:114
  67.5 3.4 %collective-permute-start.1 = (bf16[3,512]{1,0:T(4,128)(2,1)S(1)}, bf16[3,512]{1,0:T(4,128)(2,1)S(1)}, u32[]{:S(2)}, u32[]{:S(2)}) collective-permute-start(bf16[3,512]{1,0:T(4,128)(2,1)S(1)} %slice.136), channel_id=1, source_target_pairs={{0,8},{8,16},{16,24},{1,9},{9,17},{17,25},{2,10},{10,18},{18,26},{... | collective-permute-start | bytes 9224 | tf_op jit(solution)/shard_map/ppermute | solution.py:21
  76.8 1.9 multiply_cosine_fusion
  78.7 3.8 %and_or_fusion = pred[256,2048]{0,1:T(8,128)(4,1)} fusion(s32[256]{0:T(256)} %iota_add_fusion, s32[2048]{0:T(1024)S(1)} %fusion.82, pred[2048]{0:T(1024)(128)(4,1)} %get-tuple-element.92, pred[2048]{0:T(1024)(128)(4,1)} %get-tuple-element.91), kind=kLoop, calls=%fused_computation.17 | loop fusion | flops 1572864 | bytes 537600 | tf_op jit(solution)/shard_map/or | solution.py:175
  82.5 9.8 %all-gather.3 = f32[4,1,3]{2,1,0:T(1,128)S(1)} all-gather(f32[1,1,3]{2,1,0:T(1,128)} %bitcast.175), channel_id=1, replica_groups=mesh['seq'=4,'mp'=4,'req'=2] {'seq'}, dimensions={0}, use_global_device_ids=true | all-gather | bytes 60 | tf_op jit(solution)/shard_map/all_gather | solution.py:26
  92.2 1.9 copy.57
  94.2 2.6 %fusion.101 = f32[256,256]{0,1:T(8,128)S(1)} fusion(bf16[256,3072]{1,0:T(8,128)(2,1)} %copy-done.1, bf16[3072,256]{1,0:T(8,128)(2,1)} %param.24), kind=kOutput, calls=%fused_computation.164 | convolution fusion | flops 402653184 | bytes 3407872 | tf_op jit(solution)/shard_map/dot_general | solution.py:103
  99.4 2.3 %fusion.100 = f32[256,128]{0,1:T(8,128)S(1)} fusion(bf16[256,3072]{1,0:T(8,128)(2,1)} %copy-done.1, bf16[3072,128]{1,0:T(8,128)(2,1)} %param.25), kind=kOutput, calls=%fused_computation.163 | convolution fusion | flops 201326592 | bytes 2490368 | tf_op jit(solution)/shard_map/dot_general | solution.py:108
  102.0 7.9 %all_gather.27 = bf16[256,512]{0,1:T(8,128)(2,1)S(1)} all-gather(bf16[256,128]{0,1:T(8,128)(2,1)S(1)} %fusion.63), channel_id=1, replica_groups=mesh['seq'=4,'mp'=4,'req'=2] {'mp'}, dimensions={1}, use_global_device_ids=true | all-gather | bytes 327680 | tf_op jit(solution)/shard_map/all_gather | solution.py:113
  110.8 1.8 subtract_convert_fusion
  115.7 2.6 %multiply_reduce_fusion = (f32[256,3]{0,1:T(4,128)S(1)}, f32[256,3,128]{0,2,1:T(8,128)S(1)}) fusion(f32[256,3,128]{0,2,1:T(8,128)} %bitcast.164, f32[256,3,128]{0,2,1:T(8,128)} %bitcast.159, f32[3]{0:T(128)S(1)} %copy-done.20, f32[256,3,128]{0,2,1:T(8,128)S(1)} %convolution_multiply_fusion, f32[256,3]{0,1:T(4,128)S(1)} %copy-done.14, ...), kind=kOutput, calls=%fused_computation.63 | convolution fusion | flops 303955200 | bytes 1909772 | tf_op jit(solution)/shard_map/tsh,shp->thp/dot_general | solution.py:139
  118.4 40.4 %all-gather.8.cloned.1.call-done = bf16[2048,512]{0,1:T(8,128)(2,1)} async-done(((bf16[512,512]{0,1:T(8,128)(2,1)}), bf16[2048,512]{0,1:T(8,128)(2,1)}) %all-gather.8.cloned.1.call-update) | async-done | bytes 2097168 | tf_op jit(solution)/shard_map/all_gather | solution.py:165
  158.9 2.0 fusion.2
  162.0 2.3 %fusion.26 = bf16[256,2,128]{0,2,1:T(8,128)(2,1)S(1)} fusion(f32[2048,256,2]{1,0,2:T(8,128)S(1)} %get-tuple-element.86, f32[2,256]{1,0:T(2,128)S(1)} %broadcast_maximum_fusion, pred[256,2048]{0,1:T(8,128)(4,1)S(1)} %copy-done.3, bf16[2048,512]{0,1:T(8,128)(2,1)} %all-gather.8.cloned.1.call-done, s32[]{:T(128)S(6)} %add.229, f32[256,2]{0,1:T(2,128)S(1)} %bitcast.174), kind=kOutput, calls=%fused_computation.29 | convolution fusion | flops 273809408 | bytes 5378052 | tf_op jit(solution)/shard_map/hqk,kd->hqd/dot_general | solution.py:183
  164.9 2.7 %convolution_add_fusion = f32[256,3072]{1,0:T(8,128)} fusion(f32[256,3072]{1,0:T(8,128)S(1)} %fusion.102, bf16[256,384]{0,1:T(8,128)(2,1)S(1)} %fusion.44, bf16[384,3072]{1,0:T(8,128)(2,1)S(1)} %copy-done), kind=kOutput, calls=%fused_computation.6 | convolution fusion | flops 604766208 | bytes 8847360 | tf_op jit(solution)/shard_map/dot_general | solution.py:193
  169.0 1.9 add_bitcast_fusion
  170.9 39.6 %reduce-scatter.2.cloned.1.call-done = f32[256,768]{1,0:T(8,128)} async-done(((f32[256,3072]{1,0:T(8,128)}), f32[256,768]{1,0:T(8,128)}) %reduce-scatter.2.cloned.1.call-update) | async-done | bytes 786448 | tf_op jit(solution)/shard_map/reduce_scatter | solution.py:194
  210.5 2.0 fusion.40
  (109 shorter events, 29.1 us)
Async XLA Ops:
  7.2 157.8 %copy-start = (bf16[384,3072]{1,0:T(8,128)(2,1)S(1)}, bf16[384,3072]{1,0:T(8,128)(2,1)}, u32[]{:S(2)}) copy-start(bf16[384,3072]{1,0:T(8,128)(2,1)} %param.36) | copy-start | bytes 7077892
  7.2 37.0 %all-gather.10.cloned.1.call-start = ((), (), s32[]{:S(2)}) async-start(), calls=%async_computation.3 | async-start | bytes 1966080 | tf_op jit(solution)/shard_map/all_gather | solution.py:96
  7.9 105.9 %all-gather.12.cloned.1.call-start = ((), (), s32[]{:S(2)}) async-start(), calls=%async_computation.4 | async-start | bytes 1966080 | tf_op jit(solution)/shard_map/all_gather | solution.py:26
  44.2 3.9 %copy-start.19 = (bf16[3072,2,384]{2,1,0:T(2,128)(2,1)S(1)}, bf16[3072,2,384]{2,1,0:T(2,128)(2,1)}, u32[]{:S(2)}) copy-start(bf16[3072,2,384]{2,1,0:T(2,128)(2,1)} %param.27) | copy-start | bytes 14155780
  48.0 2.4 %copy-start.1 = (bf16[256,3072]{1,0:T(8,128)(2,1)}, bf16[256,3072]{1,0:T(8,128)(2,1)S(1)}, u32[]{:S(2)}) copy-start(bf16[256,3072]{1,0:T(8,128)(2,1)S(1)} %fusion.5) | copy-start | bytes 4718596
  48.0 2.4 %copy-start.9 = (bf16[3072,3]{0,1:T(4,128)(2,1)S(1)}, bf16[3072,3]{0,1:T(4,128)(2,1)}, u32[]{:S(2)}) copy-start(bf16[3072,3]{0,1:T(4,128)(2,1)} %param.29) | copy-start | bytes 55300
  48.1 2.3 %copy-start.18 = (f32[3]{0:T(128)S(1)}, f32[3]{0:T(128)}, u32[]{:S(2)}) copy-start(f32[3]{0:T(128)} %param.30) | copy-start | bytes 40
  48.1 8.3 %copy-start.7 = (bf16[3072,128]{1,0:T(8,128)(2,1)S(1)}, bf16[3072,128]{1,0:T(8,128)(2,1)}, u32[]{:S(2)}) copy-start(bf16[3072,128]{1,0:T(8,128)(2,1)} %param.28) | copy-start | bytes 2359300
  49.5 22.0 %copy-start.15 = (bf16[1,3,384]{2,1,0:T(4,128)(2,1)S(1)}, bf16[1,3,384]{2,1,0:T(4,128)(2,1)}, u32[]{:S(2)}) copy-start(bf16[1,3,384]{2,1,0:T(4,128)(2,1)} %param.39) | copy-start | bytes 6916
  53.0 19.5 %copy-start.16 = (f32[3]{0:T(128)}, f32[3]{0:T(128)S(1)}, u32[]{:S(2)}) copy-start(f32[3]{0:T(128)S(1)} %get-tuple-element.48) | copy-start | bytes 40
  53.0 18.5 %collective-permute-start = (bf16[3,384]{1,0:T(4,128)(2,1)S(1)}, bf16[3,384]{1,0:T(4,128)(2,1)S(1)}, u32[]{:S(2)}, u32[]{:S(2)}) collective-permute-start(bf16[3,384]{1,0:T(4,128)(2,1)S(1)} %slice_bitcast_fusion.1), channel_id=1, source_target_pairs={{0,8},{8,16},{16,24},{1,9},{9,17},{17,25},{2,10},{10,18},{18,26},{... | collective-permute-start | bytes 6920 | tf_op jit(solution)/shard_map/ppermute | solution.py:21
  67.5 5.5 %collective-permute-start.1 = (bf16[3,512]{1,0:T(4,128)(2,1)S(1)}, bf16[3,512]{1,0:T(4,128)(2,1)S(1)}, u32[]{:S(2)}, u32[]{:S(2)}) collective-permute-start(bf16[3,512]{1,0:T(4,128)(2,1)S(1)} %slice.136), channel_id=1, source_target_pairs={{0,8},{8,16},{16,24},{1,9},{9,17},{17,25},{2,10},{10,18},{18,26},{... | collective-permute-start | bytes 9224 | tf_op jit(solution)/shard_map/ppermute | solution.py:21
  72.9 21.2 %copy-start.4 = (f32[256,384]{0,1:T(8,128)}, f32[256,384]{0,1:T(8,128)S(1)}, u32[]{:S(2)}) copy-start(f32[256,384]{0,1:T(8,128)S(1)} %copy.54) | copy-start | bytes 1179652
  76.1 82.8 %all-gather.8.cloned.1.call-start = ((), (), s32[]{:S(2)}) async-start(), calls=%async_computation.1 | async-start | bytes 2621440 | tf_op jit(solution)/shard_map/all_gather | solution.py:165
  94.2 7.5 %copy-start.13 = (f32[256]{0:T(256)S(1)}, f32[256]{0:T(256)}, u32[]{:S(2)}) copy-start(f32[256]{0:T(256)} %add_convert_fusion.1) | copy-start | bytes 3076
  96.8 13.1 %copy-start.6 = (bf16[1,256,512]{1,2,0:T(8,128)(2,1)S(1)}, bf16[1,256,512]{1,2,0:T(8,128)(2,1)}, u32[]{:S(2)}) copy-start(bf16[1,256,512]{1,2,0:T(8,128)(2,1)} %all-gather) | copy-start | bytes 786436
  110.8 99.7 %reduce-scatter.2.cloned.1.call-start = ((), (), s32[]{:S(2)}) async-start(), calls=%async_computation.2 | async-start | bytes 3932160 | tf_op jit(solution)/shard_map/reduce_scatter | solution.py:194
  113.8 1.8 copy-start.8
  113.8 1.8 copy-start.11
  113.9 1.8 copy-start.14
  113.9 1.8 copy-start.20
  114.1 4.2 %copy-start.12 = (f32[384]{0:T(512)S(1)}, f32[384]{0:T(512)}, u32[]{:S(2)}) copy-start(f32[384]{0:T(512)} %convert_element_type.91) | copy-start | bytes 4612
  115.6 43.2 %copy-start.3 = (pred[256,2048]{0,1:T(8,128)(4,1)S(1)}, pred[256,2048]{0,1:T(8,128)(4,1)}, u32[]{:S(2)}) copy-start(pred[256,2048]{0,1:T(8,128)(4,1)} %and_or_fusion) | copy-start | bytes 1572868
  162.0 2.4 %copy-start.5 = (bf16[256,3072]{1,0:T(8,128)(2,1)S(1)}, bf16[256,3072]{1,0:T(8,128)(2,1)}, u32[]{:S(2)}) copy-start(bf16[256,3072]{1,0:T(8,128)(2,1)} %param.26) | copy-start | bytes 4718596
  (3 other events, 2.8 us)
Sparse Core Ops, SparseCore 0:
  9.9 34.2 all-gather.9
  76.2 36.1 all-gather.11
  114.0 44.7 all-gather.7
  167.8 42.6 reduce-scatter.1
where the time goes:
time: 220 us; the launch traced here: 219 us
  waiting for transfers between devices  96.5 us (44%)
  blocking collectives  38.9 us (18%)
  other arithmetic  30 us (14%)
  matrix products  22.9 us (10%)
  between operations  14.9 us (7%)
  local copies, waits for them, and re-layouts  8.74 us (4%)
  starting transfers between devices  6.94 us (3%)
    all_gather x1, waiting for transfers between devices, shards(): piece = lax.all_gather(local_rows, 'seq', axis=0, tiled=True)  40.4 us
    reduce_scatter x1, waiting for transfers between devices, shards(): summed = lax.psum_scatter(term, 'mp', scatter_dimension=1, tiled=True)  39.6 us
    all_gather x1, waiting for transfers between devices, shards(): whole = lax.all_gather(own_rows, 'mp', axis=1, tiled=True)  15.8 us
    all_gather x1, blocking collectives, shards(): lax.all_gather(cache[0], 'mp', axis=1, tiled=True)  12.1 us
    all_gather x1, blocking collectives, prefix(): gathered = jax.tree.map(lambda a: lax.all_gather(a, axis), part)  9.75 us
    all_gather x1, blocking collectives, shards(): lax.all_gather(bc_block, 'mp', axis=1, tiled=True)  9.1 us
    all_gather x1, blocking collectives, shards(): lax.all_gather(kv_block, 'mp', axis=1, tiled=True)  7.92 us
    ppermute x2, starting transfers between devices, shifted(): return lax.ppermute(block, axis, route)  6.78 us
  transfers between devices with their start and end apart: 6, of which 3 were waited for; matrix products, arithmetic and copies ran while one was open for 18% of the time, Pallas kernels for 0%

commit v1 on v0

v1 whole, which is shorter than its diff:
```python
import jax
import jax.numpy as jnp
from jax import lax
from jax.sharding import PartitionSpec as P

HD = 128
QH = 8
KVH = 2
NS = 256
CONV = 4
RIM = 16


epsilon = 1e-05
rope_base = 100000000000.0
negative = -1e30


def swap(block, turn):
    return lax.ppermute(block, "mp", [(i, i ^ turn) for i in range(lax.axis_size("mp"))])


def ahead(block, distance, wrap=False):
    count = lax.axis_size("seq")
    if wrap:
        return lax.ppermute(block, "seq", [(i, (i + distance) % count) for i in range(count)])
    return lax.ppermute(block, "seq", [(i, i + distance) for i in range(count - distance)])


def ahead_and_swap(block, turn):
    rows, cols = lax.axis_size("seq"), lax.axis_size("mp")
    route = [(i * cols + j, (i + 1) * cols + (j ^ turn)) for i in range(rows - 1) for j in range(cols)]
    return lax.ppermute(block, ("seq", "mp"), route)


def rotate(values, positions):
    half = HD // 2
    freqs = rope_base ** (-jnp.arange(half, dtype=jnp.float32) * 2.0 / HD)
    angles = positions.astype(jnp.float32)[:, None] * freqs[None, :]
    cosine = jnp.cos(angles)[:, None, :]
    sine = jnp.sin(angles)[:, None, :]
    first = values[..., :half]
    second = values[..., half:]
    return jnp.concatenate(
        [first * cosine - second * sine, second * cosine + first * sine], axis=-1
    )


def rms_scale(values):
    mean_sq = jnp.mean(values * values, axis=-1, keepdims=True)
    return values * lax.rsqrt(mean_sq + epsilon)


def causal_conv(padded, count, taps):
    padded = padded.astype(jnp.float32)
    total = jnp.zeros((count, padded.shape[1]), jnp.float32)
    for offset in range(CONV):
        start = RIM - CONV + 1 + offset
        total = total + taps[offset].astype(jnp.float32)[None, :] * padded[start : start + count]
    return jax.nn.silu(total)


def shards(
    hidden,
    norm_gain,
    w_query,
    w_keyval,
    w_attn_out,
    w_inner,
    w_bc,
    w_dt,
    dt_bias,
    a_log,
    d_skip,
    conv_x,
    conv_bc,
    mamba_gain,
    w_mamba_out,
    cache,
    cache_len,
    tail_x,
    tail_bc,
    ssm_init,
):
    own_rows = hidden[0]
    tokens, width = own_rows.shape
    half_rows = tokens // 2
    seq_pos = lax.axis_index("seq")
    mp_pos = lax.axis_index("mp")
    n_seq = lax.axis_size("seq")
    n_mp = lax.axis_size("mp")
    length = cache_len[0]

    def natural(parts):
        out = jnp.zeros((parts[0].shape[0], parts[0].shape[1] * n_mp), parts[0].dtype)
        for turn, part in enumerate(parts):
            out = lax.dynamic_update_slice(out, part, (0, (mp_pos ^ turn) * part.shape[1]))
        return out

    from_x = swap(own_rows, 1)
    from_y = swap(own_rows, 2)
    rims = [ahead_and_swap(own_rows[tokens - RIM :], turn) for turn in range(n_mp)]
    diag_top = swap(from_x[:half_rows], 2)
    diag_low = swap(from_y[half_rows:], 1)
    diag = jnp.concatenate([diag_top, diag_low], axis=0)
    whole = natural(
        [jnp.concatenate([r, c], axis=0) for r, c in zip(rims, [own_rows, from_x, from_y, diag])]
    )
    normed = (rms_scale(whole.astype(jnp.float32)) * norm_gain.astype(jnp.float32)).astype(
        jnp.bfloat16
    )
    positions = length + seq_pos * tokens + jnp.arange(tokens, dtype=jnp.int32)
    local_heads = w_query.shape[1] // HD
    bc_block = jnp.dot(normed, w_bc, preferred_element_type=jnp.float32).astype(jnp.bfloat16)
    bc_parts = [bc_block] + [swap(bc_block, turn) for turn in (1, 2, 3)]
    current = normed[RIM:]
    query = rotate(
        jnp.dot(current, w_query, preferred_element_type=jnp.float32).reshape(
            tokens, local_heads, HD
        ),
        positions,
    ).astype(jnp.bfloat16)
    projected = jnp.dot(current, w_keyval, preferred_element_type=jnp.float32)
    roped = rotate(projected[:, None, :], positions)[:, 0, :]
    kv_block = jnp.where(mp_pos % 2 == 0, roped, projected).astype(jnp.bfloat16)

    owners = [(seq_pos + n_seq - step) % n_seq for step in range(n_seq)]
    if n_seq <= 4:
        cached = [cache[0]] + [ahead(cache[0], step, True) for step in range(1, n_seq)]
        fresh = [kv_block] + [ahead(kv_block, step) for step in range(1, n_seq)]
        mine = jnp.concatenate(cached + fresh, axis=0)
        starts = jnp.stack(owners)
    else:
        cached = lax.all_gather(cache[0], "seq", axis=0, tiled=True)
        fresh = lax.all_gather(kv_block, "seq", axis=0, tiled=True)
        mine = jnp.concatenate([cached, fresh], axis=0)
        starts = jnp.arange(n_seq)
    other = swap(mine, 1)
    is_key = mp_pos % 2 == 0
    keys = jnp.where(is_key, mine, other)
    values = jnp.where(is_key, other, mine)

    inner = jnp.einsum("td,dkc->ktc", normed, w_inner, preferred_element_type=jnp.float32).astype(
        jnp.bfloat16
    )
    gate_z = inner[0, RIM:]
    x_in = inner[1]
    first_block = seq_pos == 0

    def rimmed(block, tail):
        top = jnp.concatenate([jnp.zeros((RIM - CONV + 1, tail.shape[1]), tail.dtype), tail], axis=0)
        return jnp.concatenate([jnp.where(first_block, top, block[:RIM]), block[RIM:]], axis=0)

    mamba_heads = dt_bias.shape[0]
    x_conv = causal_conv(rimmed(x_in, tail_x[0]), tokens, conv_x).reshape(tokens, mamba_heads, HD)
    bc_conv = causal_conv(rimmed(natural(bc_parts), tail_bc[0]), tokens, conv_bc)
    b_mat = bc_conv[:, :NS].astype(jnp.bfloat16)
    c_mat = bc_conv[:, NS:].astype(jnp.bfloat16)
    step_size = jax.nn.softplus(
        jnp.dot(current, w_dt, preferred_element_type=jnp.float32) + dt_bias
    )
    log_decay = -step_size * jnp.exp(a_log)[None, :]
    cumulative = jnp.cumsum(log_decay, axis=0)
    block_log = cumulative[-1]
    to_end = jnp.exp(block_log[None, :] - cumulative) * step_size
    weighted = (to_end[:, :, None] * x_conv).astype(jnp.bfloat16)
    own_state = jnp.einsum("shp,sn->hpn", weighted, b_mat, preferred_element_type=jnp.float32)

    def grown(log):
        return jnp.exp(log)[:, None, None]

    prior = ahead(own_state.astype(jnp.bfloat16), 1).astype(jnp.float32)
    prior_log = ahead(block_log, 1)
    window = 1
    while window < n_seq - 1:
        with_own = (own_state + grown(block_log) * prior).astype(jnp.bfloat16)
        more = ahead(with_own, window + 1).astype(jnp.float32)
        more_log = ahead(block_log + prior_log, window + 1)
        prior = prior + grown(prior_log) * more
        prior_log = prior_log + more_log
        window = 2 * window + 1
    incoming = prior + grown(prior_log) * ssm_init[0]
    state_after = grown(block_log) * incoming + own_state

    pairs = jnp.dot(c_mat, b_mat.T, preferred_element_type=jnp.float32)
    gap = cumulative.T[:, :, None] - cumulative.T[:, None, :]
    token_ids = jnp.arange(tokens)
    lower = (token_ids[:, None] >= token_ids[None, :])[None]
    decay = jnp.exp(jnp.where(lower, gap, negative))
    mixing = (decay * pairs[None] * step_size.T[:, None, :]).astype(jnp.bfloat16)
    inner_out = jnp.einsum(
        "hts,shp->thp", mixing, x_conv.astype(jnp.bfloat16), preferred_element_type=jnp.float32
    )
    carried = jnp.exp(cumulative)[:, :, None] * jnp.einsum(
        "tn,hpn->thp", c_mat, incoming.astype(jnp.bfloat16), preferred_element_type=jnp.float32
    )
    mamba_y = inner_out + carried + d_skip[None, :, None] * x_conv
    gated = mamba_y * jax.nn.silu(gate_z.astype(jnp.float32).reshape(tokens, mamba_heads, HD))
    mixed = (
        rms_scale(gated).reshape(tokens, mamba_heads * HD) * mamba_gain.astype(jnp.float32)
    ).astype(jnp.bfloat16)

    cache_rows = cache.shape[1]
    query_index = seq_pos * tokens + jnp.arange(tokens, dtype=jnp.int32)
    slots = (starts[:, None] * cache_rows + jnp.arange(cache_rows, dtype=jnp.int32)).reshape(-1)
    news = (starts[:, None] * tokens + jnp.arange(tokens, dtype=jnp.int32)).reshape(-1)
    valid = jnp.concatenate(
        [
            jnp.broadcast_to((slots < length)[None], (tokens, slots.shape[0])),
            news[None, :] <= query_index[:, None],
        ],
        axis=1,
    )
    scale = 1.0 / float(HD) ** 0.5
    scores = jnp.einsum("qhd,kd->hqk", query, keys, preferred_element_type=jnp.float32) * scale
    masked = jnp.where(valid[None], scores, negative)
    top = jnp.max(masked, axis=-1)
    weights = jnp.where(valid[None], jnp.exp(masked - top[:, :, None]), 0.0)
    total = jnp.sum(weights, axis=-1)
    accum = jnp.einsum(
        "hqk,kd->hqd", weights.astype(jnp.bfloat16), values, preferred_element_type=jnp.float32
    )
    attended = jnp.transpose(accum / total[:, :, None], (1, 0, 2)).reshape(tokens, local_heads * HD)
    attended = attended.astype(jnp.bfloat16)

    term = jnp.dot(attended, w_attn_out, preferred_element_type=jnp.float32)
    term = term + jnp.dot(mixed, w_mamba_out, preferred_element_type=jnp.float32)
    part = [
        lax.dynamic_slice_in_dim(term, (mp_pos ^ turn) * width, width, 1) for turn in range(n_mp)
    ]
    top_part = [p[:half_rows] for p in part]
    low_part = [p[half_rows:] for p in part]

    def packed(*blocks):
        return jnp.concatenate(blocks, axis=0).astype(jnp.bfloat16)

    top_in = swap(packed(top_part[1], top_part[3]), 1).astype(jnp.float32)
    low_in = swap(packed(low_part[2], low_part[3]), 2).astype(jnp.float32)
    top_last = swap((top_part[2] + top_in[half_rows:]).astype(jnp.bfloat16), 2)
    low_last = swap((low_part[1] + low_in[half_rows:]).astype(jnp.bfloat16), 1)
    summed = jnp.concatenate(
        [
            top_part[0] + top_in[:half_rows] + top_last.astype(jnp.float32),
            low_part[0] + low_in[:half_rows] + low_last.astype(jnp.float32),
        ],
        axis=0,
    )
    layer = (summed + own_rows.astype(jnp.float32)).astype(jnp.bfloat16)
    return (layer[None], kv_block[None], state_after[None, None])


def solution(mesh):
    placed = (
        P("req", "seq", "mp"),
        P(),
        P(None, "mp"),
        P(None, "mp"),
        P("mp", None),
        P(None, None, "mp"),
        P(None, "mp"),
        P(None, "mp"),
        P("mp"),
        P("mp"),
        P("mp"),
        P(None, "mp"),
        P(),
        P("mp"),
        P("mp", None),
        P("req", "seq", "mp"),
        P("req"),
        P("req", None, "mp"),
        P("req", None, None),
        P("req", "mp", None, None),
    )
    return jax.shard_map(
        shards,
        mesh=mesh,
        in_specs=placed,
        out_specs=(P("req", "seq", "mp"), P("req", "seq", "mp"), P("req", "seq", "mp", None, None)),
        check_vma=False,
    )
```

time: 220 us -> 166 us (0.75)
  waiting for transfers between devices: 96.5 us -> 40.4 us
  starting transfers between devices: 6.94 us -> 52.3 us
  blocking collectives: 38.9 us -> 0 us
  between operations: 14.9 us -> 2.24 us
  local copies, waits for them, and re-layouts: 8.74 us -> 19.4 us
  other arithmetic: 30 us -> 25.6 us
    all_gather x3 -> x0, waiting for transfers between devices: 56.2 us -> none  [the longest x1 40.4 us: shards(): piece = lax.all_gather(local_rows, 'seq', axis=0, tiled=True)]
    ppermute x2 -> x26, starting transfers between devices: 6.78 us -> 52.3 us  [the longest x7 23.9 us: ahead(): lax.ppermute(block, 'seq', [(i, i + distance) for i in range(count - dist...]
    ppermute x2 -> x26, waiting for transfers between devices: 0.01 us -> 40.4 us  [the longest x12 18.2 us: swap(): lax.ppermute(block, 'mp', [(i, i ^ turn) for i in range(lax.axis_size('mp...]
    reduce_scatter x1 -> x0, waiting for transfers between devices: 39.6 us -> none  [shards(): summed = lax.psum_scatter(term, 'mp', scatter_dimension=1, tiled=True)]
    all_gather x4 -> x0, blocking collectives: 38.9 us -> none  [the longest x1 12.1 us: shards(): lax.all_gather(cache[0], 'mp', axis=1, tiled=True)]
    dynamic_update_slice x0 -> x3, local copies, waits for them, and re-layouts: none -> 4.56 us  [natural(): lax.dynamic_update_slice(out, part, (0, (mp_pos ^ turn) * part.shape[1]))]
    concatenate x1 -> x5, other arithmetic: 0.84 us -> 4.96 us  [the longest x2 2.3 us: shards(): jnp.concatenate([top_part[0] + top_in[:half_rows] + top_last.astype(jnp.f...]
    or x1 -> x0, other arithmetic: 3.78 us -> none  [shards(): slot_ok[None, :]]
  transfers between devices with their start and end apart: 6 -> 26, of which waited for: 3 -> 12; matrix products, arithmetic and copies ran while one was open for 18% -> 30% of each run, Pallas kernels for 0% -> 0%
where the time goes in v1:
time: 166 us; the launch traced here: 163 us
  starting transfers between devices  52.3 us (32%)
  waiting for transfers between devices  40.4 us (24%)
  other arithmetic  25.6 us (15%)
  matrix products  23.2 us (14%)
  local copies, waits for them, and re-layouts  19.4 us (12%)
  between operations  2.24 us (1%)
    ppermute x7, starting transfers between devices, ahead(): lax.ppermute(block, 'seq', [(i, i + distance) for i in range(count - dist...  23.9 us
    ppermute x12, waiting for transfers between devices, swap(): lax.ppermute(block, 'mp', [(i, i ^ turn) for i in range(lax.axis_size('mp...  18.2 us
    ppermute x4, starting transfers between devices, ahead_and_swap(): return lax.ppermute(block, ('seq', 'mp'), route)  16.9 us
    ppermute x3, waiting for transfers between devices, ahead(): lax.ppermute(block, 'seq', [(i, (i + distance) % count) for i in range(co...  13.6 us
    ppermute x12, starting transfers between devices, swap(): lax.ppermute(block, 'mp', [(i, i ^ turn) for i in range(lax.axis_size('mp...  11.5 us
    ppermute x7, waiting for transfers between devices, ahead(): lax.ppermute(block, 'seq', [(i, i + distance) for i in range(count - dist...  8.58 us
    unnamed x106, local copies, waits for them, and re-layouts  7.92 us
    dynamic_update_slice x3, local copies, waits for them, and re-layouts, natural(): lax.dynamic_update_slice(out, part, (0, (mp_pos ^ turn) * part.shape[1]))  4.56 us
  transfers between devices with their start and end apart: 26, of which 12 were waited for; matrix products, arithmetic and copies ran while one was open for 30% of the time, Pallas kernels for 0%

profile of v1, /device:TPU:0, one launch (start us, length us, event | category | flops | bytes accessed | tf_op | source)
XLA Modules:
  0.0 163.2 jit_solution(14200386303398717140)
XLA Ops:
  2.2 5.5 %collective-permute-start.3 = (bf16[16,768]{1,0:T(8,128)(2,1)}, bf16[16,768]{1,0:T(8,128)(2,1)}, u32[]{:S(2)}, u32[]{:S(2)}) collective-permute-start(bf16[16,768]{1,0:T(8,128)(2,1)} %slice_bitcast_fusion.1), channel_id=1, source_target_pairs={{0,8},{2,10},{4,12},{6,14},{8,16},{10,18},{12,20},{14,22},{16,24},... | collective-permute-start | bytes 73736 | tf_op jit(solution)/shard_map/ppermute | solution.py:33
  7.7 4.4 %collective-permute-start.4 = (bf16[16,768]{1,0:T(8,128)(2,1)}, bf16[16,768]{1,0:T(8,128)(2,1)}, u32[]{:S(2)}, u32[]{:S(2)}) collective-permute-start(bf16[16,768]{1,0:T(8,128)(2,1)} %slice_bitcast_fusion.1), channel_id=1, source_target_pairs={{0,10},{2,8},{4,14},{6,12},{8,18},{10,16},{12,22},{14,20},{16,26},... | collective-permute-start | bytes 73736 | tf_op jit(solution)/shard_map/ppermute | solution.py:33
  14.2 3.5 %collective-permute-start.6 = (bf16[16,768]{1,0:T(8,128)(2,1)}, bf16[16,768]{1,0:T(8,128)(2,1)}, u32[]{:S(2)}, u32[]{:S(2)}) collective-permute-start(bf16[16,768]{1,0:T(8,128)(2,1)} %slice_bitcast_fusion.1), channel_id=1, source_target_pairs={{0,12},{2,14},{4,8},{6,10},{8,20},{10,22},{12,16},{14,18},{16,28},... | collective-permute-start | bytes 73736 | tf_op jit(solution)/shard_map/ppermute | solution.py:33
  31.9 5.4 %collective-permute-done = bf16[256,128]{0,1:T(8,128)(2,1)S(1)} collective-permute-done((bf16[256,128]{0,1:T(8,128)(2,1)}, bf16[256,128]{0,1:T(8,128)(2,1)S(1)}, u32[]{:S(2)}, u32[]{:S(2)}) %collective-permute-start) | collective-permute-done | bytes 65568 | tf_op jit(solution)/shard_map/ppermute | solution.py:26
  38.0 4.5 %collective-permute-done.1 = bf16[256,128]{0,1:T(8,128)(2,1)S(1)} collective-permute-done((bf16[256,128]{0,1:T(8,128)(2,1)S(1)}, bf16[256,128]{0,1:T(8,128)(2,1)S(1)}, u32[]{:S(2)}, u32[]{:S(2)}) %collective-permute-start.1) | collective-permute-done | bytes 65568 | tf_op jit(solution)/shard_map/ppermute | solution.py:26
  43.2 3.6 %collective-permute-done.2 = bf16[256,128]{0,1:T(8,128)(2,1)S(1)} collective-permute-done((bf16[256,128]{0,1:T(8,128)(2,1)S(1)}, bf16[256,128]{0,1:T(8,128)(2,1)S(1)}, u32[]{:S(2)}, u32[]{:S(2)}) %collective-permute-start.2) | collective-permute-done | bytes 65568 | tf_op jit(solution)/shard_map/ppermute | solution.py:26
  46.8 3.4 %collective-permute-start.8 = (bf16[16,768]{1,0:T(8,128)(2,1)}, bf16[16,768]{1,0:T(8,128)(2,1)S(1)}, u32[]{:S(2)}, u32[]{:S(2)}) collective-permute-start(bf16[16,768]{1,0:T(8,128)(2,1)} %slice_bitcast_fusion.1), channel_id=1, source_target_pairs={{0,14},{2,12},{4,10},{6,8},{8,22},{10,20},{12,18},{14,16},{16,30},... | collective-permute-start | bytes 73736 | tf_op jit(solution)/shard_map/ppermute | solution.py:33
  53.7 3.0 %collective-permute-done.10 = bf16[128,768]{1,0:T(8,128)(2,1)S(1)} collective-permute-done((bf16[128,768]{1,0:T(8,128)(2,1)S(1)}, bf16[128,768]{1,0:T(8,128)(2,1)S(1)}, u32[]{:S(2)}, u32[]{:S(2)}) %collective-permute-start.10) | collective-permute-done | bytes 196640 | tf_op jit(solution)/shard_map/ppermute | solution.py:20
  67.1 3.7 %collective-permute-start.19 = (f32[3]{0:T(128)}, f32[3]{0:T(128)}, u32[]{:S(2)}, u32[]{:S(2)}) collective-permute-start(f32[3]{0:T(128)} %slice_reduce_fusion), channel_id=1, source_target_pairs={{0,8},{8,16},{16,24},{1,9},{9,17},{17,25},{2,10},{10,18},{18,26},{... | collective-permute-start | bytes 44 | tf_op jit(solution)/shard_map/ppermute | solution.py:27
  72.1 4.3 %fusion.18 = bf16[2,272,384]{2,1,0:T(8,128)(2,1)S(1)} fusion(bf16[3072,2,384]{2,1,0:T(2,128)(2,1)} %param.25, bf16[272,3072]{1,0:T(8,128)(2,1)} %copy-done.1), kind=kOutput, calls=%fused_computation.20 | convolution fusion | flops 1283665920 | bytes 6807552 | tf_op jit(solution)/shard_map/td,dkc->ktc/dot_general | solution.py:143
  77.9 2.6 %fusion.28 = f32[256,256]{0,1:T(8,128)S(1)} fusion(bf16[3072,256]{1,0:T(8,128)(2,1)} %param.22, bf16[272,3072]{1,0:T(8,128)(2,1)} %copy-done.1), kind=kOutput, calls=%fused_computation.28 | convolution fusion | flops 402653184 | bytes 3407872 | tf_op jit(solution)/shard_map/dot_general | solution.py:118
  80.8 2.3 %fusion.30 = f32[256,128]{0,1:T(8,128)S(1)} fusion(bf16[3072,128]{1,0:T(8,128)(2,1)} %param.23, bf16[272,3072]{1,0:T(8,128)(2,1)} %copy-done.1), kind=kOutput, calls=%fused_computation.30 | convolution fusion | flops 201326592 | bytes 2490368 | tf_op jit(solution)/shard_map/dot_general | solution.py:123
  84.2 3.6 %collective-permute-start.11 = (bf16[256,128]{0,1:T(8,128)(2,1)S(1)}, bf16[256,128]{0,1:T(8,128)(2,1)S(1)}, u32[]{:S(2)}, u32[]{:S(2)}) collective-permute-start(bf16[256,128]{0,1:T(8,128)(2,1)S(1)} %get-tuple-element.14), channel_id=1, source_target_pairs={{0,8},{8,16},{16,24},{1,9},{9,17},{17,25},{2,10},{10,18},{18,26},{... | collective-permute-start | bytes 196616 | tf_op jit(solution)/shard_map/ppermute | solution.py:27
  92.0 5.0 %collective-permute-start.12 = (bf16[256,128]{0,1:T(8,128)(2,1)S(1)}, bf16[256,128]{0,1:T(8,128)(2,1)S(1)}, u32[]{:S(2)}, u32[]{:S(2)}) collective-permute-start(bf16[256,128]{0,1:T(8,128)(2,1)S(1)} %get-tuple-element.14), channel_id=1, source_target_pairs={{0,16},{8,24},{1,17},{9,25},{2,18},{10,26},{3,19},{11,27},{4,20},{... | collective-permute-start | bytes 196616 | tf_op jit(solution)/shard_map/ppermute | solution.py:27
  100.9 2.6 %collective-permute-start.14 = (bf16[2048,128]{0,1:T(8,128)(2,1)S(1)}, bf16[2048,128]{0,1:T(8,128)(2,1)S(1)}, u32[]{:S(2)}, u32[]{:S(2)}) collective-permute-start(bf16[2048,128]{0,1:T(8,128)(2,1)S(1)} %constant_dynamic-update-slice_fusion), channel_id=1, source_target_pairs={{0,2},{2,0},{4,6},{6,4},{1,3},{3,1},{5,7},{7,5},{8,10},{10,8},{12,... | collective-permute-start | bytes 1572872 | tf_op jit(solution)/shard_map/ppermute | solution.py:20
  112.1 2.9 %collective-permute-done.18 = bf16[3,128,256]{2,1,0:T(8,128)(2,1)S(1)} collective-permute-done((bf16[3,128,256]{2,1,0:T(8,128)(2,1)S(1)}, bf16[3,128,256]{2,1,0:T(8,128)(2,1)S(1)}, u32[]{:S(2)}, u32[]{:S(2)}) %collective-permute-start.18) | collective-permute-done | bytes 196640 | tf_op jit(solution)/shard_map/ppermute | solution.py:27
  115.1 7.7 %collective-permute-start.20 = (bf16[3,128,256]{2,1,0:T(8,128)(2,1)S(1)}, bf16[3,128,256]{2,1,0:T(8,128)(2,1)S(1)}, u32[]{:S(2)}, u32[]{:S(2)}) collective-permute-start(bf16[3,128,256]{2,1,0:T(8,128)(2,1)S(1)} %fusion.60), channel_id=1, source_target_pairs={{0,16},{8,24},{1,17},{9,25},{2,18},{10,26},{3,19},{11,27},{4,20},{... | collective-permute-start | bytes 589832 | tf_op jit(solution)/shard_map/ppermute | solution.py:27
  123.2 2.5 %collective-permute-done.20 = bf16[3,128,256]{2,1,0:T(8,128)(2,1)S(1)} collective-permute-done((bf16[3,128,256]{2,1,0:T(8,128)(2,1)S(1)}, bf16[3,128,256]{2,1,0:T(8,128)(2,1)S(1)}, u32[]{:S(2)}, u32[]{:S(2)}) %collective-permute-start.20) | collective-permute-done | bytes 196640 | tf_op jit(solution)/shard_map/ppermute | solution.py:27
  127.2 3.6 %fusion.124 = f32[2,256]{1,0:T(2,128)S(1)} fusion(pred[256,2048]{0,1:T(8,128)(4,1)} %pad_add_fusion, bf16[2048,128]{0,1:T(8,128)(2,1)} %copy-done.25, bf16[2048,128]{0,1:T(8,128)(2,1)} %copy-done.41, pred[]{:T(512)S(6)} %eq.14, bf16[256,2,64]{2,0,1:T(8,128)(2,1)S(1)} %copy-done.18, bf16[256,2,64]{2,0,1:T(8,128)(2,1)S(1)} %copy-done.17), kind=kOutput, calls=%fused_computation.193 | convolution fusion | flops 274204672 | bytes 1705985 | tf_op jit(solution)/shard_map/sub | solution.py:218
  130.8 3.7 %fusion.38 = bf16[256,2,128]{0,2,1:T(8,128)(2,1)S(1)} fusion(bf16[2048,128]{0,1:T(8,128)(2,1)} %copy-done.41, bf16[2048,128]{0,1:T(8,128)(2,1)} %copy-done.25, pred[]{:T(512)S(6)} %eq.14, pred[256,2048]{0,1:T(8,128)(4,1)} %pad_add_fusion, f32[256,2]{0,1:T(2,128)S(1)} %bitcast.188, bf16[256,2,64]{2,0,1:T(8,128)(2,1)S(1)} %copy-done.18, ...), kind=kOutput, calls=%fused_computation.34 | convolution fusion | flops 543033856 | bytes 1837057 | tf_op jit(solution)/shard_map/hqk,kd->hqd/dot_general | solution.py:220
  134.6 2.0 %fusion.128 = f32[256,3072]{1,0:T(8,128)S(1)} fusion(bf16[256,256]{0,1:T(8,128)(2,1)S(1)} %bitcast.176, bf16[256,3072]{1,0:T(8,128)(2,1)} %param.24), kind=kOutput, calls=%fused_computation.195 | convolution fusion | flops 402653184 | bytes 4849664 | tf_op jit(solution)/shard_map/dot_general | solution.py:226
  139.7 7.8 %collective-permute-done.22 = bf16[256,768]{1,0:T(8,128)(2,1)S(1)} collective-permute-done((bf16[256,768]{1,0:T(8,128)(2,1)S(1)}, bf16[256,768]{1,0:T(8,128)(2,1)S(1)}, u32[]{:S(2)}, u32[]{:S(2)}) %collective-permute-start.22) | collective-permute-done | bytes 393248 | tf_op jit(solution)/shard_map/ppermute | solution.py:20
  151.6 2.7 %collective-permute-done.23 = bf16[128,768]{1,0:T(8,128)(2,1)} collective-permute-done((bf16[128,768]{1,0:T(8,128)(2,1)}, bf16[128,768]{1,0:T(8,128)(2,1)}, u32[]{:S(2)}, u32[]{:S(2)}) %collective-permute-start.23) | collective-permute-done | bytes 196640 | tf_op jit(solution)/shard_map/ppermute | solution.py:20
  157.1 4.2 %collective-permute-done.25 = bf16[128,768]{1,0:T(8,128)(2,1)S(1)} collective-permute-done((bf16[128,768]{1,0:T(8,128)(2,1)S(1)}, bf16[128,768]{1,0:T(8,128)(2,1)S(1)}, u32[]{:S(2)}, u32[]{:S(2)}) %collective-permute-start.25) | collective-permute-done | bytes 196640 | tf_op jit(solution)/shard_map/ppermute | solution.py:20
  (220 shorter events, 66.3 us)
Async XLA Ops:
  2.2 28.8 %collective-permute-start.3 = (bf16[16,768]{1,0:T(8,128)(2,1)}, bf16[16,768]{1,0:T(8,128)(2,1)}, u32[]{:S(2)}, u32[]{:S(2)}) collective-permute-start(bf16[16,768]{1,0:T(8,128)(2,1)} %slice_bitcast_fusion.1), channel_id=1, source_target_pairs={{0,8},{2,10},{4,12},{6,14},{8,16},{10,18},{12,20},{14,22},{16,24},... | collective-permute-start | bytes 73736 | tf_op jit(solution)/shard_map/ppermute | solution.py:33
  7.7 44.5 %collective-permute-start.4 = (bf16[16,768]{1,0:T(8,128)(2,1)}, bf16[16,768]{1,0:T(8,128)(2,1)}, u32[]{:S(2)}, u32[]{:S(2)}) collective-permute-start(bf16[16,768]{1,0:T(8,128)(2,1)} %slice_bitcast_fusion.1), channel_id=1, source_target_pairs={{0,10},{2,8},{4,14},{6,12},{8,18},{10,16},{12,22},{14,20},{16,26},... | collective-permute-start | bytes 73736 | tf_op jit(solution)/shard_map/ppermute | solution.py:33
  12.1 39.4 %collective-permute-start.5 = (bf16[256,768]{1,0:T(8,128)(2,1)}, bf16[256,768]{1,0:T(8,128)(2,1)S(1)}, u32[]{:S(2)}, u32[]{:S(2)}) collective-permute-start(bf16[256,768]{1,0:T(8,128)(2,1)} %bitcast.163), channel_id=1, source_target_pairs={{0,2},{2,0},{4,6},{6,4},{1,3},{3,1},{5,7},{7,5},{8,10},{10,8},{12,... | collective-permute-start | bytes 1179656 | tf_op jit(solution)/shard_map/ppermute | solution.py:20
  12.6 38.3 %collective-permute-start.7 = (bf16[256,768]{1,0:T(8,128)(2,1)}, bf16[256,768]{1,0:T(8,128)(2,1)S(1)}, u32[]{:S(2)}, u32[]{:S(2)}) collective-permute-start(bf16[256,768]{1,0:T(8,128)(2,1)} %bitcast.164), channel_id=1, source_target_pairs={{0,4},{2,6},{4,0},{6,2},{1,5},{3,7},{5,1},{7,3},{8,12},{10,14},{12... | collective-permute-start | bytes 1179656 | tf_op jit(solution)/shard_map/ppermute | solution.py:20
  14.2 38.8 %collective-permute-start.6 = (bf16[16,768]{1,0:T(8,128)(2,1)}, bf16[16,768]{1,0:T(8,128)(2,1)}, u32[]{:S(2)}, u32[]{:S(2)}) collective-permute-start(bf16[16,768]{1,0:T(8,128)(2,1)} %slice_bitcast_fusion.1), channel_id=1, source_target_pairs={{0,12},{2,14},{4,8},{6,10},{8,20},{10,22},{12,16},{14,18},{16,28},... | collective-permute-start | bytes 73736 | tf_op jit(solution)/shard_map/ppermute | solution.py:33
  30.9 6.4 %collective-permute-start = (bf16[256,128]{0,1:T(8,128)(2,1)}, bf16[256,128]{0,1:T(8,128)(2,1)S(1)}, u32[]{:S(2)}, u32[]{:S(2)}) collective-permute-start(bf16[256,128]{0,1:T(8,128)(2,1)} %bitcast.173), channel_id=1, source_target_pairs={{0,8},{8,16},{16,24},{24,0},{1,9},{9,17},{17,25},{25,1},{2,10},{10... | collective-permute-start | bytes 196616 | tf_op jit(solution)/shard_map/ppermute | solution.py:26
  37.4 5.2 %collective-permute-start.1 = (bf16[256,128]{0,1:T(8,128)(2,1)S(1)}, bf16[256,128]{0,1:T(8,128)(2,1)S(1)}, u32[]{:S(2)}, u32[]{:S(2)}) collective-permute-start(bf16[256,128]{0,1:T(8,128)(2,1)S(1)} %bitcast.174), channel_id=1, source_target_pairs={{0,16},{8,24},{16,0},{24,8},{1,17},{9,25},{17,1},{25,9},{2,18},{10... | collective-permute-start | bytes 196616 | tf_op jit(solution)/shard_map/ppermute | solution.py:26
  42.6 4.3 %collective-permute-start.2 = (bf16[256,128]{0,1:T(8,128)(2,1)S(1)}, bf16[256,128]{0,1:T(8,128)(2,1)S(1)}, u32[]{:S(2)}, u32[]{:S(2)}) collective-permute-start(bf16[256,128]{0,1:T(8,128)(2,1)S(1)} %bitcast.175), channel_id=1, source_target_pairs={{0,24},{8,0},{16,8},{24,16},{1,25},{9,1},{17,9},{25,17},{2,26},{10... | collective-permute-start | bytes 196616 | tf_op jit(solution)/shard_map/ppermute | solution.py:26
  46.8 6.9 %collective-permute-start.8 = (bf16[16,768]{1,0:T(8,128)(2,1)}, bf16[16,768]{1,0:T(8,128)(2,1)S(1)}, u32[]{:S(2)}, u32[]{:S(2)}) collective-permute-start(bf16[16,768]{1,0:T(8,128)(2,1)} %slice_bitcast_fusion.1), channel_id=1, source_target_pairs={{0,14},{2,12},{4,10},{6,8},{8,22},{10,20},{12,18},{14,16},{16,30},... | collective-permute-start | bytes 73736 | tf_op jit(solution)/shard_map/ppermute | solution.py:33
  50.9 5.8 %collective-permute-start.10 = (bf16[128,768]{1,0:T(8,128)(2,1)S(1)}, bf16[128,768]{1,0:T(8,128)(2,1)S(1)}, u32[]{:S(2)}, u32[]{:S(2)}) collective-permute-start(bf16[128,768]{1,0:T(8,128)(2,1)S(1)} %slice.209), channel_id=1, source_target_pairs={{0,2},{2,0},{4,6},{6,4},{1,3},{3,1},{5,7},{7,5},{8,10},{10,8},{12,... | collective-permute-start | bytes 589832 | tf_op jit(solution)/shard_map/ppermute | solution.py:20
  51.6 5.7 %collective-permute-start.9 = (bf16[128,768]{1,0:T(8,128)(2,1)S(1)}, bf16[128,768]{1,0:T(8,128)(2,1)S(1)}, u32[]{:S(2)}, u32[]{:S(2)}) collective-permute-start(bf16[128,768]{1,0:T(8,128)(2,1)S(1)} %slice.208), channel_id=1, source_target_pairs={{0,4},{2,6},{4,0},{6,2},{1,5},{3,7},{5,1},{7,3},{8,12},{10,14},{12... | collective-permute-start | bytes 589832 | tf_op jit(solution)/shard_map/ppermute | solution.py:20
  60.4 43.1 %collective-permute-start.15 = (bf16[272,128]{1,0:T(8,128)(2,1)}, bf16[272,128]{1,0:T(8,128)(2,1)}, u32[]{:S(2)}, u32[]{:S(2)}) collective-permute-start(bf16[272,128]{1,0:T(8,128)(2,1)} %get-tuple-element.47), channel_id=1, source_target_pairs={{0,2},{2,0},{4,6},{6,4},{1,3},{3,1},{5,7},{7,5},{8,10},{10,8},{12,... | collective-permute-start | bytes 208904 | tf_op jit(solution)/shard_map/ppermute | solution.py:20
  62.3 42.8 %collective-permute-start.16 = (bf16[272,128]{1,0:T(8,128)(2,1)}, bf16[272,128]{1,0:T(8,128)(2,1)}, u32[]{:S(2)}, u32[]{:S(2)}) collective-permute-start(bf16[272,128]{1,0:T(8,128)(2,1)} %get-tuple-element.47), channel_id=1, source_target_pairs={{0,4},{2,6},{4,0},{6,2},{1,5},{3,7},{5,1},{7,3},{8,12},{10,14},{12... | collective-permute-start | bytes 208904 | tf_op jit(solution)/shard_map/ppermute | solution.py:20
  62.8 43.8 %collective-permute-start.17 = (bf16[272,128]{1,0:T(8,128)(2,1)}, bf16[272,128]{1,0:T(8,128)(2,1)}, u32[]{:S(2)}, u32[]{:S(2)}) collective-permute-start(bf16[272,128]{1,0:T(8,128)(2,1)} %get-tuple-element.47), channel_id=1, source_target_pairs={{0,6},{2,4},{4,2},{6,0},{1,7},{3,5},{5,3},{7,1},{8,14},{10,12},{12... | collective-permute-start | bytes 208904 | tf_op jit(solution)/shard_map/ppermute | solution.py:20
  67.1 21.6 %collective-permute-start.19 = (f32[3]{0:T(128)}, f32[3]{0:T(128)}, u32[]{:S(2)}, u32[]{:S(2)}) collective-permute-start(f32[3]{0:T(128)} %slice_reduce_fusion), channel_id=1, source_target_pairs={{0,8},{8,16},{16,24},{1,9},{9,17},{17,25},{2,10},{10,18},{18,26},{... | collective-permute-start | bytes 44 | tf_op jit(solution)/shard_map/ppermute | solution.py:27
  84.2 13.5 %collective-permute-start.11 = (bf16[256,128]{0,1:T(8,128)(2,1)S(1)}, bf16[256,128]{0,1:T(8,128)(2,1)S(1)}, u32[]{:S(2)}, u32[]{:S(2)}) collective-permute-start(bf16[256,128]{0,1:T(8,128)(2,1)S(1)} %get-tuple-element.14), channel_id=1, source_target_pairs={{0,8},{8,16},{16,24},{1,9},{9,17},{17,25},{2,10},{10,18},{18,26},{... | collective-permute-start | bytes 196616 | tf_op jit(solution)/shard_map/ppermute | solution.py:27
  92.0 7.0 %collective-permute-start.12 = (bf16[256,128]{0,1:T(8,128)(2,1)S(1)}, bf16[256,128]{0,1:T(8,128)(2,1)S(1)}, u32[]{:S(2)}, u32[]{:S(2)}) collective-permute-start(bf16[256,128]{0,1:T(8,128)(2,1)S(1)} %get-tuple-element.14), channel_id=1, source_target_pairs={{0,16},{8,24},{1,17},{9,25},{2,18},{10,26},{3,19},{11,27},{4,20},{... | collective-permute-start | bytes 196616 | tf_op jit(solution)/shard_map/ppermute | solution.py:27
  100.9 25.5 %collective-permute-start.14 = (bf16[2048,128]{0,1:T(8,128)(2,1)S(1)}, bf16[2048,128]{0,1:T(8,128)(2,1)S(1)}, u32[]{:S(2)}, u32[]{:S(2)}) collective-permute-start(bf16[2048,128]{0,1:T(8,128)(2,1)S(1)} %constant_dynamic-update-slice_fusion), channel_id=1, source_target_pairs={{0,2},{2,0},{4,6},{6,4},{1,3},{3,1},{5,7},{7,5},{8,10},{10,8},{12,... | collective-permute-start | bytes 1572872 | tf_op jit(solution)/shard_map/ppermute | solution.py:20
  110.5 4.5 %collective-permute-start.18 = (bf16[3,128,256]{2,1,0:T(8,128)(2,1)S(1)}, bf16[3,128,256]{2,1,0:T(8,128)(2,1)S(1)}, u32[]{:S(2)}, u32[]{:S(2)}) collective-permute-start(bf16[3,128,256]{2,1,0:T(8,128)(2,1)S(1)} %get-tuple-element.48), channel_id=1, source_target_pairs={{0,8},{8,16},{16,24},{1,9},{9,17},{17,25},{2,10},{10,18},{18,26},{... | collective-permute-start | bytes 589832 | tf_op jit(solution)/shard_map/ppermute | solution.py:27
  115.1 10.6 %collective-permute-start.20 = (bf16[3,128,256]{2,1,0:T(8,128)(2,1)S(1)}, bf16[3,128,256]{2,1,0:T(8,128)(2,1)S(1)}, u32[]{:S(2)}, u32[]{:S(2)}) collective-permute-start(bf16[3,128,256]{2,1,0:T(8,128)(2,1)S(1)} %fusion.60), channel_id=1, source_target_pairs={{0,16},{8,24},{1,17},{9,25},{2,18},{10,26},{3,19},{11,27},{4,20},{... | collective-permute-start | bytes 589832 | tf_op jit(solution)/shard_map/ppermute | solution.py:27
  137.8 9.7 %collective-permute-start.22 = (bf16[256,768]{1,0:T(8,128)(2,1)S(1)}, bf16[256,768]{1,0:T(8,128)(2,1)S(1)}, u32[]{:S(2)}, u32[]{:S(2)}) collective-permute-start(bf16[256,768]{1,0:T(8,128)(2,1)S(1)} %pad_maximum_fusion), channel_id=1, source_target_pairs={{0,2},{2,0},{4,6},{6,4},{1,3},{3,1},{5,7},{7,5},{8,10},{10,8},{12,... | collective-permute-start | bytes 1179656 | tf_op jit(solution)/shard_map/ppermute | solution.py:20
  139.4 11.1 %collective-permute-start.24 = (bf16[256,768]{1,0:T(8,128)(2,1)}, bf16[256,768]{1,0:T(8,128)(2,1)}, u32[]{:S(2)}, u32[]{:S(2)}) collective-permute-start(bf16[256,768]{1,0:T(8,128)(2,1)} %pad_maximum_fusion.1), channel_id=1, source_target_pairs={{0,4},{2,6},{4,0},{6,2},{1,5},{3,7},{5,1},{7,3},{8,12},{10,14},{12... | collective-permute-start | bytes 1179656 | tf_op jit(solution)/shard_map/ppermute | solution.py:20
  148.3 6.0 %collective-permute-start.23 = (bf16[128,768]{1,0:T(8,128)(2,1)}, bf16[128,768]{1,0:T(8,128)(2,1)}, u32[]{:S(2)}, u32[]{:S(2)}) collective-permute-start(bf16[128,768]{1,0:T(8,128)(2,1)} %fusion.65), channel_id=1, source_target_pairs={{0,4},{2,6},{4,0},{6,2},{1,5},{3,7},{5,1},{7,3},{8,12},{10,14},{12... | collective-permute-start | bytes 589832 | tf_op jit(solution)/shard_map/ppermute | solution.py:20
  155.6 5.7 %collective-permute-start.25 = (bf16[128,768]{1,0:T(8,128)(2,1)S(1)}, bf16[128,768]{1,0:T(8,128)(2,1)S(1)}, u32[]{:S(2)}, u32[]{:S(2)}) collective-permute-start(bf16[128,768]{1,0:T(8,128)(2,1)S(1)} %get-tuple-element.16), channel_id=1, source_target_pairs={{0,2},{2,0},{4,6},{6,4},{1,3},{3,1},{5,7},{7,5},{8,10},{10,8},{12,... | collective-permute-start | bytes 589832 | tf_op jit(solution)/shard_map/ppermute | solution.py:20
  (49 other events, 682.3 us)

commit v2 on v0

v2 whole, which is shorter than its diff:
```python
import functools

import jax
import jax.numpy as jnp
from jax import lax
from jax.experimental import pallas as pl
from jax.experimental.pallas import tpu as pltpu
from jax.sharding import PartitionSpec as P

HD = 128
QH = 8
KVH = 2
NS = 256
CONV = 4
RIM = 16
LOGS = 32


epsilon = 1e-05
rope_base = 100000000000.0
negative = -1e30
f32 = jnp.float32
bf16 = jnp.bfloat16


def call(kernel, out_shape, n_scalars, n_arrays, micros, scratch=(), limit=24 * 1024 * 1024, left=0):
    smem = pl.BlockSpec(memory_space=pltpu.SMEM)
    vmem = pl.BlockSpec(memory_space=pltpu.VMEM)
    return pl.pallas_call(
        kernel,
        out_shape=out_shape,
        in_specs=[smem] * n_scalars + [vmem] * n_arrays + [pl.BlockSpec(memory_space=pl.ANY)] * left,
        out_specs=jax.tree.map(lambda _: vmem, out_shape),
        scratch_shapes=scratch,
        compiler_params=pltpu.CompilerParams(vmem_limit_bytes=limit),
        cost_estimate=pl.CostEstimate(flops=micros * 10**9, bytes_accessed=0, transcendentals=0),
    )


def shape(*dims, dtype=bf16):
    return jax.ShapeDtypeStruct(dims, dtype)


def swap(block, turn):
    return lax.ppermute(block, "mp", [(i, i ^ turn) for i in range(lax.axis_size("mp"))])


def cross(block, turn):
    return lax.ppermute(block, "seq", [(i, i ^ turn) for i in range(lax.axis_size("seq"))])


def ahead(block):
    count = lax.axis_size("seq")
    return lax.ppermute(block, "seq", [(i, (i + 1) % count) for i in range(count)])


def dot(a, b):
    return jnp.dot(a, b, preferred_element_type=f32)


def dot_nt(a, b):
    return lax.dot_general(a, b, (((1,), (1,)), ((), ())), preferred_element_type=f32)


def dot_tn(a, b):
    return lax.dot_general(a, b, (((0,), (0,)), ((), ())), preferred_element_type=f32)


def silu(v):
    return v / (1.0 + jnp.exp(-v))


def rope(v, cos, sin):
    return v * cos + pltpu.roll(v, HD // 2, 1) * sin


def norm_kernel(
    place, own, from_x, from_y, diag_top, diag_low, rim0, rim1, rim2, rim3, gain, w_bc, w_kv, cos, sin,
    cache, later, normed, bc, kv, packed,
):
    me = place[0]
    tokens, width = own.shape
    half = tokens // 2
    full = 1.0 / (4 * width)

    def columns(turn):
        return pl.ds(pl.multiple_of((me ^ turn) * width, 128), width)

    def rows(start, count, blocks):
        square = sum(
            jnp.sum(b.astype(f32) * b.astype(f32), axis=1, keepdims=True) for b in blocks
        )
        inverse = lax.rsqrt(square * full + epsilon)
        for turn, block in enumerate(blocks):
            scaled = block.astype(f32) * inverse * gain[:, columns(turn)]
            normed[pl.ds(start, count), columns(turn)] = scaled.astype(bf16)

    rows(0, RIM, [rim0[...], rim1[...], rim2[...], rim3[...]])
    rows(RIM, half, [own[:half], from_x[:half], from_y[:half], diag_top[...]])
    rows(RIM + half, half, [own[half:], from_x[half:], from_y[half:], diag_low[...]])
    bc[...] = dot(normed[...], w_bc[...]).astype(bf16)
    projected = dot(normed[RIM:, :], w_kv[...])
    turned = rope(projected, cos[...], sin[...])
    block = jnp.where(me % 2 == 0, turned, projected).astype(bf16)
    kv[...] = block
    packed[: cache.shape[0], :] = cache[...]
    packed[cache.shape[0] :, :] = block


def softplus(v):
    return jnp.maximum(v, 0.0) + jnp.log1p(jnp.exp(-jnp.abs(v)))


def project_kernel(
    dt_bias, a_log, normed, w_query, w_inner, w_dt, cos, sin, query, x_in, gate_z, steps, cumulative
):
    tokens = cos.shape[0]
    x_in[...] = dot(normed[...], w_inner[1]).astype(bf16)
    current = normed[RIM:, :]
    raw = jnp.concatenate([dot_nt(w_dt[...], current), jnp.zeros((5, tokens), f32)], axis=0)
    head = lax.broadcasted_iota(jnp.int32, (8, tokens), 0)
    bias = jnp.zeros((8, tokens), f32)
    rate = jnp.zeros((8, tokens), f32)
    for h in range(3):
        bias = jnp.where(head == h, dt_bias[h], bias)
        rate = jnp.where(head == h, a_log[h], rate)
    step = softplus(raw + bias)
    decay = -step * jnp.exp(rate)
    before = lax.broadcasted_iota(jnp.int32, (tokens, tokens), 0)
    after = lax.broadcasted_iota(jnp.int32, (tokens, tokens), 1)
    upper = jnp.where(before <= after, 1.0, 0.0)
    steps[...] = step
    cumulative[...] = jnp.dot(
        decay, upper, preferred_element_type=f32, precision=lax.Precision.HIGHEST
    )
    gate_z[...] = dot(current, w_inner[0]).astype(bf16)
    projected = dot(current, w_query[...])
    for h in range(projected.shape[1] // HD):
        block = pl.ds(h * HD, HD)
        query[:, block] = rope(projected[:, h * HD : (h + 1) * HD], cos[...], sin[...]).astype(bf16)


def conv(scratch, tail, taps, first, tokens):
    scratch[RIM - CONV + 1 : RIM, :] = jnp.where(
        first, tail[0].astype(f32), scratch[RIM - CONV + 1 : RIM, :]
    )
    total = None
    for offset in range(CONV):
        start = RIM - CONV + 1 + offset
        term = taps[offset : offset + 1, :].astype(f32) * scratch[start : start + tokens, :]
        total = term if total is None else total + term
    return silu(total)


def logs_of(log):
    log = jnp.maximum(log, -256.0)
    high = jnp.floor(log)
    rest = (log - high) * 256.0
    middle = jnp.floor(rest)
    low = rest - middle
    return jnp.concatenate([high, middle, low, jnp.zeros_like(low)], axis=0).astype(bf16)


def log_from(rows):
    rows = rows.astype(f32)
    return rows[0:8] + (rows[8:16] + rows[16:24]) * (1.0 / 256.0)


def state_kernel(
    place, x_in, bc0, bc1, bc2, bc3, tail_x, tail_bc, conv_x, conv_bc, steps, cumulative,
    own, packet, x_conv, b_mat, c_mat, pad_x, pad_bc,
):
    me, first = place[0], place[1] == 0
    tokens = steps.shape[1]
    for turn, part in enumerate([bc0, bc1, bc2, bc3]):
        pad_bc[:, pl.ds(pl.multiple_of((me ^ turn) * HD, HD), HD)] = part[...].astype(f32)
    pad_x[...] = x_in[...].astype(f32)
    bc = conv(pad_bc, tail_bc, conv_bc, first, tokens).astype(bf16)
    b_mat[...] = bc[:, :NS]
    c_mat[...] = bc[:, NS:]
    convolved = conv(pad_x, tail_x, conv_x, first, tokens)
    x_conv[...] = convolved.astype(bf16)
    last = cumulative[:, tokens - 1 : tokens]
    to_end = jnp.transpose(jnp.exp(last - cumulative[...]) * steps[...])
    heads = convolved.shape[1] // HD
    for h in range(heads):
        weighted = convolved[:, h * HD : (h + 1) * HD] * to_end[:, h : h + 1]
        state = dot_tn(weighted.astype(bf16), bc[:, :NS])
        own[h * HD : (h + 1) * HD, :] = state
        packet[h * HD : (h + 1) * HD, :] = state.astype(bf16)
    packet[heads * HD :, :] = logs_of(jnp.broadcast_to(last, (8, NS)))


def inside_kernel(d_skip, c_mat, b_mat, steps, cumulative, x_conv, y):
    tokens = steps.shape[1]
    pairs = dot_nt(c_mat[...], b_mat[...])
    column = jnp.transpose(cumulative[...])
    row_id = lax.broadcasted_iota(jnp.int32, (tokens, tokens), 0)
    col_id = lax.broadcasted_iota(jnp.int32, (tokens, tokens), 1)
    lower = row_id >= col_id
    for h in range(x_conv.shape[1] // HD):
        gap = column[:, h : h + 1] - cumulative[h : h + 1, :]
        mixing = jnp.exp(jnp.where(lower, gap, negative)) * pairs * steps[h : h + 1, :]
        block = x_conv[:, h * HD : (h + 1) * HD]
        y[:, h * HD : (h + 1) * HD] = dot(mixing.astype(bf16), block) + d_skip[h] * block.astype(f32)


def join_kernel(place, first, second, packet, *, bit):
    swapped = (place[1] // bit) % 2 == 0 if bit else False
    size = first.shape[0] - LOGS
    first_log, second_log = log_from(first[size:, :]), log_from(second[size:, :])
    grown = jnp.exp(jnp.where(swapped, second_log, first_log))
    for h in range(size // HD):
        block = pl.ds(h * HD, HD)
        a, b = first[block, :].astype(f32), second[block, :].astype(f32)
        later, earlier = jnp.where(swapped, b, a), jnp.where(swapped, a, b)
        packet[block, :] = (later + grown[h : h + 1, :] * earlier).astype(bf16)
    packet[size:, :] = logs_of(first_log + second_log)


def finish_kernel(
    place, near, far, init, own, c_mat, cumulative, y, gate_z, gain, attended, w_attn, w_mamba,
    states, keep, keep_top, keep_low, to_x, to_y, mixed,
):
    me = place[0]
    heads = init.shape[1]
    tokens = y.shape[0]
    half = tokens // 2
    size = heads * HD
    near_on, far_on = place[1] == 1, place[2] == 1
    near_log = jnp.where(near_on, log_from(near[size:, :]), 0.0)
    far_log = jnp.where(far_on, log_from(far[size:, :]), 0.0)
    near_grown, far_grown = jnp.exp(near_log), jnp.exp(near_log + far_log)
    block_grown = jnp.exp(
        jnp.broadcast_to(cumulative[:, tokens - 1 : tokens], (8, NS))
    )
    growth = jnp.transpose(jnp.exp(cumulative[...]))
    for h in range(heads):
        block = pl.ds(h * HD, HD)
        incoming = (
            jnp.where(near_on, near[block, :].astype(f32), 0.0)
            + near_grown[h : h + 1, :] * jnp.where(far_on, far[block, :].astype(f32), 0.0)
            + far_grown[h : h + 1, :] * init[0, h]
        )
        states[0, 0, h] = block_grown[h : h + 1, :] * incoming + own[block, :]
        carried = dot_nt(c_mat[...], incoming.astype(bf16)) * growth[:, h : h + 1]
        gated = (y[:, block] + carried) * silu(gate_z[:, block].astype(f32))
        mean_sq = jnp.sum(gated * gated, axis=1, keepdims=True) * (1.0 / HD)
        mixed[:, block] = (gated * lax.rsqrt(mean_sq + epsilon) * gain[:, block]).astype(bf16)

    width = keep.shape[1]

    def term(turn, start, count):
        columns = pl.ds(pl.multiple_of((me ^ turn) * width, 128), width)
        return dot(attended[start : start + count, :], w_attn[:, columns]) + dot(
            mixed[start : start + count, :], w_mamba[:, columns]
        )

    to_x[:half, :] = term(1, 0, half).astype(bf16)
    low_one = term(1, half, half)
    keep_low[...] = low_one
    to_y[:half, :] = term(2, half, half).astype(bf16)
    keep_top[...] = term(2, 0, half)
    to_x[half:, :] = term(3, 0, half).astype(bf16)
    to_y[half:, :] = term(3, half, half).astype(bf16)
    keep[...] = term(0, 0, tokens)


def attention_kernel(place, length, query, *refs, cache_rows, scale):
    n_seq = (len(refs) - 2) // 2
    mine, other, out, scores = refs[:n_seq], refs[n_seq : 2 * n_seq], refs[-2], refs[-1]
    key_first = place[0] % 2 == 0
    seq_pos = place[1]
    tokens = query.shape[0]
    heads = query.shape[1] // HD
    rows = heads * tokens
    count = mine[0].shape[0]
    both = jnp.concatenate([query[:, h * HD : (h + 1) * HD] for h in range(heads)], axis=0)
    row = lax.broadcasted_iota(jnp.int32, (rows, count), 0) % tokens
    col = lax.broadcasted_iota(jnp.int32, (rows, count), 1)
    highest = None
    for turn in range(n_seq):
        keys = jnp.where(key_first, mine[turn][...], other[turn][...])
        owner = seq_pos ^ turn
        left = length[0] - owner * cache_rows
        last = cache_rows + jnp.where(owner < seq_pos, tokens, jnp.where(owner > seq_pos, -1, row))
        limit = jnp.where(col < cache_rows, left, last + 1)
        part = jnp.where(col < limit, dot_nt(both, keys), negative)
        scores[:, turn * count : (turn + 1) * count] = part
        for start in range(0, count, 128):
            block = part[:, start : start + 128]
            highest = block if highest is None else jnp.maximum(highest, block)
    top = jnp.max(highest, axis=1, keepdims=True)
    total = None
    accum = jnp.zeros((rows, HD), f32)
    for turn in range(n_seq):
        values = jnp.where(key_first, other[turn][...], mine[turn][...])
        weights = jnp.exp2((scores[:, turn * count : (turn + 1) * count] - top) * (scale * 1.4426950408889634))
        for start in range(0, count, 128):
            block = weights[:, start : start + 128]
            total = block if total is None else total + block
        accum = accum + dot(weights.astype(bf16), values)
    attended = accum / jnp.sum(total, axis=1, keepdims=True)
    for h in range(heads):
        out[:, h * HD : (h + 1) * HD] = attended[h * tokens : (h + 1) * tokens].astype(bf16)


def attend_plain(query, keys, values, length, starts, cache_rows, seq_pos):
    tokens = query.shape[0]
    query_index = seq_pos * tokens + jnp.arange(tokens, dtype=jnp.int32)
    slots = (starts[:, None] * cache_rows + jnp.arange(cache_rows, dtype=jnp.int32)).reshape(-1)
    news = (starts[:, None] * tokens + jnp.arange(tokens, dtype=jnp.int32)).reshape(-1)
    valid = jnp.concatenate(
        [
            jnp.broadcast_to((slots < length)[None], (tokens, slots.shape[0])),
            news[None, :] <= query_index[:, None],
        ],
        axis=1,
    )
    heads = query.reshape(tokens, -1, HD)
    scores = jnp.einsum("qhd,kd->hqk", heads, keys, preferred_element_type=f32) * HD**-0.5
    masked = jnp.where(valid[None], scores, negative)
    top = jnp.max(masked, axis=-1)
    weights = jnp.where(valid[None], jnp.exp(masked - top[:, :, None]), 0.0)
    total = jnp.sum(weights, axis=-1)
    accum = jnp.einsum("hqk,kd->hqd", weights.astype(bf16), values, preferred_element_type=f32)
    out = jnp.transpose(accum / total[:, :, None], (1, 0, 2)).reshape(tokens, -1)
    return out.astype(bf16)


def shards(
    hidden,
    norm_gain,
    w_query,
    w_keyval,
    w_attn_out,
    w_inner,
    w_bc,
    w_dt,
    dt_bias,
    a_log,
    d_skip,
    conv_x,
    conv_bc,
    mamba_gain,
    w_mamba_out,
    cache,
    cache_len,
    tail_x,
    tail_bc,
    ssm_init,
):
    own_rows = hidden[0]
    tokens, width = own_rows.shape
    half = tokens // 2
    seq_pos = lax.axis_index("seq")
    mp_pos = lax.axis_index("mp")
    n_seq = lax.axis_size("seq")
    length = cache_len[0]
    place = jnp.stack([mp_pos, seq_pos, jnp.int32(n_seq)]).astype(jnp.int32)
    inner_width = w_inner.shape[2]
    heads = inner_width // HD
    w_pair = jnp.transpose(w_inner, (1, 0, 2))

    from_x = swap(own_rows, 1)
    from_y = swap(own_rows, 2)
    rim = ahead(own_rows[tokens - RIM :])
    diag_top = swap(from_x[:half], 2)
    diag_low = swap(from_y[half:], 1)
    rims = [rim] + [swap(rim, turn) for turn in (1, 2, 3)]

    positions = length + seq_pos * tokens + jnp.arange(tokens, dtype=jnp.int32)
    freqs = rope_base ** (-jnp.arange(HD // 2, dtype=f32) * 2.0 / HD)
    angles = positions.astype(f32)[:, None] * jnp.concatenate([freqs, freqs])[None, :]
    cos = jnp.cos(angles)
    sin = jnp.where(jnp.arange(HD)[None, :] < HD // 2, -jnp.sin(angles), jnp.sin(angles))
    gain = norm_gain.astype(f32)[None, :]
    mixer_gain = mamba_gain.astype(f32)[None, :]

    cache_rows = cache.shape[1]
    normed, bc_block, kv_block, packed = call(
        norm_kernel,
        (
            shape(RIM + tokens, 4 * width),
            shape(RIM + tokens, w_bc.shape[1]),
            shape(tokens, w_keyval.shape[1]),
            shape(cache_rows + tokens, w_keyval.shape[1]),
        ),
        1,
        15,
        3,
        left=1,
    )(
        place, own_rows, from_x, from_y, diag_top, diag_low, *rims, gain, w_bc, w_keyval, cos, sin,
        cache[0], w_pair,
    )

    bc_parts = [bc_block] + [swap(bc_block, turn) for turn in (1, 2, 3)]

    query, x_in, gate_z, steps, cumulative = call(
        project_kernel,
        (
            shape(tokens, w_query.shape[1]),
            shape(RIM + tokens, inner_width),
            shape(tokens, inner_width),
            shape(8, tokens, dtype=f32),
            shape(8, tokens, dtype=f32),
        ),
        2,
        6,
        4,
    )(dt_bias, a_log, normed, w_query, w_pair, w_dt.T, cos, sin)

    if n_seq <= 4:
        mine = [packed] + [cross(packed, turn) for turn in range(1, n_seq)]
    else:
        mine = [lax.all_gather(packed, "seq", axis=0)]
    other = [swap(block, 1) for block in mine]

    own_state, packet, x_conv, b_mat, c_mat = call(
        state_kernel,
        (
            shape(heads * HD, NS, dtype=f32),
            shape(heads * HD + LOGS, NS),
            shape(tokens, inner_width),
            shape(tokens, NS),
            shape(tokens, NS),
        ),
        1,
        11,
        2,
        scratch=[
            pltpu.VMEM((RIM + tokens, inner_width), f32),
            pltpu.VMEM((RIM + tokens, 2 * NS), f32),
        ],
    )(place, x_in, *bc_parts, tail_x, tail_bc, conv_x, conv_bc, steps, cumulative)

    def join(first, second, bit):
        return call(
            functools.partial(join_kernel, bit=bit), shape(heads * HD + LOGS, NS), 1, 2, 1
        )(place, first, second)

    near = far = jnp.zeros_like(packet)
    near_on = far_on = jnp.int32(0)
    total, group = packet, 1
    while group < n_seq:
        received = cross(total, group)
        on = (seq_pos // group) % 2
        if group * 2 == n_seq:
            far, far_on = received, on
        else:
            if n_seq == 4:
                near, near_on = received, on
            else:
                earlier = jnp.where(on == 1, received, jnp.zeros_like(received))
                near, near_on = earlier if group == 1 else join(near, earlier, 0), jnp.int32(1)
            total = join(total, received, group)
        group *= 2
    taken = jnp.stack([mp_pos, near_on, far_on]).astype(jnp.int32)

    y_inside = call(inside_kernel, shape(tokens, inner_width, dtype=f32), 1, 5, 1)(
        d_skip, c_mat, b_mat, steps, cumulative, x_conv
    )

    if n_seq <= 4:
        attended = call(
            functools.partial(attention_kernel, cache_rows=cache_rows, scale=HD**-0.5),
            shape(tokens, w_query.shape[1]),
            2,
            1 + 2 * n_seq,
            6,
            scratch=[
                pltpu.VMEM((tokens * w_query.shape[1] // HD, n_seq * (cache_rows + tokens)), f32)
            ],
        )(place, cache_len, query, *mine, *other)
    else:
        is_key = mp_pos % 2 == 0
        attended = attend_plain(
            query,
            *[
                jnp.concatenate(
                    [both[:, :cache_rows].reshape(-1, HD), both[:, cache_rows:].reshape(-1, HD)], axis=0
                )
                for both in (
                    jnp.where(is_key, mine[0], other[0]),
                    jnp.where(is_key, other[0], mine[0]),
                )
            ],
            length,
            jnp.arange(n_seq),
            cache_rows,
            seq_pos,
        )

    state_after, keep, keep_top, keep_low, to_x, to_y = call(
        finish_kernel,
        (
            shape(1, 1, heads, HD, NS, dtype=f32),
            shape(tokens, width, dtype=f32),
            shape(half, width, dtype=f32),
            shape(half, width, dtype=f32),
            shape(tokens, width),
            shape(tokens, width),
        ),
        1,
        12,
        4,
        scratch=[pltpu.VMEM((tokens, inner_width), bf16)],
    )(
        taken, near, far, ssm_init, own_state, c_mat, cumulative, y_inside, gate_z, mixer_gain,
        attended, w_attn_out, w_mamba_out,
    )

    top_in = swap(to_x, 1)
    low_in = swap(to_y, 2)
    top_last = swap((keep_top + top_in[half:].astype(f32)).astype(bf16), 2)
    low_last = swap((keep_low + low_in[half:].astype(f32)).astype(bf16), 1)
    summed = keep + own_rows.astype(f32)
    summed = summed + jnp.concatenate(
        [
            top_in[:half].astype(f32) + top_last.astype(f32),
            low_in[:half].astype(f32) + low_last.astype(f32),
        ],
        axis=0,
    )
    return (summed.astype(bf16)[None], kv_block[None], state_after)


def solution(mesh):
    placed = (
        P("req", "seq", "mp"),
        P(),
        P(None, "mp"),
        P(None, "mp"),
        P("mp", None),
        P(None, None, "mp"),
        P(None, "mp"),
        P(None, "mp"),
        P("mp"),
        P("mp"),
        P("mp"),
        P(None, "mp"),
        P(),
        P("mp"),
        P("mp", None),
        P("req", "seq", "mp"),
        P("req"),
        P("req", None, "mp"),
        P("req", None, None),
        P("req", "mp", None, None),
    )
    return jax.shard_map(
        shards,
        mesh=mesh,
        in_specs=placed,
        out_specs=(P("req", "seq", "mp"), P("req", "seq", "mp"), P("req", "seq", "mp", None, None)),
        check_vma=False,
    )
```

time: 220 us -> 80.2 us (0.36)
  waiting for transfers between devices: 96.5 us -> 23.2 us
  blocking collectives: 38.9 us -> 0 us
  other arithmetic: 30 us -> 2.54 us
  matrix products: 22.9 us -> 0 us
  starting transfers between devices: 6.94 us -> 29.8 us
  Pallas kernels: 0 us -> 18.8 us
  between operations: 14.9 us -> 1.6 us
  local copies, waits for them, and re-layouts: 8.74 us -> 3.98 us
    all_gather x3 -> x0, waiting for transfers between devices: 56.2 us -> none  [the longest x1 40.4 us: shards(): piece = lax.all_gather(local_rows, 'seq', axis=0, tiled=True)]
    reduce_scatter x1 -> x0, waiting for transfers between devices: 39.6 us -> none  [shards(): summed = lax.psum_scatter(term, 'mp', scatter_dimension=1, tiled=True)]
    all_gather x4 -> x0, blocking collectives: 38.9 us -> none  [the longest x1 12.1 us: shards(): lax.all_gather(cache[0], 'mp', axis=1, tiled=True)]
    ppermute x2 -> x24, waiting for transfers between devices: 0.01 us -> 23.2 us  [the longest x18 17 us: swap(): lax.ppermute(block, 'mp', [(i, i ^ turn) for i in range(lax.axis_size('mp...]
    ppermute x2 -> x24, starting transfers between devices: 6.78 us -> 29.8 us  [the longest x18 21.7 us: swap(): lax.ppermute(block, 'mp', [(i, i ^ turn) for i in range(lax.axis_size('mp...]
    dot_general x13 -> x0, matrix products: 22.9 us -> none  [the longest x1 2.68 us: shards(): jnp.dot(mixed, w_mamba_out, preferred_element_type=jnp.float32)]
    pallas_call x0 -> x7, Pallas kernels: none -> 18.8 us  [the longest x1 4.98 us: shards(): call(project_kernel, (shape(tokens, w_query.shape[1]), shape(RIM + tokens...]
    convert_element_type x9 -> x3, other arithmetic: 6.49 us -> 0.09 us  [the longest x1 0.04 us: shards(): low_last = swap((keep_low + low_in[half:].astype(f32)).astype(bf16), 1)]
  transfers between devices with their start and end apart: 6 -> 24, of which waited for: 3 -> 8; matrix products, arithmetic and copies ran while one was open for 18% -> 7% of each run, Pallas kernels for 0% -> 15%
where the time goes in v2:
time: 80.2 us; the launch traced here: 80 us
  starting transfers between devices  29.8 us (37%)
  waiting for transfers between devices  23.2 us (29%)
  Pallas kernels  18.8 us (23%)
  local copies, waits for them, and re-layouts  3.98 us (5%)
  other arithmetic  2.54 us (3%)
  between operations  1.6 us (2%)
    ppermute x18, starting transfers between devices, swap(): lax.ppermute(block, 'mp', [(i, i ^ turn) for i in range(lax.axis_size('mp...  21.7 us
    ppermute x18, waiting for transfers between devices, swap(): lax.ppermute(block, 'mp', [(i, i ^ turn) for i in range(lax.axis_size('mp...  17 us
    ppermute x5, starting transfers between devices, cross(): lax.ppermute(block, 'seq', [(i, i ^ turn) for i in range(lax.axis_size('s...  6.52 us
    ppermute x5, waiting for transfers between devices, cross(): lax.ppermute(block, 'seq', [(i, i ^ turn) for i in range(lax.axis_size('s...  6.2 us
    pallas_call x1, Pallas kernels, shards(): call(project_kernel, (shape(tokens, w_query.shape[1]), shape(RIM + tokens...  4.98 us
    pallas_call x1, Pallas kernels, shards(): call(functools.partial(attention_kernel, cache_rows=cache_rows, scale=HD...  3.71 us
    pallas_call x1, Pallas kernels, shards(): call(finish_kernel, (shape(1, 1, heads, HD, NS, dtype=f32), shape(tokens,...  3.46 us
    unnamed x35, local copies, waits for them, and re-layouts  3.18 us
  transfers between devices with their start and end apart: 24, of which 8 were waited for; matrix products, arithmetic and copies ran while one was open for 7% of the time, Pallas kernels for 15%

profile of v2, /device:TPU:0, one launch (start us, length us, event | category | flops | bytes accessed | tf_op | source)
XLA Modules:
  0.0 80.0 jit_solution(16602874343915898380)
XLA Ops:
  0.6 3.0 %collective-permute-start = (bf16[256,768]{1,0:T(8,128)(2,1)}, bf16[256,768]{1,0:T(8,128)(2,1)S(1)}, u32[]{:S(2)}, u32[]{:S(2)}) collective-permute-start(bf16[256,768]{1,0:T(8,128)(2,1)} %bitcast.21), channel_id=1, source_target_pairs={{0,2},{2,0},{4,6},{6,4},{1,3},{3,1},{5,7},{7,5},{8,10},{10,8},{12,... | collective-permute-start | bytes 1179656 | tf_op jit(solution)/shard_map/ppermute | solution.py:45
  3.6 1.5 %collective-permute-start.1 = (bf16[256,768]{1,0:T(8,128)(2,1)}, bf16[256,768]{1,0:T(8,128)(2,1)S(1)}, u32[]{:S(2)}, u32[]{:S(2)}) collective-permute-start(bf16[256,768]{1,0:T(8,128)(2,1)} %bitcast.22), channel_id=1, source_target_pairs={{0,4},{2,6},{4,0},{6,2},{1,5},{3,7},{5,1},{7,3},{8,12},{10,14},{12... | collective-permute-start | bytes 1179656 | tf_op jit(solution)/shard_map/ppermute | solution.py:45
  5.9 1.6 %collective-permute-start.4 = (bf16[16,768]{1,0:T(8,128)(2,1)S(1)}, bf16[16,768]{1,0:T(8,128)(2,1)S(1)}, u32[]{:S(2)}, u32[]{:S(2)}) collective-permute-start(bf16[16,768]{1,0:T(8,128)(2,1)S(1)} %slice_bitcast_fusion), channel_id=1, source_target_pairs={{0,8},{8,16},{16,24},{24,0},{1,9},{9,17},{17,25},{25,1},{2,10},{10... | collective-permute-start | bytes 73736 | tf_op jit(solution)/shard_map/ppermute | solution.py:54
  8.3 4.7 %collective-permute-done.from_x = bf16[256,768]{1,0:T(8,128)(2,1)S(1)} collective-permute-done((bf16[256,768]{1,0:T(8,128)(2,1)}, bf16[256,768]{1,0:T(8,128)(2,1)S(1)}, u32[]{:S(2)}, u32[]{:S(2)}) %collective-permute-start) | collective-permute-done | bytes 393248 | tf_op jit(solution)/shard_map/ppermute | solution.py:45
  13.0 1.8 %collective-permute-start.2 = (bf16[128,768]{1,0:T(8,128)(2,1)S(1)}, bf16[128,768]{1,0:T(8,128)(2,1)S(1)}, u32[]{:S(2)}, u32[]{:S(2)}) collective-permute-start(bf16[128,768]{1,0:T(8,128)(2,1)S(1)} %slice.32), channel_id=1, source_target_pairs={{0,4},{2,6},{4,0},{6,2},{1,5},{3,7},{5,1},{7,3},{8,12},{10,14},{12... | collective-permute-start | bytes 589832 | tf_op jit(solution)/shard_map/ppermute | solution.py:45
  14.8 1.6 %collective-permute-start.3 = (bf16[128,768]{1,0:T(8,128)(2,1)S(1)}, bf16[128,768]{1,0:T(8,128)(2,1)S(1)}, u32[]{:S(2)}, u32[]{:S(2)}) collective-permute-start(bf16[128,768]{1,0:T(8,128)(2,1)S(1)} %slice.33), channel_id=1, source_target_pairs={{0,2},{2,0},{4,6},{6,4},{1,3},{3,1},{5,7},{7,5},{8,10},{10,8},{12,... | collective-permute-start | bytes 589832 | tf_op jit(solution)/shard_map/ppermute | solution.py:45
  18.7 1.8 %collective-permute-start.7 = (bf16[16,768]{1,0:T(8,128)(2,1)S(1)}, bf16[16,768]{1,0:T(8,128)(2,1)S(1)}, u32[]{:S(2)}, u32[]{:S(2)}) collective-permute-start(bf16[16,768]{1,0:T(8,128)(2,1)S(1)} %collective-permute-done.4.rim0), channel_id=1, source_target_pairs={{0,6},{2,4},{4,2},{6,0},{1,7},{3,5},{5,3},{7,1},{8,14},{10,12},{12... | collective-permute-start | bytes 73736 | tf_op jit(solution)/shard_map/ppermute | solution.py:45
  21.3 3.1 %copy.25 = bf16[3072,2,384]{2,0,1:T(8,128)(2,1)S(1)} copy(bf16[3072,2,384]{2,1,0:T(2,128)(2,1)} %param.25) | data formatting | bytes 9437184 | tf_op args[5]
  24.5 3.0 %shard_map.211 = (bf16[272,3072]{1,0:T(8,128)(2,1)S(1)}, bf16[272,128]{1,0:T(8,128)(2,1)S(1)}, bf16[256,128]{1,0:T(8,128)(2,1)}, bf16[512,128]{1,0:T(8,128)(2,1)S(1)}) custom-call(s32[3]{0:T(128)S(1)} %pad_add_fusion.1.place, bf16[256,768]{1,0:T(8,128)(2,1)S(1)} %bitcast.23, bf16[256,768]{1,0:T(8,128)(2,1)S(1)} %collective-permute-done.from_x, ...), custom_call_target="tpu_custom_call" | custom-call | flops 3000000000 | tf_op jit(solution)/shard_map/pallas_call | solution.py:381
  29.2 1.8 %collective-permute-start.10 = (bf16[272,128]{1,0:T(8,128)(2,1)S(1)}, bf16[272,128]{1,0:T(8,128)(2,1)S(1)}, u32[]{:S(2)}, u32[]{:S(2)}) collective-permute-start(bf16[272,128]{1,0:T(8,128)(2,1)S(1)} %get-tuple-element.25.bc0), channel_id=1, source_target_pairs={{0,6},{2,4},{4,2},{6,0},{1,7},{3,5},{5,3},{7,1},{8,14},{10,12},{12... | collective-permute-start | bytes 208904 | tf_op jit(solution)/shard_map/ppermute | solution.py:45
  31.1 1.6 %collective-permute-start.13 = (bf16[512,128]{1,0:T(8,128)(2,1)S(1)}, bf16[512,128]{1,0:T(8,128)(2,1)S(1)}, u32[]{:S(2)}, u32[]{:S(2)}) collective-permute-start(bf16[512,128]{1,0:T(8,128)(2,1)S(1)} %get-tuple-element.35.refs_0_), channel_id=1, source_target_pairs={{0,8},{8,0},{16,24},{24,16},{1,9},{9,1},{17,25},{25,17},{2,10},{10... | collective-permute-start | bytes 393224 | tf_op jit(solution)/shard_map/ppermute | solution.py:49
  32.6 2.6 %collective-permute-start.14 = (bf16[512,128]{1,0:T(8,128)(2,1)S(1)}, bf16[512,128]{1,0:T(8,128)(2,1)S(1)}, u32[]{:S(2)}, u32[]{:S(2)}) collective-permute-start(bf16[512,128]{1,0:T(8,128)(2,1)S(1)} %get-tuple-element.35.refs_0_), channel_id=1, source_target_pairs={{0,16},{8,24},{16,0},{24,8},{1,17},{9,25},{17,1},{25,9},{2,18},{10... | collective-permute-start | bytes 393224 | tf_op jit(solution)/shard_map/ppermute | solution.py:49
  35.3 5.0 %shard_map.212 = (bf16[256,256]{1,0:T(8,128)(2,1)S(1)}, bf16[272,384]{1,0:T(8,128)(2,1)S(1)}, bf16[256,384]{1,0:T(8,128)(2,1)S(1)}, f32[8,256]{1,0:T(8,128)S(1)}, f32[8,256]{1,0:T(8,128)S(1)}) custom-call(f32[3]{0:T(128)S(1)} %copy-done.13, f32[3]{0:T(128)S(1)} %copy-done.14, bf16[272,3072]{1,0:T(8,128)(2,1)S(1)} %get-tuple-element.23.normed, ...), custom_call_target="tpu_custom_call" | custom-call | flops 4000000000 | tf_op jit(solution)/shard_map/pallas_call | solution.py:400
  40.6 1.9 %shard_map.213 = (f32[384,256]{1,0:T(8,128)S(1)}, bf16[416,256]{1,0:T(8,128)(2,1)S(1)}, bf16[256,384]{1,0:T(8,128)(2,1)S(1)}, bf16[256,256]{1,0:T(8,128)(2,1)S(1)}, bf16[256,256]{1,0:T(8,128)(2,1)S(1)}) custom-call(s32[3]{0:T(128)S(1)} %pad_add_fusion.1.place, bf16[272,384]{1,0:T(8,128)(2,1)S(1)} %get-tuple-element.24.x_in, ...), custom_call_target="tpu_custom_call" | custom-call | flops 2000000000 | tf_op jit(solution)/shard_map/pallas_call | solution.py:420
  43.9 1.5 %collective-permute-start.17 = (bf16[512,128]{1,0:T(8,128)(2,1)S(1)}, bf16[512,128]{1,0:T(8,128)(2,1)S(1)}, u32[]{:S(2)}, u32[]{:S(2)}) collective-permute-start(bf16[512,128]{1,0:T(8,128)(2,1)S(1)} %collective-permute-done.13.refs_1_), channel_id=1, source_target_pairs={{0,2},{2,0},{4,6},{6,4},{1,3},{3,1},{5,7},{7,5},{8,10},{10,8},{12,... | collective-permute-start | bytes 393224 | tf_op jit(solution)/shard_map/ppermute | solution.py:45
  45.9 1.3 %collective-permute-done.15.refs_3_ = bf16[512,128]{1,0:T(8,128)(2,1)S(1)} collective-permute-done((bf16[512,128]{1,0:T(8,128)(2,1)S(1)}, bf16[512,128]{1,0:T(8,128)(2,1)S(1)}, u32[]{:S(2)}, u32[]{:S(2)}) %collective-permute-start.15) | collective-permute-done | bytes 131104 | tf_op jit(solution)/shard_map/ppermute | solution.py:49
  48.8 1.9 %collective-permute-done.11.second.near = bf16[416,256]{1,0:T(8,128)(2,1)S(1)} collective-permute-done((bf16[416,256]{1,0:T(8,128)(2,1)S(1)}, bf16[416,256]{1,0:T(8,128)(2,1)S(1)}, u32[]{:S(2)}, u32[]{:S(2)}) %collective-permute-start.11) | collective-permute-done | bytes 213024 | tf_op jit(solution)/shard_map/ppermute | solution.py:49
  51.4 1.3 %collective-permute-start.12 = (bf16[416,256]{1,0:T(8,128)(2,1)S(1)}, bf16[416,256]{1,0:T(8,128)(2,1)S(1)}, u32[]{:S(2)}, u32[]{:S(2)}) collective-permute-start(bf16[416,256]{1,0:T(8,128)(2,1)S(1)} %shard_map.214), channel_id=1, source_target_pairs={{0,16},{8,24},{16,0},{24,8},{1,17},{9,25},{17,1},{25,9},{2,18},{10... | collective-permute-start | bytes 638984 | tf_op jit(solution)/shard_map/ppermute | solution.py:49
  52.8 3.7 %shard_map.216.attended = bf16[256,256]{1,0:T(8,128)(2,1)S(1)} custom-call(s32[3]{0:T(128)S(1)} %pad_add_fusion.1.place, s32[1]{0:T(128)} %copy.26.length, bf16[256,256]{1,0:T(8,128)(2,1)S(1)} %get-tuple-element.34.query, bf16[512,128]{1,0:T(8,128)(2,1)S(1)} %get-tuple-element.35.refs_0_, bf16[512,128]{1,0:T(8,128)(2,1)S(1)} %collective-permute-done.13.refs_1_, ...), custom_call_target="tpu_custom_call" | custom-call | flops 6000000000 | tf_op jit(solution)/shard_map/pallas_call | solution.py:466
  56.5 3.0 %collective-permute-done.12.far = bf16[416,256]{1,0:T(8,128)(2,1)S(1)} collective-permute-done((bf16[416,256]{1,0:T(8,128)(2,1)S(1)}, bf16[416,256]{1,0:T(8,128)(2,1)S(1)}, u32[]{:S(2)}, u32[]{:S(2)}) %collective-permute-start.12) | collective-permute-done | bytes 213024 | tf_op jit(solution)/shard_map/ppermute | solution.py:49
  59.5 3.5 %shard_map.217 = (f32[1,1,3,128,256]{4,3,2,1,0:T(8,128)}, f32[256,768]{1,0:T(8,128)S(1)}, f32[128,768]{1,0:T(8,128)S(1)}, f32[128,768]{1,0:T(8,128)S(1)}, bf16[2...) custom-call(s32[3]{0:T(128)S(1)} %pad_add_fusion.place, bf16[416,256]{1,0:T(8,128)(2,1)S(1)} %collective-permute-done.11.second.near, ...), custom_call_target="tpu_custom_call" | custom-call | flops 4000000000 | tf_op jit(solution)/shard_map/pallas_call | solution.py:495
  64.7 8.1 %collective-permute-done.22 = bf16[256,768]{1,0:T(8,128)(2,1)S(1)} collective-permute-done((bf16[256,768]{1,0:T(8,128)(2,1)S(1)}, bf16[256,768]{1,0:T(8,128)(2,1)S(1)}, u32[]{:S(2)}, u32[]{:S(2)}) %collective-permute-start.22) | collective-permute-done | bytes 393248 | tf_op jit(solution)/shard_map/ppermute | solution.py:45
  73.4 1.5 %collective-permute-start.21 = (bf16[128,768]{1,0:T(8,128)(2,1)S(1)}, bf16[128,768]{1,0:T(8,128)(2,1)S(1)}, u32[]{:S(2)}, u32[]{:S(2)}) collective-permute-start(bf16[128,768]{1,0:T(8,128)(2,1)S(1)} %add_convert_fusion.1), channel_id=1, source_target_pairs={{0,4},{2,6},{4,0},{6,2},{1,5},{3,7},{5,1},{7,3},{8,12},{10,14},{12... | collective-permute-start | bytes 589832 | tf_op jit(solution)/shard_map/ppermute | solution.py:45
  74.8 3.7 %collective-permute-done.23 = bf16[128,768]{1,0:T(8,128)(2,1)S(1)} collective-permute-done((bf16[128,768]{1,0:T(8,128)(2,1)S(1)}, bf16[128,768]{1,0:T(8,128)(2,1)S(1)}, u32[]{:S(2)}, u32[]{:S(2)}) %collective-permute-start.23) | collective-permute-done | bytes 196640 | tf_op jit(solution)/shard_map/ppermute | solution.py:45
  (83 shorter events, 14.0 us)
Async XLA Ops:
  0.6 12.3 %collective-permute-start = (bf16[256,768]{1,0:T(8,128)(2,1)}, bf16[256,768]{1,0:T(8,128)(2,1)S(1)}, u32[]{:S(2)}, u32[]{:S(2)}) collective-permute-start(bf16[256,768]{1,0:T(8,128)(2,1)} %bitcast.21), channel_id=1, source_target_pairs={{0,2},{2,0},{4,6},{6,4},{1,3},{3,1},{5,7},{7,5},{8,10},{10,8},{12,... | collective-permute-start | bytes 1179656 | tf_op jit(solution)/shard_map/ppermute | solution.py:45
  3.6 11.2 %collective-permute-start.1 = (bf16[256,768]{1,0:T(8,128)(2,1)}, bf16[256,768]{1,0:T(8,128)(2,1)S(1)}, u32[]{:S(2)}, u32[]{:S(2)}) collective-permute-start(bf16[256,768]{1,0:T(8,128)(2,1)} %bitcast.22), channel_id=1, source_target_pairs={{0,4},{2,6},{4,0},{6,2},{1,5},{3,7},{5,1},{7,3},{8,12},{10,14},{12... | collective-permute-start | bytes 1179656 | tf_op jit(solution)/shard_map/ppermute | solution.py:45
  5.9 11.0 %collective-permute-start.4 = (bf16[16,768]{1,0:T(8,128)(2,1)S(1)}, bf16[16,768]{1,0:T(8,128)(2,1)S(1)}, u32[]{:S(2)}, u32[]{:S(2)}) collective-permute-start(bf16[16,768]{1,0:T(8,128)(2,1)S(1)} %slice_bitcast_fusion), channel_id=1, source_target_pairs={{0,8},{8,16},{16,24},{24,0},{1,9},{9,17},{17,25},{25,1},{2,10},{10... | collective-permute-start | bytes 73736 | tf_op jit(solution)/shard_map/ppermute | solution.py:54
  13.0 11.4 %collective-permute-start.2 = (bf16[128,768]{1,0:T(8,128)(2,1)S(1)}, bf16[128,768]{1,0:T(8,128)(2,1)S(1)}, u32[]{:S(2)}, u32[]{:S(2)}) collective-permute-start(bf16[128,768]{1,0:T(8,128)(2,1)S(1)} %slice.32), channel_id=1, source_target_pairs={{0,4},{2,6},{4,0},{6,2},{1,5},{3,7},{5,1},{7,3},{8,12},{10,14},{12... | collective-permute-start | bytes 589832 | tf_op jit(solution)/shard_map/ppermute | solution.py:45
  14.8 9.6 %collective-permute-start.3 = (bf16[128,768]{1,0:T(8,128)(2,1)S(1)}, bf16[128,768]{1,0:T(8,128)(2,1)S(1)}, u32[]{:S(2)}, u32[]{:S(2)}) collective-permute-start(bf16[128,768]{1,0:T(8,128)(2,1)S(1)} %slice.33), channel_id=1, source_target_pairs={{0,2},{2,0},{4,6},{6,4},{1,3},{3,1},{5,7},{7,5},{8,10},{10,8},{12,... | collective-permute-start | bytes 589832 | tf_op jit(solution)/shard_map/ppermute | solution.py:45
  16.9 7.4 %collective-permute-start.5 = (bf16[16,768]{1,0:T(8,128)(2,1)S(1)}, bf16[16,768]{1,0:T(8,128)(2,1)S(1)}, u32[]{:S(2)}, u32[]{:S(2)}) collective-permute-start(bf16[16,768]{1,0:T(8,128)(2,1)S(1)} %collective-permute-done.4.rim0), channel_id=1, source_target_pairs={{0,2},{2,0},{4,6},{6,4},{1,3},{3,1},{5,7},{7,5},{8,10},{10,8},{12,... | collective-permute-start | bytes 73736 | tf_op jit(solution)/shard_map/ppermute | solution.py:45
  17.6 6.8 %collective-permute-start.6 = (bf16[16,768]{1,0:T(8,128)(2,1)S(1)}, bf16[16,768]{1,0:T(8,128)(2,1)S(1)}, u32[]{:S(2)}, u32[]{:S(2)}) collective-permute-start(bf16[16,768]{1,0:T(8,128)(2,1)S(1)} %collective-permute-done.4.rim0), channel_id=1, source_target_pairs={{0,4},{2,6},{4,0},{6,2},{1,5},{3,7},{5,1},{7,3},{8,12},{10,14},{12... | collective-permute-start | bytes 73736 | tf_op jit(solution)/shard_map/ppermute | solution.py:45
  18.7 5.7 %collective-permute-start.7 = (bf16[16,768]{1,0:T(8,128)(2,1)S(1)}, bf16[16,768]{1,0:T(8,128)(2,1)S(1)}, u32[]{:S(2)}, u32[]{:S(2)}) collective-permute-start(bf16[16,768]{1,0:T(8,128)(2,1)S(1)} %collective-permute-done.4.rim0), channel_id=1, source_target_pairs={{0,6},{2,4},{4,2},{6,0},{1,7},{3,5},{5,3},{7,1},{8,14},{10,12},{12... | collective-permute-start | bytes 73736 | tf_op jit(solution)/shard_map/ppermute | solution.py:45
  27.6 12.7 %collective-permute-start.8 = (bf16[272,128]{1,0:T(8,128)(2,1)S(1)}, bf16[272,128]{1,0:T(8,128)(2,1)S(1)}, u32[]{:S(2)}, u32[]{:S(2)}) collective-permute-start(bf16[272,128]{1,0:T(8,128)(2,1)S(1)} %get-tuple-element.25.bc0), channel_id=1, source_target_pairs={{0,2},{2,0},{4,6},{6,4},{1,3},{3,1},{5,7},{7,5},{8,10},{10,8},{12,... | collective-permute-start | bytes 208904 | tf_op jit(solution)/shard_map/ppermute | solution.py:45
  28.1 12.5 %collective-permute-start.9 = (bf16[272,128]{1,0:T(8,128)(2,1)S(1)}, bf16[272,128]{1,0:T(8,128)(2,1)S(1)}, u32[]{:S(2)}, u32[]{:S(2)}) collective-permute-start(bf16[272,128]{1,0:T(8,128)(2,1)S(1)} %get-tuple-element.25.bc0), channel_id=1, source_target_pairs={{0,4},{2,6},{4,0},{6,2},{1,5},{3,7},{5,1},{7,3},{8,12},{10,14},{12... | collective-permute-start | bytes 208904 | tf_op jit(solution)/shard_map/ppermute | solution.py:45
  29.2 11.3 %collective-permute-start.10 = (bf16[272,128]{1,0:T(8,128)(2,1)S(1)}, bf16[272,128]{1,0:T(8,128)(2,1)S(1)}, u32[]{:S(2)}, u32[]{:S(2)}) collective-permute-start(bf16[272,128]{1,0:T(8,128)(2,1)S(1)} %get-tuple-element.25.bc0), channel_id=1, source_target_pairs={{0,6},{2,4},{4,2},{6,0},{1,7},{3,5},{5,3},{7,1},{8,14},{10,12},{12... | collective-permute-start | bytes 208904 | tf_op jit(solution)/shard_map/ppermute | solution.py:45
  31.1 12.9 %collective-permute-start.13 = (bf16[512,128]{1,0:T(8,128)(2,1)S(1)}, bf16[512,128]{1,0:T(8,128)(2,1)S(1)}, u32[]{:S(2)}, u32[]{:S(2)}) collective-permute-start(bf16[512,128]{1,0:T(8,128)(2,1)S(1)} %get-tuple-element.35.refs_0_), channel_id=1, source_target_pairs={{0,8},{8,0},{16,24},{24,16},{1,9},{9,1},{17,25},{25,17},{2,10},{10... | collective-permute-start | bytes 393224 | tf_op jit(solution)/shard_map/ppermute | solution.py:49
  32.6 12.8 %collective-permute-start.14 = (bf16[512,128]{1,0:T(8,128)(2,1)S(1)}, bf16[512,128]{1,0:T(8,128)(2,1)S(1)}, u32[]{:S(2)}, u32[]{:S(2)}) collective-permute-start(bf16[512,128]{1,0:T(8,128)(2,1)S(1)} %get-tuple-element.35.refs_0_), channel_id=1, source_target_pairs={{0,16},{8,24},{16,0},{24,8},{1,17},{9,25},{17,1},{25,9},{2,18},{10... | collective-permute-start | bytes 393224 | tf_op jit(solution)/shard_map/ppermute | solution.py:49
  40.3 6.9 %collective-permute-start.15 = (bf16[512,128]{1,0:T(8,128)(2,1)S(1)}, bf16[512,128]{1,0:T(8,128)(2,1)S(1)}, u32[]{:S(2)}, u32[]{:S(2)}) collective-permute-start(bf16[512,128]{1,0:T(8,128)(2,1)S(1)} %get-tuple-element.35.refs_0_), channel_id=1, source_target_pairs={{0,24},{8,16},{16,8},{24,0},{1,25},{9,17},{17,9},{25,1},{2,26},{10... | collective-permute-start | bytes 393224 | tf_op jit(solution)/shard_map/ppermute | solution.py:49
  42.5 8.2 %collective-permute-start.11 = (bf16[416,256]{1,0:T(8,128)(2,1)S(1)}, bf16[416,256]{1,0:T(8,128)(2,1)S(1)}, u32[]{:S(2)}, u32[]{:S(2)}) collective-permute-start(bf16[416,256]{1,0:T(8,128)(2,1)S(1)} %get-tuple-element.28.first), channel_id=1, source_target_pairs={{0,8},{8,0},{16,24},{24,16},{1,9},{9,1},{17,25},{25,17},{2,10},{10... | collective-permute-start | bytes 638984 | tf_op jit(solution)/shard_map/ppermute | solution.py:49
  43.4 9.4 %collective-permute-start.16 = (bf16[512,128]{1,0:T(8,128)(2,1)S(1)}, bf16[512,128]{1,0:T(8,128)(2,1)S(1)}, u32[]{:S(2)}, u32[]{:S(2)}) collective-permute-start(bf16[512,128]{1,0:T(8,128)(2,1)S(1)} %get-tuple-element.35.refs_0_), channel_id=1, source_target_pairs={{0,2},{2,0},{4,6},{6,4},{1,3},{3,1},{5,7},{7,5},{8,10},{10,8},{12,... | collective-permute-start | bytes 393224 | tf_op jit(solution)/shard_map/ppermute | solution.py:45
  43.9 8.8 %collective-permute-start.17 = (bf16[512,128]{1,0:T(8,128)(2,1)S(1)}, bf16[512,128]{1,0:T(8,128)(2,1)S(1)}, u32[]{:S(2)}, u32[]{:S(2)}) collective-permute-start(bf16[512,128]{1,0:T(8,128)(2,1)S(1)} %collective-permute-done.13.refs_1_), channel_id=1, source_target_pairs={{0,2},{2,0},{4,6},{6,4},{1,3},{3,1},{5,7},{7,5},{8,10},{10,8},{12,... | collective-permute-start | bytes 393224 | tf_op jit(solution)/shard_map/ppermute | solution.py:45
  45.4 7.3 %collective-permute-start.18 = (bf16[512,128]{1,0:T(8,128)(2,1)S(1)}, bf16[512,128]{1,0:T(8,128)(2,1)S(1)}, u32[]{:S(2)}, u32[]{:S(2)}) collective-permute-start(bf16[512,128]{1,0:T(8,128)(2,1)S(1)} %collective-permute-done.14.refs_2_), channel_id=1, source_target_pairs={{0,2},{2,0},{4,6},{6,4},{1,3},{3,1},{5,7},{7,5},{8,10},{10,8},{12,... | collective-permute-start | bytes 393224 | tf_op jit(solution)/shard_map/ppermute | solution.py:45
  47.2 5.6 %collective-permute-start.19 = (bf16[512,128]{1,0:T(8,128)(2,1)S(1)}, bf16[512,128]{1,0:T(8,128)(2,1)S(1)}, u32[]{:S(2)}, u32[]{:S(2)}) collective-permute-start(bf16[512,128]{1,0:T(8,128)(2,1)S(1)} %collective-permute-done.15.refs_3_), channel_id=1, source_target_pairs={{0,2},{2,0},{4,6},{6,4},{1,3},{3,1},{5,7},{7,5},{8,10},{10,8},{12,... | collective-permute-start | bytes 393224 | tf_op jit(solution)/shard_map/ppermute | solution.py:45
  51.4 8.1 %collective-permute-start.12 = (bf16[416,256]{1,0:T(8,128)(2,1)S(1)}, bf16[416,256]{1,0:T(8,128)(2,1)S(1)}, u32[]{:S(2)}, u32[]{:S(2)}) collective-permute-start(bf16[416,256]{1,0:T(8,128)(2,1)S(1)} %shard_map.214), channel_id=1, source_target_pairs={{0,16},{8,24},{16,0},{24,8},{1,17},{9,25},{17,1},{25,9},{2,18},{10... | collective-permute-start | bytes 638984 | tf_op jit(solution)/shard_map/ppermute | solution.py:49
  63.0 9.8 %collective-permute-start.22 = (bf16[256,768]{1,0:T(8,128)(2,1)S(1)}, bf16[256,768]{1,0:T(8,128)(2,1)S(1)}, u32[]{:S(2)}, u32[]{:S(2)}) collective-permute-start(bf16[256,768]{1,0:T(8,128)(2,1)S(1)} %get-tuple-element.39), channel_id=1, source_target_pairs={{0,4},{2,6},{4,0},{6,2},{1,5},{3,7},{5,1},{7,3},{8,12},{10,14},{12... | collective-permute-start | bytes 1179656 | tf_op jit(solution)/shard_map/ppermute | solution.py:45
  63.5 9.8 %collective-permute-start.20 = (bf16[256,768]{1,0:T(8,128)(2,1)S(1)}, bf16[256,768]{1,0:T(8,128)(2,1)S(1)}, u32[]{:S(2)}, u32[]{:S(2)}) collective-permute-start(bf16[256,768]{1,0:T(8,128)(2,1)S(1)} %get-tuple-element.37), channel_id=1, source_target_pairs={{0,2},{2,0},{4,6},{6,4},{1,3},{3,1},{5,7},{7,5},{8,10},{10,8},{12,... | collective-permute-start | bytes 1179656 | tf_op jit(solution)/shard_map/ppermute | solution.py:45
  72.8 5.7 %collective-permute-start.23 = (bf16[128,768]{1,0:T(8,128)(2,1)S(1)}, bf16[128,768]{1,0:T(8,128)(2,1)S(1)}, u32[]{:S(2)}, u32[]{:S(2)}) collective-permute-start(bf16[128,768]{1,0:T(8,128)(2,1)S(1)} %add_convert_fusion), channel_id=1, source_target_pairs={{0,2},{2,0},{4,6},{6,4},{1,3},{3,1},{5,7},{7,5},{8,10},{10,8},{12,... | collective-permute-start | bytes 589832 | tf_op jit(solution)/shard_map/ppermute | solution.py:45
  73.4 5.7 %collective-permute-start.21 = (bf16[128,768]{1,0:T(8,128)(2,1)S(1)}, bf16[128,768]{1,0:T(8,128)(2,1)S(1)}, u32[]{:S(2)}, u32[]{:S(2)}) collective-permute-start(bf16[128,768]{1,0:T(8,128)(2,1)S(1)} %add_convert_fusion.1), channel_id=1, source_target_pairs={{0,4},{2,6},{4,0},{6,2},{1,5},{3,7},{5,1},{7,3},{8,12},{10,14},{12... | collective-permute-start | bytes 589832 | tf_op jit(solution)/shard_map/ppermute | solution.py:45
  (17 other events, 106.9 us)

commit v3 on v2

--- a/solution.py
+++ b/solution.py
@@ -111,13 +111,10 @@
     return jnp.maximum(v, 0.0) + jnp.log1p(jnp.exp(-jnp.abs(v)))
 
 
-def project_kernel(
-    dt_bias, a_log, normed, w_query, w_inner, w_dt, cos, sin, query, x_in, gate_z, steps, cumulative
-):
-    tokens = cos.shape[0]
+def steps_kernel(dt_bias, a_log, normed, w_inner, w_dt, x_in, steps, cumulative):
+    tokens = steps.shape[1]
     x_in[...] = dot(normed[...], w_inner[1]).astype(bf16)
-    current = normed[RIM:, :]
-    raw = jnp.concatenate([dot_nt(w_dt[...], current), jnp.zeros((5, tokens), f32)], axis=0)
+    raw = jnp.concatenate([dot_nt(w_dt[...], normed[RIM:, :]), jnp.zeros((5, tokens), f32)], axis=0)
     head = lax.broadcasted_iota(jnp.int32, (8, tokens), 0)
     bias = jnp.zeros((8, tokens), f32)
     rate = jnp.zeros((8, tokens), f32)
@@ -133,6 +130,11 @@
     cumulative[...] = jnp.dot(
         decay, upper, preferred_element_type=f32, precision=lax.Precision.HIGHEST
     )
+
+
+def query_kernel(normed, w_query, w_inner, cos, sin, *refs):
+    query, gate_z = refs[-2:]
+    current = normed[RIM:, :]
     gate_z[...] = dot(current, w_inner[0]).astype(bf16)
     projected = dot(current, w_query[...])
     for h in range(projected.shape[1] // HD):
@@ -218,9 +220,19 @@
     packet[size:, :] = logs_of(first_log + second_log)
 
 
+def term_of(me, attended, mixed, w_attn, w_mamba, width):
+    def term(turn, start, count):
+        columns = pl.ds(pl.multiple_of((me ^ turn) * width, 128), width)
+        return dot(attended[start : start + count, :], w_attn[:, columns]) + dot(
+            mixed[start : start + count, :], w_mamba[:, columns]
+        )
+
+    return term
+
+
 def finish_kernel(
     place, near, far, init, own, c_mat, cumulative, y, gate_z, gain, attended, w_attn, w_mamba,
-    states, keep, keep_top, keep_low, to_x, to_y, mixed,
+    states, mixed, far_x, far_y,
 ):
     me = place[0]
     heads = init.shape[1]
@@ -248,22 +260,22 @@
         mean_sq = jnp.sum(gated * gated, axis=1, keepdims=True) * (1.0 / HD)
         mixed[:, block] = (gated * lax.rsqrt(mean_sq + epsilon) * gain[:, block]).astype(bf16)
 
-    width = keep.shape[1]
-
-    def term(turn, start, count):
-        columns = pl.ds(pl.multiple_of((me ^ turn) * width, 128), width)
-        return dot(attended[start : start + count, :], w_attn[:, columns]) + dot(
-            mixed[start : start + count, :], w_mamba[:, columns]
-        )
-
-    to_x[:half, :] = term(1, 0, half).astype(bf16)
-    low_one = term(1, half, half)
-    keep_low[...] = low_one
-    to_y[:half, :] = term(2, half, half).astype(bf16)
+    term = term_of(me, attended, mixed, w_attn, w_mamba, far_x.shape[1])
+    far_x[...] = term(3, 0, half).astype(bf16)
+    far_y[...] = term(3, half, half).astype(bf16)
+
+
+def rest_kernel(
+    place, attended, mixed, w_attn, w_mamba, own, to_x, to_y, keep, keep_top, keep_low
+):
+    tokens, width = own.shape
+    half = tokens // 2
+    term = term_of(place[0], attended, mixed, w_attn, w_mamba, width)
+    to_x[...] = term(1, 0, half).astype(bf16)
+    to_y[...] = term(2, half, half).astype(bf16)
     keep_top[...] = term(2, 0, half)
-    to_x[half:, :] = term(3, 0, half).astype(bf16)
-    to_y[half:, :] = term(3, half, half).astype(bf16)
-    keep[...] = term(0, 0, tokens)
+    keep_low[...] = term(1, half, half)
+    keep[...] = term(0, 0, tokens) + own[...].astype(f32)
 
 
 def attention_kernel(place, length, query, *refs, cache_rows, scale):
@@ -397,19 +409,17 @@
 
     bc_parts = [bc_block] + [swap(bc_block, turn) for turn in (1, 2, 3)]
 
-    query, x_in, gate_z, steps, cumulative = call(
-        project_kernel,
+    x_in, steps, cumulative = call(
+        steps_kernel,
         (
-            shape(tokens, w_query.shape[1]),
             shape(RIM + tokens, inner_width),
-            shape(tokens, inner_width),
             shape(8, tokens, dtype=f32),
             shape(8, tokens, dtype=f32),
         ),
         2,
-        6,
-        4,
-    )(dt_bias, a_log, normed, w_query, w_pair, w_dt.T, cos, sin)
+        3,
+        2,
+    )(dt_bias, a_log, normed, w_pair, w_dt.T)
 
     if n_seq <= 4:
         mine = [packed] + [cross(packed, turn) for turn in range(1, n_seq)]
@@ -458,6 +468,14 @@
         group *= 2
     taken = jnp.stack([mp_pos, near_on, far_on]).astype(jnp.int32)
 
+    query, gate_z = call(
+        query_kernel,
+        (shape(tokens, w_query.shape[1]), shape(tokens, inner_width)),
+        0,
+        5,
+        2,
+        left=1,
+    )(normed, w_query, w_pair, cos, sin, b_mat)
     y_inside = call(inside_kernel, shape(tokens, inner_width, dtype=f32), 1, 5, 1)(
         d_skip, c_mat, b_mat, steps, cumulative, x_conv
     )
@@ -492,34 +510,45 @@
             seq_pos,
         )
 
-    state_after, keep, keep_top, keep_low, to_x, to_y = call(
+    state_after, mixed, far_x, far_y = call(
         finish_kernel,
         (
             shape(1, 1, heads, HD, NS, dtype=f32),
+            shape(tokens, inner_width),
+            shape(half, width),
+            shape(half, width),
+        ),
+        1,
+        12,
+        3,
+    )(
+        taken, near, far, ssm_init, own_state, c_mat, cumulative, y_inside, gate_z, mixer_gain,
+        attended, w_attn_out, w_mamba_out,
+    )
+
+    far_x_in = swap(far_x, 1)
+    far_y_in = swap(far_y, 2)
+    to_x, to_y, keep, keep_top, keep_low = call(
+        rest_kernel,
+        (
+            shape(half, width),
+            shape(half, width),
             shape(tokens, width, dtype=f32),
             shape(half, width, dtype=f32),
             shape(half, width, dtype=f32),
-            shape(tokens, width),
-            shape(tokens, width),
         ),
         1,
-        12,
-        4,
-        scratch=[pltpu.VMEM((tokens, inner_width), bf16)],
-    )(
-        taken, near, far, ssm_init, own_state, c_mat, cumulative, y_inside, gate_z, mixer_gain,
-        attended, w_attn_out, w_mamba_out,
-    )
-
+        5,
+        2,
+    )(place, attended, mixed, w_attn_out, w_mamba_out, own_rows)
     top_in = swap(to_x, 1)
     low_in = swap(to_y, 2)
-    top_last = swap((keep_top + top_in[half:].astype(f32)).astype(bf16), 2)
-    low_last = swap((keep_low + low_in[half:].astype(f32)).astype(bf16), 1)
-    summed = keep + own_rows.astype(f32)
-    summed = summed + jnp.concatenate(
+    top_last = swap((keep_top + far_x_in.astype(f32)).astype(bf16), 2)
+    low_last = swap((keep_low + far_y_in.astype(f32)).astype(bf16), 1)
+    summed = keep + jnp.concatenate(
         [
-            top_in[:half].astype(f32) + top_last.astype(f32),
-            low_in[:half].astype(f32) + low_last.astype(f32),
+            top_in.astype(f32) + top_last.astype(f32),
+            low_in.astype(f32) + low_last.astype(f32),
         ],
         axis=0,
     )

time: 80.2 us -> 75.9 us (0.946)
  waiting for transfers between devices: 23.2 us -> 15.3 us
  starting transfers between devices: 29.8 us -> 34 us
    ppermute x18 -> x20, waiting for transfers between devices: 17 us -> 12.8 us  [swap(): lax.ppermute(block, 'mp', [(i, i ^ turn) for i in range(lax.axis_size('mp...]
    ppermute x5, waiting for transfers between devices: 6.2 us -> 2.46 us  [cross(): lax.ppermute(block, 'seq', [(i, i ^ turn) for i in range(lax.axis_size('s...]
    ppermute x5, starting transfers between devices: 6.52 us -> 8.69 us  [cross(): lax.ppermute(block, 'seq', [(i, i ^ turn) for i in range(lax.axis_size('s...]
    ppermute x18 -> x20, starting transfers between devices: 21.7 us -> 23.7 us  [swap(): lax.ppermute(block, 'mp', [(i, i ^ turn) for i in range(lax.axis_size('mp...]
    pallas_call x1, Pallas kernels: 3.46 us -> 2.5 us  [shards(): call(finish_kernel, (shape(1, 1, heads, HD, NS, dtype=f32), shape(tokens,...]
    pallas_call x1 -> x3, Pallas kernels: 4.98 us -> 5.46 us  [the longest x1 2.34 us: shards(): call(steps_kernel, (shape(RIM + tokens, inner_width), shape(8, tokens, dt...]
  transfers between devices with their start and end apart: 24 -> 26, of which waited for: 8 -> 7; matrix products, arithmetic and copies ran while one was open for 7% -> 7% of each run, Pallas kernels for 15% -> 17%
where the time goes in v3:
time: 75.9 us; the launch traced here: 75.7 us
  starting transfers between devices  34 us (45%)
  Pallas kernels  18.3 us (24%)
  waiting for transfers between devices  15.3 us (20%)
  local copies, waits for them, and re-layouts  3.98 us (5%)
  other arithmetic  2.49 us (3%)
  between operations  1.65 us (2%)
    ppermute x20, starting transfers between devices, swap(): lax.ppermute(block, 'mp', [(i, i ^ turn) for i in range(lax.axis_size('mp...  23.7 us
    ppermute x20, waiting for transfers between devices, swap(): lax.ppermute(block, 'mp', [(i, i ^ turn) for i in range(lax.axis_size('mp...  12.8 us
    ppermute x5, starting transfers between devices, cross(): lax.ppermute(block, 'seq', [(i, i ^ turn) for i in range(lax.axis_size('s...  8.69 us
    pallas_call x1, Pallas kernels, shards(): call(functools.partial(attention_kernel, cache_rows=cache_rows, scale=HD...  3.67 us
    unnamed x35, local copies, waits for them, and re-layouts  3.18 us
    pallas_call x1, Pallas kernels, shards(): call(norm_kernel, (shape(RIM + tokens, 4 * width), shape(RIM + tokens, w_...  3.04 us
    pallas_call x1, Pallas kernels, shards(): call(finish_kernel, (shape(1, 1, heads, HD, NS, dtype=f32), shape(tokens,...  2.5 us
    ppermute x5, waiting for transfers between devices, cross(): lax.ppermute(block, 'seq', [(i, i ^ turn) for i in range(lax.axis_size('s...  2.46 us
  transfers between devices with their start and end apart: 26, of which 7 were waited for; matrix products, arithmetic and copies ran while one was open for 7% of the time, Pallas kernels for 17%

profile of v3, /device:TPU:0, one launch (start us, length us, event | category | flops | bytes accessed | tf_op | source)
XLA Modules:
  0.0 75.7 jit_solution(4998814495548578405)
XLA Ops:
  0.6 3.0 %collective-permute-start = (bf16[256,768]{1,0:T(8,128)(2,1)}, bf16[256,768]{1,0:T(8,128)(2,1)S(1)}, u32[]{:S(2)}, u32[]{:S(2)}) collective-permute-start(bf16[256,768]{1,0:T(8,128)(2,1)} %bitcast.22), channel_id=1, source_target_pairs={{0,2},{2,0},{4,6},{6,4},{1,3},{3,1},{5,7},{7,5},{8,10},{10,8},{12,... | collective-permute-start | bytes 1179656 | tf_op jit(solution)/shard_map/ppermute | solution.py:45
  3.6 1.5 %collective-permute-start.1 = (bf16[256,768]{1,0:T(8,128)(2,1)}, bf16[256,768]{1,0:T(8,128)(2,1)S(1)}, u32[]{:S(2)}, u32[]{:S(2)}) collective-permute-start(bf16[256,768]{1,0:T(8,128)(2,1)} %bitcast.23), channel_id=1, source_target_pairs={{0,4},{2,6},{4,0},{6,2},{1,5},{3,7},{5,1},{7,3},{8,12},{10,14},{12... | collective-permute-start | bytes 1179656 | tf_op jit(solution)/shard_map/ppermute | solution.py:45
  5.9 1.6 %collective-permute-start.4 = (bf16[16,768]{1,0:T(8,128)(2,1)S(1)}, bf16[16,768]{1,0:T(8,128)(2,1)S(1)}, u32[]{:S(2)}, u32[]{:S(2)}) collective-permute-start(bf16[16,768]{1,0:T(8,128)(2,1)S(1)} %slice_bitcast_fusion), channel_id=1, source_target_pairs={{0,8},{8,16},{16,24},{24,0},{1,9},{9,17},{17,25},{25,1},{2,10},{10... | collective-permute-start | bytes 73736 | tf_op jit(solution)/shard_map/ppermute | solution.py:54
  8.8 4.1 %collective-permute-done.from_x = bf16[256,768]{1,0:T(8,128)(2,1)S(1)} collective-permute-done((bf16[256,768]{1,0:T(8,128)(2,1)}, bf16[256,768]{1,0:T(8,128)(2,1)S(1)}, u32[]{:S(2)}, u32[]{:S(2)}) %collective-permute-start) | collective-permute-done | bytes 393248 | tf_op jit(solution)/shard_map/ppermute | solution.py:45
  13.0 1.8 %collective-permute-start.2 = (bf16[128,768]{1,0:T(8,128)(2,1)S(1)}, bf16[128,768]{1,0:T(8,128)(2,1)S(1)}, u32[]{:S(2)}, u32[]{:S(2)}) collective-permute-start(bf16[128,768]{1,0:T(8,128)(2,1)S(1)} %slice.16), channel_id=1, source_target_pairs={{0,4},{2,6},{4,0},{6,2},{1,5},{3,7},{5,1},{7,3},{8,12},{10,14},{12... | collective-permute-start | bytes 589832 | tf_op jit(solution)/shard_map/ppermute | solution.py:45
  14.8 1.6 %collective-permute-start.3 = (bf16[128,768]{1,0:T(8,128)(2,1)S(1)}, bf16[128,768]{1,0:T(8,128)(2,1)S(1)}, u32[]{:S(2)}, u32[]{:S(2)}) collective-permute-start(bf16[128,768]{1,0:T(8,128)(2,1)S(1)} %slice.17), channel_id=1, source_target_pairs={{0,2},{2,0},{4,6},{6,4},{1,3},{3,1},{5,7},{7,5},{8,10},{10,8},{12,... | collective-permute-start | bytes 589832 | tf_op jit(solution)/shard_map/ppermute | solution.py:45
  18.2 1.8 %collective-permute-start.7 = (bf16[16,768]{1,0:T(8,128)(2,1)S(1)}, bf16[16,768]{1,0:T(8,128)(2,1)S(1)}, u32[]{:S(2)}, u32[]{:S(2)}) collective-permute-start(bf16[16,768]{1,0:T(8,128)(2,1)S(1)} %collective-permute-done.4.rim0), channel_id=1, source_target_pairs={{0,6},{2,4},{4,2},{6,0},{1,7},{3,5},{5,3},{7,1},{8,14},{10,12},{12... | collective-permute-start | bytes 73736 | tf_op jit(solution)/shard_map/ppermute | solution.py:45
  20.8 3.1 %copy.25 = bf16[3072,2,384]{2,0,1:T(8,128)(2,1)S(1)} copy(bf16[3072,2,384]{2,1,0:T(2,128)(2,1)} %param.25) | data formatting | bytes 9437184 | tf_op args[5]
  24.0 3.0 %shard_map.211 = (bf16[272,3072]{1,0:T(8,128)(2,1)S(1)}, bf16[272,128]{1,0:T(8,128)(2,1)S(1)}, bf16[256,128]{1,0:T(8,128)(2,1)}, bf16[512,128]{1,0:T(8,128)(2,1)S(1)}) custom-call(s32[3]{0:T(128)S(1)} %pad_add_fusion.place, bf16[256,768]{1,0:T(8,128)(2,1)S(1)} %bitcast.24, bf16[256,768]{1,0:T(8,128)(2,1)S(1)} %collective-permute-done.from_x, ...), custom_call_target="tpu_custom_call" | custom-call | flops 3000000000 | tf_op jit(solution)/shard_map/pallas_call | solution.py:393
  28.7 1.8 %collective-permute-start.10 = (bf16[272,128]{1,0:T(8,128)(2,1)S(1)}, bf16[272,128]{1,0:T(8,128)(2,1)S(1)}, u32[]{:S(2)}, u32[]{:S(2)}) collective-permute-start(bf16[272,128]{1,0:T(8,128)(2,1)S(1)} %get-tuple-element.28.bc0), channel_id=1, source_target_pairs={{0,6},{2,4},{4,2},{6,0},{1,7},{3,5},{5,3},{7,1},{8,14},{10,12},{12... | collective-permute-start | bytes 208904 | tf_op jit(solution)/shard_map/ppermute | solution.py:45
  30.6 1.6 %collective-permute-start.11 = (bf16[512,128]{1,0:T(8,128)(2,1)S(1)}, bf16[512,128]{1,0:T(8,128)(2,1)S(1)}, u32[]{:S(2)}, u32[]{:S(2)}) collective-permute-start(bf16[512,128]{1,0:T(8,128)(2,1)S(1)} %get-tuple-element.33.refs_0_), channel_id=1, source_target_pairs={{0,8},{8,0},{16,24},{24,16},{1,9},{9,1},{17,25},{25,17},{2,10},{10... | collective-permute-start | bytes 393224 | tf_op jit(solution)/shard_map/ppermute | solution.py:49
  32.1 2.6 %collective-permute-start.12 = (bf16[512,128]{1,0:T(8,128)(2,1)S(1)}, bf16[512,128]{1,0:T(8,128)(2,1)S(1)}, u32[]{:S(2)}, u32[]{:S(2)}) collective-permute-start(bf16[512,128]{1,0:T(8,128)(2,1)S(1)} %get-tuple-element.33.refs_0_), channel_id=1, source_target_pairs={{0,16},{8,24},{16,0},{24,8},{1,17},{9,25},{17,1},{25,9},{2,18},{10... | collective-permute-start | bytes 393224 | tf_op jit(solution)/shard_map/ppermute | solution.py:49
  34.8 2.3 %shard_map.212 = (bf16[272,384]{1,0:T(8,128)(2,1)S(1)}, f32[8,256]{1,0:T(8,128)S(1)}, f32[8,256]{1,0:T(8,128)S(1)}) custom-call(f32[3]{0:T(128)S(1)} %copy-done.13, f32[3]{0:T(128)S(1)} %copy-done.14, bf16[272,3072]{1,0:T(8,128)(2,1)S(1)} %get-tuple-element.26.normed, bf16[2,3072,384]{2,1,0:T(8,128)(2,1)S(1)} %bitcast.19, bf16[3,3072]{1,0:T(4,128)(2,1)S(1)} %bitcast.27), custom_call_target="tpu_custom_call" | custom-call | flops 2000000000 | tf_op jit(solution)/shard_map/pallas_call | solution.py:412
  38.0 1.9 %shard_map.213 = (f32[384,256]{1,0:T(8,128)S(1)}, bf16[416,256]{1,0:T(8,128)(2,1)S(1)}, bf16[256,384]{1,0:T(8,128)(2,1)S(1)}, bf16[256,256]{1,0:T(8,128)(2,1)S(1)}, bf16[256,256]{1,0:T(8,128)(2,1)S(1)}) custom-call(s32[3]{0:T(128)S(1)} %pad_add_fusion.place, bf16[272,384]{1,0:T(8,128)(2,1)S(1)} %get-tuple-element.27.x_in, ...), custom_call_target="tpu_custom_call" | custom-call | flops 2000000000 | tf_op jit(solution)/shard_map/pallas_call | solution.py:430
  42.1 1.6 %collective-permute-start.15 = (bf16[512,128]{1,0:T(8,128)(2,1)S(1)}, bf16[512,128]{1,0:T(8,128)(2,1)S(1)}, u32[]{:S(2)}, u32[]{:S(2)}) collective-permute-start(bf16[512,128]{1,0:T(8,128)(2,1)S(1)} %collective-permute-done.11.refs_1_), channel_id=1, source_target_pairs={{0,2},{2,0},{4,6},{6,4},{1,3},{3,1},{5,7},{7,5},{8,10},{10,8},{12,... | collective-permute-start | bytes 393224 | tf_op jit(solution)/shard_map/ppermute | solution.py:45
  47.4 3.5 %collective-permute-start.19 = (bf16[416,256]{1,0:T(8,128)(2,1)S(1)}, bf16[416,256]{1,0:T(8,128)(2,1)S(1)}, u32[]{:S(2)}, u32[]{:S(2)}) collective-permute-start(bf16[416,256]{1,0:T(8,128)(2,1)S(1)} %shard_map.216), channel_id=1, source_target_pairs={{0,16},{8,24},{16,0},{24,8},{1,17},{9,25},{17,1},{25,9},{2,18},{10... | collective-permute-start | bytes 638984 | tf_op jit(solution)/shard_map/ppermute | solution.py:49
  51.1 3.7 %shard_map.215.attended = bf16[256,256]{1,0:T(8,128)(2,1)S(1)} custom-call(s32[3]{0:T(128)S(1)} %pad_add_fusion.place, s32[1]{0:T(128)} %copy.26.length, bf16[256,256]{1,0:T(8,128)(2,1)S(1)} %get-tuple-element.32.query, bf16[512,128]{1,0:T(8,128)(2,1)S(1)} %get-tuple-element.33.refs_0_, bf16[512,128]{1,0:T(8,128)(2,1)S(1)} %collective-permute-done.11.refs_1_, ...), custom_call_target="tpu_custom_call" | custom-call | flops 6000000000 | tf_op jit(solution)/shard_map/pallas_call | solution.py:484
  54.7 2.4 %collective-permute-done.19.far = bf16[416,256]{1,0:T(8,128)(2,1)S(1)} collective-permute-done((bf16[416,256]{1,0:T(8,128)(2,1)S(1)}, bf16[416,256]{1,0:T(8,128)(2,1)S(1)}, u32[]{:S(2)}, u32[]{:S(2)}) %collective-permute-start.19) | collective-permute-done | bytes 213024 | tf_op jit(solution)/shard_map/ppermute | solution.py:49
  57.1 2.5 %shard_map.218 = (f32[1,1,3,128,256]{4,3,2,1,0:T(8,128)}, bf16[256,384]{1,0:T(8,128)(2,1)S(1)}, bf16[128,768]{1,0:T(8,128)(2,1)S(1)}, bf16[128,768]{1,0:T(8,128)(2,1)S(1)}) custom-call(s32[3]{0:T(128)S(1)} %pad_add_fusion.1.place, bf16[416,256]{1,0:T(8,128)(2,1)S(1)} %collective-permute-done.18.second.near, ...), custom_call_target="tpu_custom_call" | custom-call | flops 3000000000 | tf_op jit(solution)/shard_map/pallas_call | solution.py:513
  60.1 1.7 %shard_map.219 = (bf16[128,768]{1,0:T(8,128)(2,1)S(1)}, bf16[128,768]{1,0:T(8,128)(2,1)S(1)}, f32[256,768]{1,0:T(8,128)S(1)}, f32[128,768]{1,0:T(8,128)S(1)}, f32[128,768]{1,0:T(8,128)S(1)}) custom-call(s32[3]{0:T(128)S(1)} %pad_add_fusion.place, bf16[256,256]{1,0:T(8,128)(2,1)S(1)} %shard_map.215.attended, bf16[256,384]{1,0:T(8,128)(2,1)S(1)} %get-tuple-element.39.mixed, ...), custom_call_target="tpu_custom_call" | custom-call | flops 2000000000 | tf_op jit(solution)/shard_map/pallas_call | solution.py:531
  61.8 1.6 %collective-permute-start.23 = (bf16[128,768]{1,0:T(8,128)(2,1)S(1)}, bf16[128,768]{1,0:T(8,128)(2,1)S(1)}, u32[]{:S(2)}, u32[]{:S(2)}) collective-permute-start(bf16[128,768]{1,0:T(8,128)(2,1)S(1)} %get-tuple-element.44), channel_id=1, source_target_pairs={{0,4},{2,6},{4,0},{6,2},{1,5},{3,7},{5,1},{7,3},{8,12},{10,14},{12... | collective-permute-start | bytes 589832 | tf_op jit(solution)/shard_map/ppermute | solution.py:45
  66.4 2.7 %collective-permute-done.21 = bf16[128,768]{1,0:T(8,128)(2,1)S(1)} collective-permute-done((bf16[128,768]{1,0:T(8,128)(2,1)S(1)}, bf16[128,768]{1,0:T(8,128)(2,1)S(1)}, u32[]{:S(2)}, u32[]{:S(2)}) %collective-permute-start.21) | collective-permute-done | bytes 196640 | tf_op jit(solution)/shard_map/ppermute | solution.py:45
  69.7 3.6 %collective-permute-done.25 = bf16[128,768]{1,0:T(8,128)(2,1)S(1)} collective-permute-done((bf16[128,768]{1,0:T(8,128)(2,1)S(1)}, bf16[128,768]{1,0:T(8,128)(2,1)S(1)}, u32[]{:S(2)}, u32[]{:S(2)}) %collective-permute-start.25) | collective-permute-done | bytes 196640 | tf_op jit(solution)/shard_map/ppermute | solution.py:45
  73.3 1.5 %collective-permute-done.22 = bf16[128,768]{1,0:T(8,128)(2,1)S(1)} collective-permute-done((bf16[128,768]{1,0:T(8,128)(2,1)S(1)}, bf16[128,768]{1,0:T(8,128)(2,1)S(1)}, u32[]{:S(2)}, u32[]{:S(2)}) %collective-permute-start.22) | collective-permute-done | bytes 196640 | tf_op jit(solution)/shard_map/ppermute | solution.py:45
  (89 shorter events, 17.6 us)
Async XLA Ops:
  0.6 12.3 %collective-permute-start = (bf16[256,768]{1,0:T(8,128)(2,1)}, bf16[256,768]{1,0:T(8,128)(2,1)S(1)}, u32[]{:S(2)}, u32[]{:S(2)}) collective-permute-start(bf16[256,768]{1,0:T(8,128)(2,1)} %bitcast.22), channel_id=1, source_target_pairs={{0,2},{2,0},{4,6},{6,4},{1,3},{3,1},{5,7},{7,5},{8,10},{10,8},{12,... | collective-permute-start | bytes 1179656 | tf_op jit(solution)/shard_map/ppermute | solution.py:45
  3.6 11.2 %collective-permute-start.1 = (bf16[256,768]{1,0:T(8,128)(2,1)}, bf16[256,768]{1,0:T(8,128)(2,1)S(1)}, u32[]{:S(2)}, u32[]{:S(2)}) collective-permute-start(bf16[256,768]{1,0:T(8,128)(2,1)} %bitcast.23), channel_id=1, source_target_pairs={{0,4},{2,6},{4,0},{6,2},{1,5},{3,7},{5,1},{7,3},{8,12},{10,14},{12... | collective-permute-start | bytes 1179656 | tf_op jit(solution)/shard_map/ppermute | solution.py:45
  5.9 10.5 %collective-permute-start.4 = (bf16[16,768]{1,0:T(8,128)(2,1)S(1)}, bf16[16,768]{1,0:T(8,128)(2,1)S(1)}, u32[]{:S(2)}, u32[]{:S(2)}) collective-permute-start(bf16[16,768]{1,0:T(8,128)(2,1)S(1)} %slice_bitcast_fusion), channel_id=1, source_target_pairs={{0,8},{8,16},{16,24},{24,0},{1,9},{9,17},{17,25},{25,1},{2,10},{10... | collective-permute-start | bytes 73736 | tf_op jit(solution)/shard_map/ppermute | solution.py:54
  13.0 11.0 %collective-permute-start.2 = (bf16[128,768]{1,0:T(8,128)(2,1)S(1)}, bf16[128,768]{1,0:T(8,128)(2,1)S(1)}, u32[]{:S(2)}, u32[]{:S(2)}) collective-permute-start(bf16[128,768]{1,0:T(8,128)(2,1)S(1)} %slice.16), channel_id=1, source_target_pairs={{0,4},{2,6},{4,0},{6,2},{1,5},{3,7},{5,1},{7,3},{8,12},{10,14},{12... | collective-permute-start | bytes 589832 | tf_op jit(solution)/shard_map/ppermute | solution.py:45
  14.8 9.1 %collective-permute-start.3 = (bf16[128,768]{1,0:T(8,128)(2,1)S(1)}, bf16[128,768]{1,0:T(8,128)(2,1)S(1)}, u32[]{:S(2)}, u32[]{:S(2)}) collective-permute-start(bf16[128,768]{1,0:T(8,128)(2,1)S(1)} %slice.17), channel_id=1, source_target_pairs={{0,2},{2,0},{4,6},{6,4},{1,3},{3,1},{5,7},{7,5},{8,10},{10,8},{12,... | collective-permute-start | bytes 589832 | tf_op jit(solution)/shard_map/ppermute | solution.py:45
  16.5 7.4 %collective-permute-start.5 = (bf16[16,768]{1,0:T(8,128)(2,1)S(1)}, bf16[16,768]{1,0:T(8,128)(2,1)S(1)}, u32[]{:S(2)}, u32[]{:S(2)}) collective-permute-start(bf16[16,768]{1,0:T(8,128)(2,1)S(1)} %collective-permute-done.4.rim0), channel_id=1, source_target_pairs={{0,2},{2,0},{4,6},{6,4},{1,3},{3,1},{5,7},{7,5},{8,10},{10,8},{12,... | collective-permute-start | bytes 73736 | tf_op jit(solution)/shard_map/ppermute | solution.py:45
  17.0 6.9 %collective-permute-start.6 = (bf16[16,768]{1,0:T(8,128)(2,1)S(1)}, bf16[16,768]{1,0:T(8,128)(2,1)S(1)}, u32[]{:S(2)}, u32[]{:S(2)}) collective-permute-start(bf16[16,768]{1,0:T(8,128)(2,1)S(1)} %collective-permute-done.4.rim0), channel_id=1, source_target_pairs={{0,4},{2,6},{4,0},{6,2},{1,5},{3,7},{5,1},{7,3},{8,12},{10,14},{12... | collective-permute-start | bytes 73736 | tf_op jit(solution)/shard_map/ppermute | solution.py:45
  18.2 5.8 %collective-permute-start.7 = (bf16[16,768]{1,0:T(8,128)(2,1)S(1)}, bf16[16,768]{1,0:T(8,128)(2,1)S(1)}, u32[]{:S(2)}, u32[]{:S(2)}) collective-permute-start(bf16[16,768]{1,0:T(8,128)(2,1)S(1)} %collective-permute-done.4.rim0), channel_id=1, source_target_pairs={{0,6},{2,4},{4,2},{6,0},{1,7},{3,5},{5,3},{7,1},{8,14},{10,12},{12... | collective-permute-start | bytes 73736 | tf_op jit(solution)/shard_map/ppermute | solution.py:45
  27.1 10.0 %collective-permute-start.8 = (bf16[272,128]{1,0:T(8,128)(2,1)S(1)}, bf16[272,128]{1,0:T(8,128)(2,1)S(1)}, u32[]{:S(2)}, u32[]{:S(2)}) collective-permute-start(bf16[272,128]{1,0:T(8,128)(2,1)S(1)} %get-tuple-element.28.bc0), channel_id=1, source_target_pairs={{0,2},{2,0},{4,6},{6,4},{1,3},{3,1},{5,7},{7,5},{8,10},{10,8},{12,... | collective-permute-start | bytes 208904 | tf_op jit(solution)/shard_map/ppermute | solution.py:45
  27.6 9.8 %collective-permute-start.9 = (bf16[272,128]{1,0:T(8,128)(2,1)S(1)}, bf16[272,128]{1,0:T(8,128)(2,1)S(1)}, u32[]{:S(2)}, u32[]{:S(2)}) collective-permute-start(bf16[272,128]{1,0:T(8,128)(2,1)S(1)} %get-tuple-element.28.bc0), channel_id=1, source_target_pairs={{0,4},{2,6},{4,0},{6,2},{1,5},{3,7},{5,1},{7,3},{8,12},{10,14},{12... | collective-permute-start | bytes 208904 | tf_op jit(solution)/shard_map/ppermute | solution.py:45
  28.7 9.2 %collective-permute-start.10 = (bf16[272,128]{1,0:T(8,128)(2,1)S(1)}, bf16[272,128]{1,0:T(8,128)(2,1)S(1)}, u32[]{:S(2)}, u32[]{:S(2)}) collective-permute-start(bf16[272,128]{1,0:T(8,128)(2,1)S(1)} %get-tuple-element.28.bc0), channel_id=1, source_target_pairs={{0,6},{2,4},{4,2},{6,0},{1,7},{3,5},{5,3},{7,1},{8,14},{10,12},{12... | collective-permute-start | bytes 208904 | tf_op jit(solution)/shard_map/ppermute | solution.py:45
  30.6 11.5 %collective-permute-start.11 = (bf16[512,128]{1,0:T(8,128)(2,1)S(1)}, bf16[512,128]{1,0:T(8,128)(2,1)S(1)}, u32[]{:S(2)}, u32[]{:S(2)}) collective-permute-start(bf16[512,128]{1,0:T(8,128)(2,1)S(1)} %get-tuple-element.33.refs_0_), channel_id=1, source_target_pairs={{0,8},{8,0},{16,24},{24,16},{1,9},{9,1},{17,25},{25,17},{2,10},{10... | collective-permute-start | bytes 393224 | tf_op jit(solution)/shard_map/ppermute | solution.py:49
  32.1 11.5 %collective-permute-start.12 = (bf16[512,128]{1,0:T(8,128)(2,1)S(1)}, bf16[512,128]{1,0:T(8,128)(2,1)S(1)}, u32[]{:S(2)}, u32[]{:S(2)}) collective-permute-start(bf16[512,128]{1,0:T(8,128)(2,1)S(1)} %get-tuple-element.33.refs_0_), channel_id=1, source_target_pairs={{0,16},{8,24},{16,0},{24,8},{1,17},{9,25},{17,1},{25,9},{2,18},{10... | collective-permute-start | bytes 393224 | tf_op jit(solution)/shard_map/ppermute | solution.py:49
  37.1 7.2 %collective-permute-start.13 = (bf16[512,128]{1,0:T(8,128)(2,1)S(1)}, bf16[512,128]{1,0:T(8,128)(2,1)S(1)}, u32[]{:S(2)}, u32[]{:S(2)}) collective-permute-start(bf16[512,128]{1,0:T(8,128)(2,1)S(1)} %get-tuple-element.33.refs_0_), channel_id=1, source_target_pairs={{0,24},{8,16},{16,8},{24,0},{1,25},{9,17},{17,9},{25,1},{2,26},{10... | collective-permute-start | bytes 393224 | tf_op jit(solution)/shard_map/ppermute | solution.py:49
  37.4 13.6 %collective-permute-start.14 = (bf16[512,128]{1,0:T(8,128)(2,1)S(1)}, bf16[512,128]{1,0:T(8,128)(2,1)S(1)}, u32[]{:S(2)}, u32[]{:S(2)}) collective-permute-start(bf16[512,128]{1,0:T(8,128)(2,1)S(1)} %get-tuple-element.33.refs_0_), channel_id=1, source_target_pairs={{0,2},{2,0},{4,6},{6,4},{1,3},{3,1},{5,7},{7,5},{8,10},{10,8},{12,... | collective-permute-start | bytes 393224 | tf_op jit(solution)/shard_map/ppermute | solution.py:45
  39.9 6.9 %collective-permute-start.18 = (bf16[416,256]{1,0:T(8,128)(2,1)S(1)}, bf16[416,256]{1,0:T(8,128)(2,1)S(1)}, u32[]{:S(2)}, u32[]{:S(2)}) collective-permute-start(bf16[416,256]{1,0:T(8,128)(2,1)S(1)} %get-tuple-element.34.first), channel_id=1, source_target_pairs={{0,8},{8,0},{16,24},{24,16},{1,9},{9,1},{17,25},{25,17},{2,10},{10... | collective-permute-start | bytes 638984 | tf_op jit(solution)/shard_map/ppermute | solution.py:49
  42.1 8.9 %collective-permute-start.15 = (bf16[512,128]{1,0:T(8,128)(2,1)S(1)}, bf16[512,128]{1,0:T(8,128)(2,1)S(1)}, u32[]{:S(2)}, u32[]{:S(2)}) collective-permute-start(bf16[512,128]{1,0:T(8,128)(2,1)S(1)} %collective-permute-done.11.refs_1_), channel_id=1, source_target_pairs={{0,2},{2,0},{4,6},{6,4},{1,3},{3,1},{5,7},{7,5},{8,10},{10,8},{12,... | collective-permute-start | bytes 393224 | tf_op jit(solution)/shard_map/ppermute | solution.py:45
  43.7 7.3 %collective-permute-start.16 = (bf16[512,128]{1,0:T(8,128)(2,1)S(1)}, bf16[512,128]{1,0:T(8,128)(2,1)S(1)}, u32[]{:S(2)}, u32[]{:S(2)}) collective-permute-start(bf16[512,128]{1,0:T(8,128)(2,1)S(1)} %collective-permute-done.12.refs_2_), channel_id=1, source_target_pairs={{0,2},{2,0},{4,6},{6,4},{1,3},{3,1},{5,7},{7,5},{8,10},{10,8},{12,... | collective-permute-start | bytes 393224 | tf_op jit(solution)/shard_map/ppermute | solution.py:45
  44.3 6.7 %collective-permute-start.17 = (bf16[512,128]{1,0:T(8,128)(2,1)S(1)}, bf16[512,128]{1,0:T(8,128)(2,1)S(1)}, u32[]{:S(2)}, u32[]{:S(2)}) collective-permute-start(bf16[512,128]{1,0:T(8,128)(2,1)S(1)} %collective-permute-done.13.refs_3_), channel_id=1, source_target_pairs={{0,2},{2,0},{4,6},{6,4},{1,3},{3,1},{5,7},{7,5},{8,10},{10,8},{12,... | collective-permute-start | bytes 393224 | tf_op jit(solution)/shard_map/ppermute | solution.py:45
  47.4 9.7 %collective-permute-start.19 = (bf16[416,256]{1,0:T(8,128)(2,1)S(1)}, bf16[416,256]{1,0:T(8,128)(2,1)S(1)}, u32[]{:S(2)}, u32[]{:S(2)}) collective-permute-start(bf16[416,256]{1,0:T(8,128)(2,1)S(1)} %shard_map.216), channel_id=1, source_target_pairs={{0,16},{8,24},{16,0},{24,8},{1,17},{9,25},{17,1},{25,9},{2,18},{10... | collective-permute-start | bytes 638984 | tf_op jit(solution)/shard_map/ppermute | solution.py:49
  59.6 6.6 %collective-permute-start.24 = (bf16[128,768]{1,0:T(8,128)(2,1)S(1)}, bf16[128,768]{1,0:T(8,128)(2,1)S(1)}, u32[]{:S(2)}, u32[]{:S(2)}) collective-permute-start(bf16[128,768]{1,0:T(8,128)(2,1)S(1)} %get-tuple-element.46), channel_id=1, source_target_pairs={{0,4},{2,6},{4,0},{6,2},{1,5},{3,7},{5,1},{7,3},{8,12},{10,14},{12... | collective-permute-start | bytes 589832 | tf_op jit(solution)/shard_map/ppermute | solution.py:45
  61.8 7.9 %collective-permute-start.23 = (bf16[128,768]{1,0:T(8,128)(2,1)S(1)}, bf16[128,768]{1,0:T(8,128)(2,1)S(1)}, u32[]{:S(2)}, u32[]{:S(2)}) collective-permute-start(bf16[128,768]{1,0:T(8,128)(2,1)S(1)} %get-tuple-element.44), channel_id=1, source_target_pairs={{0,4},{2,6},{4,0},{6,2},{1,5},{3,7},{5,1},{7,3},{8,12},{10,14},{12... | collective-permute-start | bytes 589832 | tf_op jit(solution)/shard_map/ppermute | solution.py:45
  63.9 9.4 %collective-permute-start.20 = (bf16[128,768]{1,0:T(8,128)(2,1)S(1)}, bf16[128,768]{1,0:T(8,128)(2,1)S(1)}, u32[]{:S(2)}, u32[]{:S(2)}) collective-permute-start(bf16[128,768]{1,0:T(8,128)(2,1)S(1)} %get-tuple-element.41), channel_id=1, source_target_pairs={{0,2},{2,0},{4,6},{6,4},{1,3},{3,1},{5,7},{7,5},{8,10},{10,8},{12,... | collective-permute-start | bytes 589832 | tf_op jit(solution)/shard_map/ppermute | solution.py:45
  66.3 7.0 %collective-permute-start.25 = (bf16[128,768]{1,0:T(8,128)(2,1)S(1)}, bf16[128,768]{1,0:T(8,128)(2,1)S(1)}, u32[]{:S(2)}, u32[]{:S(2)}) collective-permute-start(bf16[128,768]{1,0:T(8,128)(2,1)S(1)} %add_convert_fusion), channel_id=1, source_target_pairs={{0,2},{2,0},{4,6},{6,4},{1,3},{3,1},{5,7},{7,5},{8,10},{10,8},{12,... | collective-permute-start | bytes 589832 | tf_op jit(solution)/shard_map/ppermute | solution.py:45
  (19 other events, 98.2 us)

commit v4 on v3

--- a/solution.py
+++ b/solution.py
@@ -74,8 +74,17 @@
     return v * cos + pltpu.roll(v, HD // 2, 1) * sin
 
 
+def pack_kernel(from_x, from_y, rim, *refs):
+    to_y, to_x = refs[-2:]
+    half = to_y.shape[0] - RIM
+    to_y[:half, :] = from_x[:half]
+    to_y[half:, :] = rim[...]
+    to_x[:half, :] = from_y[half:]
+    to_x[half:, :] = rim[...]
+
+
 def norm_kernel(
-    place, own, from_x, from_y, diag_top, diag_low, rim0, rim1, rim2, rim3, gain, w_bc, w_kv, cos, sin,
+    place, own, from_x, from_y, by_y, by_x, rim, diag_rim, gain, w_bc, w_kv, cos, sin,
     cache, later, normed, bc, kv, packed,
 ):
     me = place[0]
@@ -95,9 +104,9 @@
             scaled = block.astype(f32) * inverse * gain[:, columns(turn)]
             normed[pl.ds(start, count), columns(turn)] = scaled.astype(bf16)
 
-    rows(0, RIM, [rim0[...], rim1[...], rim2[...], rim3[...]])
-    rows(RIM, half, [own[:half], from_x[:half], from_y[:half], diag_top[...]])
-    rows(RIM + half, half, [own[half:], from_x[half:], from_y[half:], diag_low[...]])
+    rows(0, RIM, [rim[...], by_x[half:], by_y[half:], diag_rim[...]])
+    rows(RIM, half, [own[:half], from_x[:half], from_y[:half], by_y[:half]])
+    rows(RIM + half, half, [own[half:], from_x[half:], from_y[half:], by_x[:half]])
     bc[...] = dot(normed[...], w_bc[...]).astype(bf16)
     projected = dot(normed[RIM:, :], w_kv[...])
     turned = rope(projected, cos[...], sin[...])
@@ -265,14 +274,17 @@
     far_y[...] = term(3, half, half).astype(bf16)
 
 
-def rest_kernel(
-    place, attended, mixed, w_attn, w_mamba, own, to_x, to_y, keep, keep_top, keep_low
-):
+def near_kernel(place, attended, mixed, w_attn, w_mamba, to_x, to_y):
+    half, width = to_x.shape
+    term = term_of(place[0], attended, mixed, w_attn, w_mamba, width)
+    to_x[...] = term(1, 0, half).astype(bf16)
+    to_y[...] = term(2, half, half).astype(bf16)
+
+
+def keep_kernel(place, attended, mixed, w_attn, w_mamba, own, sent, keep, keep_top, keep_low):
     tokens, width = own.shape
     half = tokens // 2
     term = term_of(place[0], attended, mixed, w_attn, w_mamba, width)
-    to_x[...] = term(1, 0, half).astype(bf16)
-    to_y[...] = term(2, half, half).astype(bf16)
     keep_top[...] = term(2, 0, half)
     keep_low[...] = term(1, half, half)
     keep[...] = term(0, 0, tokens) + own[...].astype(f32)
@@ -377,10 +389,6 @@
     from_x = swap(own_rows, 1)
     from_y = swap(own_rows, 2)
     rim = ahead(own_rows[tokens - RIM :])
-    diag_top = swap(from_x[:half], 2)
-    diag_low = swap(from_y[half:], 1)
-    rims = [rim] + [swap(rim, turn) for turn in (1, 2, 3)]
-
     positions = length + seq_pos * tokens + jnp.arange(tokens, dtype=jnp.int32)
     freqs = rope_base ** (-jnp.arange(HD // 2, dtype=f32) * 2.0 / HD)
     angles = positions.astype(f32)[:, None] * jnp.concatenate([freqs, freqs])[None, :]
@@ -388,6 +396,13 @@
     sin = jnp.where(jnp.arange(HD)[None, :] < HD // 2, -jnp.sin(angles), jnp.sin(angles))
     gain = norm_gain.astype(f32)[None, :]
     mixer_gain = mamba_gain.astype(f32)[None, :]
+
+    to_y, to_x = call(
+        pack_kernel, (shape(half + RIM, width), shape(half + RIM, width)), 0, 3, 3
+    )(from_x, from_y, rim)
+    by_y = swap(to_y, 2)
+    by_x = swap(to_x, 1)
+    diag_rim = swap(rim, 3)
 
     cache_rows = cache.shape[1]
     normed, bc_block, kv_block, packed = call(
@@ -399,11 +414,11 @@
             shape(cache_rows + tokens, w_keyval.shape[1]),
         ),
         1,
-        15,
+        13,
         3,
         left=1,
     )(
-        place, own_rows, from_x, from_y, diag_top, diag_low, *rims, gain, w_bc, w_keyval, cos, sin,
+        place, own_rows, from_x, from_y, by_y, by_x, rim, diag_rim, gain, w_bc, w_keyval, cos, sin,
         cache[0], w_pair,
     )
 
@@ -528,19 +543,21 @@
 
     far_x_in = swap(far_x, 1)
     far_y_in = swap(far_y, 2)
-    to_x, to_y, keep, keep_top, keep_low = call(
-        rest_kernel,
+    to_x, to_y = call(
+        near_kernel, (shape(half, width), shape(half, width)), 1, 4, 1
+    )(place, attended, mixed, w_attn_out, w_mamba_out)
+    keep, keep_top, keep_low = call(
+        keep_kernel,
         (
-            shape(half, width),
-            shape(half, width),
             shape(tokens, width, dtype=f32),
             shape(half, width, dtype=f32),
             shape(half, width, dtype=f32),
         ),
         1,
         5,
-        2,
-    )(place, attended, mixed, w_attn_out, w_mamba_out, own_rows)
+        1,
+        left=1,
+    )(place, attended, mixed, w_attn_out, w_mamba_out, own_rows, to_x)
     top_in = swap(to_x, 1)
     low_in = swap(to_y, 2)
     top_last = swap((keep_top + far_x_in.astype(f32)).astype(bf16), 2)

time: 75.9 us -> 73.5 us (0.968)
  starting transfers between devices: 34 us -> 32.2 us
  Pallas kernels: 18.3 us -> 19.1 us
    ppermute x20 -> x18, waiting for transfers between devices: 12.8 us -> 9.61 us  [swap(): lax.ppermute(block, 'mp', [(i, i ^ turn) for i in range(lax.axis_size('mp...]
    ppermute x1, waiting for transfers between devices: 0.01 us -> 2.68 us  [ahead(): lax.ppermute(block, 'seq', [(i, (i + 1) % count) for i in range(count)])]
    ppermute x20 -> x18, starting transfers between devices: 23.7 us -> 21.9 us  [swap(): lax.ppermute(block, 'mp', [(i, i ^ turn) for i in range(lax.axis_size('mp...]
    pallas_call x1 -> x3, Pallas kernels: 1.65 us -> 2.39 us  [the longest x1 1.33 us: shards(): call(keep_kernel, (shape(tokens, width, dtype=f32), shape(half, width, dt...]
    unnamed x35 -> x37, local copies, waits for them, and re-layouts: 3.18 us -> 3.19 us
  transfers between devices with their start and end apart: 26 -> 24, of which waited for: 7 -> 9; matrix products, arithmetic and copies ran while one was open for 7% -> 7% of each run, Pallas kernels for 17% -> 18%
where the time goes in v4:
time: 73.5 us; the launch traced here: 73.3 us
  starting transfers between devices  32.2 us (44%)
  Pallas kernels  19.1 us (26%)
  waiting for transfers between devices  14.6 us (20%)
  local copies, waits for them, and re-layouts  3.97 us (5%)
  other arithmetic  1.79 us (2%)
  between operations  1.66 us (2%)
    ppermute x18, starting transfers between devices, swap(): lax.ppermute(block, 'mp', [(i, i ^ turn) for i in range(lax.axis_size('mp...  21.9 us
    ppermute x18, waiting for transfers between devices, swap(): lax.ppermute(block, 'mp', [(i, i ^ turn) for i in range(lax.axis_size('mp...  9.61 us
    ppermute x5, starting transfers between devices, cross(): lax.ppermute(block, 'seq', [(i, i ^ turn) for i in range(lax.axis_size('s...  8.66 us
    pallas_call x1, Pallas kernels, shards(): call(functools.partial(attention_kernel, cache_rows=cache_rows, scale=HD...  3.72 us
    unnamed x37, local copies, waits for them, and re-layouts  3.19 us
    pallas_call x1, Pallas kernels, shards(): call(norm_kernel, (shape(RIM + tokens, 4 * width), shape(RIM + tokens, w_...  3.04 us
    ppermute x1, waiting for transfers between devices, ahead(): lax.ppermute(block, 'seq', [(i, (i + 1) % count) for i in range(count)])  2.68 us
    pallas_call x1, Pallas kernels, shards(): call(finish_kernel, (shape(1, 1, heads, HD, NS, dtype=f32), shape(tokens,...  2.48 us
  transfers between devices with their start and end apart: 24, of which 9 were waited for; matrix products, arithmetic and copies ran while one was open for 7% of the time, Pallas kernels for 18%

profile of v4, /device:TPU:0, one launch (start us, length us, event | category | flops | bytes accessed | tf_op | source)
XLA Modules:
  0.0 73.3 jit_solution(11950552084415620707)
XLA Ops:
  0.6 3.0 %collective-permute-start = (bf16[256,768]{1,0:T(8,128)(2,1)}, bf16[256,768]{1,0:T(8,128)(2,1)S(1)}, u32[]{:S(2)}, u32[]{:S(2)}) collective-permute-start(bf16[256,768]{1,0:T(8,128)(2,1)} %bitcast.21), channel_id=1, source_target_pairs={{0,2},{2,0},{4,6},{6,4},{1,3},{3,1},{5,7},{7,5},{8,10},{10,8},{12,... | collective-permute-start | bytes 1179656 | tf_op jit(solution)/shard_map/ppermute | solution.py:45
  3.6 1.5 %collective-permute-start.1 = (bf16[256,768]{1,0:T(8,128)(2,1)}, bf16[256,768]{1,0:T(8,128)(2,1)S(1)}, u32[]{:S(2)}, u32[]{:S(2)}) collective-permute-start(bf16[256,768]{1,0:T(8,128)(2,1)} %bitcast.22), channel_id=1, source_target_pairs={{0,4},{2,6},{4,0},{6,2},{1,5},{3,7},{5,1},{7,3},{8,12},{10,14},{12... | collective-permute-start | bytes 1179656 | tf_op jit(solution)/shard_map/ppermute | solution.py:45
  5.9 1.6 %collective-permute-start.2 = (bf16[16,768]{1,0:T(8,128)(2,1)S(1)}, bf16[16,768]{1,0:T(8,128)(2,1)S(1)}, u32[]{:S(2)}, u32[]{:S(2)}) collective-permute-start(bf16[16,768]{1,0:T(8,128)(2,1)S(1)} %slice_bitcast_fusion), channel_id=1, source_target_pairs={{0,8},{8,16},{16,24},{24,0},{1,9},{9,17},{17,25},{25,1},{2,10},{10... | collective-permute-start | bytes 73736 | tf_op jit(solution)/shard_map/ppermute | solution.py:54
  8.9 2.7 %collective-permute-done.2.rim = bf16[16,768]{1,0:T(8,128)(2,1)S(1)} collective-permute-done((bf16[16,768]{1,0:T(8,128)(2,1)S(1)}, bf16[16,768]{1,0:T(8,128)(2,1)S(1)}, u32[]{:S(2)}, u32[]{:S(2)}) %collective-permute-start.2) | collective-permute-done | bytes 24608 | tf_op jit(solution)/shard_map/ppermute | solution.py:54
  11.6 1.4 %collective-permute-done.from_x = bf16[256,768]{1,0:T(8,128)(2,1)S(1)} collective-permute-done((bf16[256,768]{1,0:T(8,128)(2,1)}, bf16[256,768]{1,0:T(8,128)(2,1)S(1)}, u32[]{:S(2)}, u32[]{:S(2)}) %collective-permute-start) | collective-permute-done | bytes 393248 | tf_op jit(solution)/shard_map/ppermute | solution.py:45
  13.0 1.5 %collective-permute-done.1.from_y = bf16[256,768]{1,0:T(8,128)(2,1)S(1)} collective-permute-done((bf16[256,768]{1,0:T(8,128)(2,1)}, bf16[256,768]{1,0:T(8,128)(2,1)S(1)}, u32[]{:S(2)}, u32[]{:S(2)}) %collective-permute-start.1) | collective-permute-done | bytes 393248 | tf_op jit(solution)/shard_map/ppermute | solution.py:45
  14.5 1.6 %collective-permute-start.3 = (bf16[144,768]{1,0:T(8,128)(2,1)S(1)}, bf16[144,768]{1,0:T(8,128)(2,1)S(1)}, u32[]{:S(2)}, u32[]{:S(2)}) collective-permute-start(bf16[144,768]{1,0:T(8,128)(2,1)S(1)} %get-tuple-element.28), channel_id=1, source_target_pairs={{0,4},{2,6},{4,0},{6,2},{1,5},{3,7},{5,1},{7,3},{8,12},{10,14},{12... | collective-permute-start | bytes 663560 | tf_op jit(solution)/shard_map/ppermute | solution.py:45
  16.6 1.4 %collective-permute-start.5 = (bf16[16,768]{1,0:T(8,128)(2,1)S(1)}, bf16[16,768]{1,0:T(8,128)(2,1)S(1)}, u32[]{:S(2)}, u32[]{:S(2)}) collective-permute-start(bf16[16,768]{1,0:T(8,128)(2,1)S(1)} %collective-permute-done.2.rim), channel_id=1, source_target_pairs={{0,6},{2,4},{4,2},{6,0},{1,7},{3,5},{5,3},{7,1},{8,14},{10,12},{12... | collective-permute-start | bytes 73736 | tf_op jit(solution)/shard_map/ppermute | solution.py:45
  18.2 3.1 %copy.25 = bf16[3072,2,384]{2,0,1:T(8,128)(2,1)S(1)} copy(bf16[3072,2,384]{2,1,0:T(2,128)(2,1)} %param.25) | data formatting | bytes 9437184 | tf_op args[5]
  22.3 3.0 %shard_map.212 = (bf16[272,3072]{1,0:T(8,128)(2,1)S(1)}, bf16[272,128]{1,0:T(8,128)(2,1)S(1)}, bf16[256,128]{1,0:T(8,128)(2,1)}, bf16[512,128]{1,0:T(8,128)(2,1)S(1)}) custom-call(s32[3]{0:T(128)S(1)} %pad_add_fusion.place, bf16[256,768]{1,0:T(8,128)(2,1)S(1)} %bitcast.23, bf16[256,768]{1,0:T(8,128)(2,1)S(1)} %collective-permute-done.from_x, ...), custom_call_target="tpu_custom_call" | custom-call | flops 3000000000 | tf_op jit(solution)/shard_map/pallas_call | solution.py:408
  26.0 1.4 %collective-permute-start.7 = (bf16[272,128]{1,0:T(8,128)(2,1)S(1)}, bf16[272,128]{1,0:T(8,128)(2,1)S(1)}, u32[]{:S(2)}, u32[]{:S(2)}) collective-permute-start(bf16[272,128]{1,0:T(8,128)(2,1)S(1)} %get-tuple-element.32.bc0), channel_id=1, source_target_pairs={{0,4},{2,6},{4,0},{6,2},{1,5},{3,7},{5,1},{7,3},{8,12},{10,14},{12... | collective-permute-start | bytes 208904 | tf_op jit(solution)/shard_map/ppermute | solution.py:45
  28.8 1.6 %collective-permute-start.9 = (bf16[512,128]{1,0:T(8,128)(2,1)S(1)}, bf16[512,128]{1,0:T(8,128)(2,1)S(1)}, u32[]{:S(2)}, u32[]{:S(2)}) collective-permute-start(bf16[512,128]{1,0:T(8,128)(2,1)S(1)} %get-tuple-element.37.refs_0_), channel_id=1, source_target_pairs={{0,8},{8,0},{16,24},{24,16},{1,9},{9,1},{17,25},{25,17},{2,10},{10... | collective-permute-start | bytes 393224 | tf_op jit(solution)/shard_map/ppermute | solution.py:49
  30.4 2.6 %collective-permute-start.10 = (bf16[512,128]{1,0:T(8,128)(2,1)S(1)}, bf16[512,128]{1,0:T(8,128)(2,1)S(1)}, u32[]{:S(2)}, u32[]{:S(2)}) collective-permute-start(bf16[512,128]{1,0:T(8,128)(2,1)S(1)} %get-tuple-element.37.refs_0_), channel_id=1, source_target_pairs={{0,16},{8,24},{16,0},{24,8},{1,17},{9,25},{17,1},{25,9},{2,18},{10... | collective-permute-start | bytes 393224 | tf_op jit(solution)/shard_map/ppermute | solution.py:49
  33.0 2.3 %shard_map.213 = (bf16[272,384]{1,0:T(8,128)(2,1)S(1)}, f32[8,256]{1,0:T(8,128)S(1)}, f32[8,256]{1,0:T(8,128)S(1)}) custom-call(f32[3]{0:T(128)S(1)} %copy-done.13, f32[3]{0:T(128)S(1)} %copy-done.14, bf16[272,3072]{1,0:T(8,128)(2,1)S(1)} %get-tuple-element.30.normed, bf16[2,3072,384]{2,1,0:T(8,128)(2,1)S(1)} %bitcast.19, bf16[3,3072]{1,0:T(4,128)(2,1)S(1)} %bitcast.27), custom_call_target="tpu_custom_call" | custom-call | flops 2000000000 | tf_op jit(solution)/shard_map/pallas_call | solution.py:427
  36.4 1.9 %shard_map.214 = (f32[384,256]{1,0:T(8,128)S(1)}, bf16[416,256]{1,0:T(8,128)(2,1)S(1)}, bf16[256,384]{1,0:T(8,128)(2,1)S(1)}, bf16[256,256]{1,0:T(8,128)(2,1)S(1)}, bf16[256,256]{1,0:T(8,128)(2,1)S(1)}) custom-call(s32[3]{0:T(128)S(1)} %pad_add_fusion.place, bf16[272,384]{1,0:T(8,128)(2,1)S(1)} %get-tuple-element.31.x_in, ...), custom_call_target="tpu_custom_call" | custom-call | flops 2000000000 | tf_op jit(solution)/shard_map/pallas_call | solution.py:445
  39.0 1.5 %shard_map.215 = (bf16[256,256]{1,0:T(8,128)(2,1)S(1)}, bf16[256,384]{1,0:T(8,128)(2,1)S(1)}) custom-call(bf16[272,3072]{1,0:T(8,128)(2,1)S(1)} %get-tuple-element.30.normed, bf16[3072,256]{1,0:T(8,128)(2,1)S(1)} %copy-done.2, bf16[2,3072,384]{2,1,0:T(8,128)(2,1)S(1)} %bitcast.20, f32[256,128]{1,0:T(8,128)S(1)} %get-tuple-element.54.cos, ...), custom_call_target="tpu_custom_call" | custom-call | flops 2000000000 | tf_op jit(solution)/shard_map/pallas_call | solution.py:486
  40.5 1.4 %collective-permute-start.13 = (bf16[512,128]{1,0:T(8,128)(2,1)S(1)}, bf16[512,128]{1,0:T(8,128)(2,1)S(1)}, u32[]{:S(2)}, u32[]{:S(2)}) collective-permute-start(bf16[512,128]{1,0:T(8,128)(2,1)S(1)} %collective-permute-done.9.refs_1_), channel_id=1, source_target_pairs={{0,2},{2,0},{4,6},{6,4},{1,3},{3,1},{5,7},{7,5},{8,10},{10,8},{12,... | collective-permute-start | bytes 393224 | tf_op jit(solution)/shard_map/ppermute | solution.py:45
  45.7 3.6 %collective-permute-start.17 = (bf16[416,256]{1,0:T(8,128)(2,1)S(1)}, bf16[416,256]{1,0:T(8,128)(2,1)S(1)}, u32[]{:S(2)}, u32[]{:S(2)}) collective-permute-start(bf16[416,256]{1,0:T(8,128)(2,1)S(1)} %shard_map.217), channel_id=1, source_target_pairs={{0,16},{8,24},{16,0},{24,8},{1,17},{9,25},{17,1},{25,9},{2,18},{10... | collective-permute-start | bytes 638984 | tf_op jit(solution)/shard_map/ppermute | solution.py:49
  49.3 3.7 %shard_map.216.attended = bf16[256,256]{1,0:T(8,128)(2,1)S(1)} custom-call(s32[3]{0:T(128)S(1)} %pad_add_fusion.place, s32[1]{0:T(128)} %copy.26.length, bf16[256,256]{1,0:T(8,128)(2,1)S(1)} %get-tuple-element.36.query, bf16[512,128]{1,0:T(8,128)(2,1)S(1)} %get-tuple-element.37.refs_0_, bf16[512,128]{1,0:T(8,128)(2,1)S(1)} %collective-permute-done.9.refs_1_, ...), custom_call_target="tpu_custom_call" | custom-call | flops 6000000000 | tf_op jit(solution)/shard_map/pallas_call | solution.py:499
  53.0 2.3 %collective-permute-done.17.far = bf16[416,256]{1,0:T(8,128)(2,1)S(1)} collective-permute-done((bf16[416,256]{1,0:T(8,128)(2,1)S(1)}, bf16[416,256]{1,0:T(8,128)(2,1)S(1)}, u32[]{:S(2)}, u32[]{:S(2)}) %collective-permute-start.17) | collective-permute-done | bytes 213024 | tf_op jit(solution)/shard_map/ppermute | solution.py:49
  55.4 2.5 %shard_map.219 = (f32[1,1,3,128,256]{4,3,2,1,0:T(8,128)}, bf16[256,384]{1,0:T(8,128)(2,1)S(1)}, bf16[128,768]{1,0:T(8,128)(2,1)S(1)}, bf16[128,768]{1,0:T(8,128)(2,1)S(1)}) custom-call(s32[3]{0:T(128)S(1)} %pad_add_fusion.1.place, bf16[416,256]{1,0:T(8,128)(2,1)S(1)} %collective-permute-done.16.second.near, ...), custom_call_target="tpu_custom_call" | custom-call | flops 3000000000 | tf_op jit(solution)/shard_map/pallas_call | solution.py:528
  57.8 1.5 %collective-permute-start.22 = (bf16[128,768]{1,0:T(8,128)(2,1)S(1)}, bf16[128,768]{1,0:T(8,128)(2,1)S(1)}, u32[]{:S(2)}, u32[]{:S(2)}) collective-permute-start(bf16[128,768]{1,0:T(8,128)(2,1)S(1)} %get-tuple-element.50), channel_id=1, source_target_pairs={{0,4},{2,6},{4,0},{6,2},{1,5},{3,7},{5,1},{7,3},{8,12},{10,14},{12... | collective-permute-start | bytes 589832 | tf_op jit(solution)/shard_map/ppermute | solution.py:45
  66.7 1.6 %collective-permute-start.20 = (bf16[128,768]{1,0:T(8,128)(2,1)S(1)}, bf16[128,768]{1,0:T(8,128)(2,1)S(1)}, u32[]{:S(2)}, u32[]{:S(2)}) collective-permute-start(bf16[128,768]{1,0:T(8,128)(2,1)S(1)} %add_convert_fusion.1), channel_id=1, source_target_pairs={{0,4},{2,6},{4,0},{6,2},{1,5},{3,7},{5,1},{7,3},{8,12},{10,14},{12... | collective-permute-start | bytes 589832 | tf_op jit(solution)/shard_map/ppermute | solution.py:45
  68.3 3.1 %collective-permute-done.23 = bf16[128,768]{1,0:T(8,128)(2,1)S(1)} collective-permute-done((bf16[128,768]{1,0:T(8,128)(2,1)S(1)}, bf16[128,768]{1,0:T(8,128)(2,1)S(1)}, u32[]{:S(2)}, u32[]{:S(2)}) %collective-permute-start.23) | collective-permute-done | bytes 196640 | tf_op jit(solution)/shard_map/ppermute | solution.py:45
  (87 shorter events, 19.9 us)
Async XLA Ops:
  0.6 12.3 %collective-permute-start = (bf16[256,768]{1,0:T(8,128)(2,1)}, bf16[256,768]{1,0:T(8,128)(2,1)S(1)}, u32[]{:S(2)}, u32[]{:S(2)}) collective-permute-start(bf16[256,768]{1,0:T(8,128)(2,1)} %bitcast.21), channel_id=1, source_target_pairs={{0,2},{2,0},{4,6},{6,4},{1,3},{3,1},{5,7},{7,5},{8,10},{10,8},{12,... | collective-permute-start | bytes 1179656 | tf_op jit(solution)/shard_map/ppermute | solution.py:45
  3.6 10.8 %collective-permute-start.1 = (bf16[256,768]{1,0:T(8,128)(2,1)}, bf16[256,768]{1,0:T(8,128)(2,1)S(1)}, u32[]{:S(2)}, u32[]{:S(2)}) collective-permute-start(bf16[256,768]{1,0:T(8,128)(2,1)} %bitcast.22), channel_id=1, source_target_pairs={{0,4},{2,6},{4,0},{6,2},{1,5},{3,7},{5,1},{7,3},{8,12},{10,14},{12... | collective-permute-start | bytes 1179656 | tf_op jit(solution)/shard_map/ppermute | solution.py:45
  5.9 5.6 %collective-permute-start.2 = (bf16[16,768]{1,0:T(8,128)(2,1)S(1)}, bf16[16,768]{1,0:T(8,128)(2,1)S(1)}, u32[]{:S(2)}, u32[]{:S(2)}) collective-permute-start(bf16[16,768]{1,0:T(8,128)(2,1)S(1)} %slice_bitcast_fusion), channel_id=1, source_target_pairs={{0,8},{8,16},{16,24},{24,0},{1,9},{9,17},{17,25},{25,1},{2,10},{10... | collective-permute-start | bytes 73736 | tf_op jit(solution)/shard_map/ppermute | solution.py:54
  14.5 7.8 %collective-permute-start.3 = (bf16[144,768]{1,0:T(8,128)(2,1)S(1)}, bf16[144,768]{1,0:T(8,128)(2,1)S(1)}, u32[]{:S(2)}, u32[]{:S(2)}) collective-permute-start(bf16[144,768]{1,0:T(8,128)(2,1)S(1)} %get-tuple-element.28), channel_id=1, source_target_pairs={{0,4},{2,6},{4,0},{6,2},{1,5},{3,7},{5,1},{7,3},{8,12},{10,14},{12... | collective-permute-start | bytes 663560 | tf_op jit(solution)/shard_map/ppermute | solution.py:45
  16.0 6.2 %collective-permute-start.4 = (bf16[144,768]{1,0:T(8,128)(2,1)S(1)}, bf16[144,768]{1,0:T(8,128)(2,1)S(1)}, u32[]{:S(2)}, u32[]{:S(2)}) collective-permute-start(bf16[144,768]{1,0:T(8,128)(2,1)S(1)} %get-tuple-element.29), channel_id=1, source_target_pairs={{0,2},{2,0},{4,6},{6,4},{1,3},{3,1},{5,7},{7,5},{8,10},{10,8},{12,... | collective-permute-start | bytes 663560 | tf_op jit(solution)/shard_map/ppermute | solution.py:45
  16.6 5.6 %collective-permute-start.5 = (bf16[16,768]{1,0:T(8,128)(2,1)S(1)}, bf16[16,768]{1,0:T(8,128)(2,1)S(1)}, u32[]{:S(2)}, u32[]{:S(2)}) collective-permute-start(bf16[16,768]{1,0:T(8,128)(2,1)S(1)} %collective-permute-done.2.rim), channel_id=1, source_target_pairs={{0,6},{2,4},{4,2},{6,0},{1,7},{3,5},{5,3},{7,1},{8,14},{10,12},{12... | collective-permute-start | bytes 73736 | tf_op jit(solution)/shard_map/ppermute | solution.py:45
  25.3 10.1 %collective-permute-start.6 = (bf16[272,128]{1,0:T(8,128)(2,1)S(1)}, bf16[272,128]{1,0:T(8,128)(2,1)S(1)}, u32[]{:S(2)}, u32[]{:S(2)}) collective-permute-start(bf16[272,128]{1,0:T(8,128)(2,1)S(1)} %get-tuple-element.32.bc0), channel_id=1, source_target_pairs={{0,2},{2,0},{4,6},{6,4},{1,3},{3,1},{5,7},{7,5},{8,10},{10,8},{12,... | collective-permute-start | bytes 208904 | tf_op jit(solution)/shard_map/ppermute | solution.py:45
  26.0 9.6 %collective-permute-start.7 = (bf16[272,128]{1,0:T(8,128)(2,1)S(1)}, bf16[272,128]{1,0:T(8,128)(2,1)S(1)}, u32[]{:S(2)}, u32[]{:S(2)}) collective-permute-start(bf16[272,128]{1,0:T(8,128)(2,1)S(1)} %get-tuple-element.32.bc0), channel_id=1, source_target_pairs={{0,4},{2,6},{4,0},{6,2},{1,5},{3,7},{5,1},{7,3},{8,12},{10,14},{12... | collective-permute-start | bytes 208904 | tf_op jit(solution)/shard_map/ppermute | solution.py:45
  27.4 8.9 %collective-permute-start.8 = (bf16[272,128]{1,0:T(8,128)(2,1)S(1)}, bf16[272,128]{1,0:T(8,128)(2,1)S(1)}, u32[]{:S(2)}, u32[]{:S(2)}) collective-permute-start(bf16[272,128]{1,0:T(8,128)(2,1)S(1)} %get-tuple-element.32.bc0), channel_id=1, source_target_pairs={{0,6},{2,4},{4,2},{6,0},{1,7},{3,5},{5,3},{7,1},{8,14},{10,12},{12... | collective-permute-start | bytes 208904 | tf_op jit(solution)/shard_map/ppermute | solution.py:45
  28.8 11.7 %collective-permute-start.9 = (bf16[512,128]{1,0:T(8,128)(2,1)S(1)}, bf16[512,128]{1,0:T(8,128)(2,1)S(1)}, u32[]{:S(2)}, u32[]{:S(2)}) collective-permute-start(bf16[512,128]{1,0:T(8,128)(2,1)S(1)} %get-tuple-element.37.refs_0_), channel_id=1, source_target_pairs={{0,8},{8,0},{16,24},{24,16},{1,9},{9,1},{17,25},{25,17},{2,10},{10... | collective-permute-start | bytes 393224 | tf_op jit(solution)/shard_map/ppermute | solution.py:49
  30.4 11.5 %collective-permute-start.10 = (bf16[512,128]{1,0:T(8,128)(2,1)S(1)}, bf16[512,128]{1,0:T(8,128)(2,1)S(1)}, u32[]{:S(2)}, u32[]{:S(2)}) collective-permute-start(bf16[512,128]{1,0:T(8,128)(2,1)S(1)} %get-tuple-element.37.refs_0_), channel_id=1, source_target_pairs={{0,16},{8,24},{16,0},{24,8},{1,17},{9,25},{17,1},{25,9},{2,18},{10... | collective-permute-start | bytes 393224 | tf_op jit(solution)/shard_map/ppermute | solution.py:49
  35.4 7.2 %collective-permute-start.11 = (bf16[512,128]{1,0:T(8,128)(2,1)S(1)}, bf16[512,128]{1,0:T(8,128)(2,1)S(1)}, u32[]{:S(2)}, u32[]{:S(2)}) collective-permute-start(bf16[512,128]{1,0:T(8,128)(2,1)S(1)} %get-tuple-element.37.refs_0_), channel_id=1, source_target_pairs={{0,24},{8,16},{16,8},{24,0},{1,25},{9,17},{17,9},{25,1},{2,26},{10... | collective-permute-start | bytes 393224 | tf_op jit(solution)/shard_map/ppermute | solution.py:49
  35.6 13.6 %collective-permute-start.12 = (bf16[512,128]{1,0:T(8,128)(2,1)S(1)}, bf16[512,128]{1,0:T(8,128)(2,1)S(1)}, u32[]{:S(2)}, u32[]{:S(2)}) collective-permute-start(bf16[512,128]{1,0:T(8,128)(2,1)S(1)} %get-tuple-element.37.refs_0_), channel_id=1, source_target_pairs={{0,2},{2,0},{4,6},{6,4},{1,3},{3,1},{5,7},{7,5},{8,10},{10,8},{12,... | collective-permute-start | bytes 393224 | tf_op jit(solution)/shard_map/ppermute | solution.py:45
  38.3 6.7 %collective-permute-start.16 = (bf16[416,256]{1,0:T(8,128)(2,1)S(1)}, bf16[416,256]{1,0:T(8,128)(2,1)S(1)}, u32[]{:S(2)}, u32[]{:S(2)}) collective-permute-start(bf16[416,256]{1,0:T(8,128)(2,1)S(1)} %get-tuple-element.38.first), channel_id=1, source_target_pairs={{0,8},{8,0},{16,24},{24,16},{1,9},{9,1},{17,25},{25,17},{2,10},{10... | collective-permute-start | bytes 638984 | tf_op jit(solution)/shard_map/ppermute | solution.py:49
  40.5 8.8 %collective-permute-start.13 = (bf16[512,128]{1,0:T(8,128)(2,1)S(1)}, bf16[512,128]{1,0:T(8,128)(2,1)S(1)}, u32[]{:S(2)}, u32[]{:S(2)}) collective-permute-start(bf16[512,128]{1,0:T(8,128)(2,1)S(1)} %collective-permute-done.9.refs_1_), channel_id=1, source_target_pairs={{0,2},{2,0},{4,6},{6,4},{1,3},{3,1},{5,7},{7,5},{8,10},{10,8},{12,... | collective-permute-start | bytes 393224 | tf_op jit(solution)/shard_map/ppermute | solution.py:45
  41.9 7.3 %collective-permute-start.14 = (bf16[512,128]{1,0:T(8,128)(2,1)S(1)}, bf16[512,128]{1,0:T(8,128)(2,1)S(1)}, u32[]{:S(2)}, u32[]{:S(2)}) collective-permute-start(bf16[512,128]{1,0:T(8,128)(2,1)S(1)} %collective-permute-done.10.refs_2_), channel_id=1, source_target_pairs={{0,2},{2,0},{4,6},{6,4},{1,3},{3,1},{5,7},{7,5},{8,10},{10,8},{12,... | collective-permute-start | bytes 393224 | tf_op jit(solution)/shard_map/ppermute | solution.py:45
  42.6 6.7 %collective-permute-start.15 = (bf16[512,128]{1,0:T(8,128)(2,1)S(1)}, bf16[512,128]{1,0:T(8,128)(2,1)S(1)}, u32[]{:S(2)}, u32[]{:S(2)}) collective-permute-start(bf16[512,128]{1,0:T(8,128)(2,1)S(1)} %collective-permute-done.11.refs_3_), channel_id=1, source_target_pairs={{0,2},{2,0},{4,6},{6,4},{1,3},{3,1},{5,7},{7,5},{8,10},{10,8},{12,... | collective-permute-start | bytes 393224 | tf_op jit(solution)/shard_map/ppermute | solution.py:45
  45.7 9.7 %collective-permute-start.17 = (bf16[416,256]{1,0:T(8,128)(2,1)S(1)}, bf16[416,256]{1,0:T(8,128)(2,1)S(1)}, u32[]{:S(2)}, u32[]{:S(2)}) collective-permute-start(bf16[416,256]{1,0:T(8,128)(2,1)S(1)} %shard_map.217), channel_id=1, source_target_pairs={{0,16},{8,24},{16,0},{24,8},{1,17},{9,25},{17,1},{25,9},{2,18},{10... | collective-permute-start | bytes 638984 | tf_op jit(solution)/shard_map/ppermute | solution.py:49
  57.8 7.7 %collective-permute-start.22 = (bf16[128,768]{1,0:T(8,128)(2,1)S(1)}, bf16[128,768]{1,0:T(8,128)(2,1)S(1)}, u32[]{:S(2)}, u32[]{:S(2)}) collective-permute-start(bf16[128,768]{1,0:T(8,128)(2,1)S(1)} %get-tuple-element.50), channel_id=1, source_target_pairs={{0,4},{2,6},{4,0},{6,2},{1,5},{3,7},{5,1},{7,3},{8,12},{10,14},{12... | collective-permute-start | bytes 589832 | tf_op jit(solution)/shard_map/ppermute | solution.py:45
  60.4 7.9 %collective-permute-start.21 = (bf16[128,768]{1,0:T(8,128)(2,1)S(1)}, bf16[128,768]{1,0:T(8,128)(2,1)S(1)}, u32[]{:S(2)}, u32[]{:S(2)}) collective-permute-start(bf16[128,768]{1,0:T(8,128)(2,1)S(1)} %get-tuple-element.48), channel_id=1, source_target_pairs={{0,4},{2,6},{4,0},{6,2},{1,5},{3,7},{5,1},{7,3},{8,12},{10,14},{12... | collective-permute-start | bytes 589832 | tf_op jit(solution)/shard_map/ppermute | solution.py:45
  61.0 5.7 %collective-permute-start.19 = (bf16[128,768]{1,0:T(8,128)(2,1)S(1)}, bf16[128,768]{1,0:T(8,128)(2,1)S(1)}, u32[]{:S(2)}, u32[]{:S(2)}) collective-permute-start(bf16[128,768]{1,0:T(8,128)(2,1)S(1)} %get-tuple-element.47), channel_id=1, source_target_pairs={{0,2},{2,0},{4,6},{6,4},{1,3},{3,1},{5,7},{7,5},{8,10},{10,8},{12,... | collective-permute-start | bytes 589832 | tf_op jit(solution)/shard_map/ppermute | solution.py:45
  61.6 9.7 %collective-permute-start.18 = (bf16[128,768]{1,0:T(8,128)(2,1)S(1)}, bf16[128,768]{1,0:T(8,128)(2,1)S(1)}, u32[]{:S(2)}, u32[]{:S(2)}) collective-permute-start(bf16[128,768]{1,0:T(8,128)(2,1)S(1)} %get-tuple-element.44.sent), channel_id=1, source_target_pairs={{0,2},{2,0},{4,6},{6,4},{1,3},{3,1},{5,7},{7,5},{8,10},{10,8},{12,... | collective-permute-start | bytes 589832 | tf_op jit(solution)/shard_map/ppermute | solution.py:45
  65.6 5.7 %collective-permute-start.23 = (bf16[128,768]{1,0:T(8,128)(2,1)S(1)}, bf16[128,768]{1,0:T(8,128)(2,1)S(1)}, u32[]{:S(2)}, u32[]{:S(2)}) collective-permute-start(bf16[128,768]{1,0:T(8,128)(2,1)S(1)} %add_convert_fusion), channel_id=1, source_target_pairs={{0,2},{2,0},{4,6},{6,4},{1,3},{3,1},{5,7},{7,5},{8,10},{10,8},{12,... | collective-permute-start | bytes 589832 | tf_op jit(solution)/shard_map/ppermute | solution.py:45
  66.7 5.7 %collective-permute-start.20 = (bf16[128,768]{1,0:T(8,128)(2,1)S(1)}, bf16[128,768]{1,0:T(8,128)(2,1)S(1)}, u32[]{:S(2)}, u32[]{:S(2)}) collective-permute-start(bf16[128,768]{1,0:T(8,128)(2,1)S(1)} %add_convert_fusion.1), channel_id=1, source_target_pairs={{0,4},{2,6},{4,0},{6,2},{1,5},{3,7},{5,1},{7,3},{8,12},{10,14},{12... | collective-permute-start | bytes 589832 | tf_op jit(solution)/shard_map/ppermute | solution.py:45
  (18 other events, 99.9 us)

commit v5 on v4

--- a/solution.py
+++ b/solution.py
@@ -96,19 +96,29 @@
         return pl.ds(pl.multiple_of((me ^ turn) * width, 128), width)
 
     def rows(start, count, blocks):
-        square = sum(
-            jnp.sum(b.astype(f32) * b.astype(f32), axis=1, keepdims=True) for b in blocks
-        )
-        inverse = lax.rsqrt(square * full + epsilon)
-        for turn, block in enumerate(blocks):
-            scaled = block.astype(f32) * inverse * gain[:, columns(turn)]
-            normed[pl.ds(start, count), columns(turn)] = scaled.astype(bf16)
+        size = min(count, 32)
+        for at in range(0, count, size):
+            parts = [block[at : at + size].astype(f32) for block in blocks]
+            square = sum(
+                part[:, lane : lane + 128] * part[:, lane : lane + 128]
+                for part in parts
+                for lane in range(0, width, 128)
+            )
+            inverse = lax.rsqrt(jnp.sum(square, axis=1, keepdims=True) * full + epsilon)
+            for turn, part in enumerate(parts):
+                scaled = part * inverse * gain[:, columns(turn)]
+                normed[pl.ds(start + at, size), columns(turn)] = scaled.astype(bf16)
 
     rows(0, RIM, [rim[...], by_x[half:], by_y[half:], diag_rim[...]])
     rows(RIM, half, [own[:half], from_x[:half], from_y[:half], by_y[:half]])
     rows(RIM + half, half, [own[half:], from_x[half:], from_y[half:], by_x[:half]])
-    bc[...] = dot(normed[...], w_bc[...]).astype(bf16)
-    projected = dot(normed[RIM:, :], w_kv[...])
+    both = None
+    for at in range(0, 4 * width, width):
+        weights = jnp.concatenate([w_bc[at : at + width], w_kv[at : at + width]], axis=1)
+        part = dot(normed[:, at : at + width], weights)
+        both = part if both is None else both + part
+    bc[...] = both[:, :HD].astype(bf16)
+    projected = both[RIM:, HD:]
     turned = rope(projected, cos[...], sin[...])
     block = jnp.where(me % 2 == 0, turned, projected).astype(bf16)
     kv[...] = block
@@ -240,8 +250,8 @@
 
 
 def finish_kernel(
-    place, near, far, init, own, c_mat, cumulative, y, gate_z, gain, attended, w_attn, w_mamba,
-    states, mixed, far_x, far_y,
+    place, near, far, init, c_mat, cumulative, y, gate_z, gain, attended, w_attn, w_mamba,
+    incomes, mixed, far_x, far_y,
 ):
     me = place[0]
     heads = init.shape[1]
@@ -252,9 +262,6 @@
     near_log = jnp.where(near_on, log_from(near[size:, :]), 0.0)
     far_log = jnp.where(far_on, log_from(far[size:, :]), 0.0)
     near_grown, far_grown = jnp.exp(near_log), jnp.exp(near_log + far_log)
-    block_grown = jnp.exp(
-        jnp.broadcast_to(cumulative[:, tokens - 1 : tokens], (8, NS))
-    )
     growth = jnp.transpose(jnp.exp(cumulative[...]))
     for h in range(heads):
         block = pl.ds(h * HD, HD)
@@ -263,7 +270,7 @@
             + near_grown[h : h + 1, :] * jnp.where(far_on, far[block, :].astype(f32), 0.0)
             + far_grown[h : h + 1, :] * init[0, h]
         )
-        states[0, 0, h] = block_grown[h : h + 1, :] * incoming + own[block, :]
+        incomes[block, :] = incoming
         carried = dot_nt(c_mat[...], incoming.astype(bf16)) * growth[:, h : h + 1]
         gated = (y[:, block] + carried) * silu(gate_z[:, block].astype(f32))
         mean_sq = jnp.sum(gated * gated, axis=1, keepdims=True) * (1.0 / HD)
@@ -281,7 +288,15 @@
     to_y[...] = term(2, half, half).astype(bf16)
 
 
-def keep_kernel(place, attended, mixed, w_attn, w_mamba, own, sent, keep, keep_top, keep_low):
+def keep_kernel(
+    place, attended, mixed, w_attn, w_mamba, own, incomes, own_state, cumulative, sent,
+    keep, keep_top, keep_low, states,
+):
+    last = cumulative.shape[1] - 1
+    grown = jnp.exp(jnp.broadcast_to(cumulative[:, last : last + 1], (8, NS)))
+    for h in range(states.shape[2]):
+        block = pl.ds(h * HD, HD)
+        states[0, 0, h] = grown[h : h + 1, :] * incomes[block, :] + own_state[block, :]
     tokens, width = own.shape
     half = tokens // 2
     term = term_of(place[0], attended, mixed, w_attn, w_mamba, width)
@@ -525,19 +540,19 @@
             seq_pos,
         )
 
-    state_after, mixed, far_x, far_y = call(
+    incomes, mixed, far_x, far_y = call(
         finish_kernel,
         (
-            shape(1, 1, heads, HD, NS, dtype=f32),
+            shape(heads * HD, NS, dtype=f32),
             shape(tokens, inner_width),
             shape(half, width),
             shape(half, width),
         ),
         1,
-        12,
+        11,
         3,
     )(
-        taken, near, far, ssm_init, own_state, c_mat, cumulative, y_inside, gate_z, mixer_gain,
+        taken, near, far, ssm_init, c_mat, cumulative, y_inside, gate_z, mixer_gain,
         attended, w_attn_out, w_mamba_out,
     )
 
@@ -546,18 +561,21 @@
     to_x, to_y = call(
         near_kernel, (shape(half, width), shape(half, width)), 1, 4, 1
     )(place, attended, mixed, w_attn_out, w_mamba_out)
-    keep, keep_top, keep_low = call(
+    keep, keep_top, keep_low, state_after = call(
         keep_kernel,
         (
             shape(tokens, width, dtype=f32),
             shape(half, width, dtype=f32),
             shape(half, width, dtype=f32),
+            shape(1, 1, heads, HD, NS, dtype=f32),
         ),
         1,
-        5,
+        8,
         1,
         left=1,
-    )(place, attended, mixed, w_attn_out, w_mamba_out, own_rows, to_x)
+    )(
+        place, attended, mixed, w_attn_out, w_mamba_out, own_rows, incomes, own_state, cumulative, to_x
+    )
     top_in = swap(to_x, 1)
     low_in = swap(to_y, 2)
     top_last = swap((keep_top + far_x_in.astype(f32)).astype(bf16), 2)

time: 73.5 us -> 72.3 us (0.984)
    ppermute x18, waiting for transfers between devices: 9.61 us -> 8.85 us  [swap(): lax.ppermute(block, 'mp', [(i, i ^ turn) for i in range(lax.axis_size('mp...]
    pallas_call x1, Pallas kernels: 2.48 us -> 1.72 us  [shards(): call(finish_kernel, (shape(heads * HD, NS, dtype=f32), shape(tokens, inne...]
    pallas_call x1, Pallas kernels: 1.33 us -> 2.07 us  [shards(): call(keep_kernel, (shape(tokens, width, dtype=f32), shape(half, width, dt...]
  transfers between devices with their start and end apart: 24 -> 24, of which waited for: 9 -> 9; matrix products, arithmetic and copies ran while one was open for 7% -> 7% of each run, Pallas kernels for 18% -> 20%
where the time goes in v5:
time: 72.3 us; the launch traced here: 72.1 us
  starting transfers between devices  32.3 us (45%)
  Pallas kernels  18.6 us (26%)
  waiting for transfers between devices  13.9 us (19%)
  local copies, waits for them, and re-layouts  3.97 us (5%)
  other arithmetic  1.79 us (2%)
  between operations  1.67 us (2%)
    ppermute x18, starting transfers between devices, swap(): lax.ppermute(block, 'mp', [(i, i ^ turn) for i in range(lax.axis_size('mp...  22 us
    ppermute x18, waiting for transfers between devices, swap(): lax.ppermute(block, 'mp', [(i, i ^ turn) for i in range(lax.axis_size('mp...  8.85 us
    ppermute x5, starting transfers between devices, cross(): lax.ppermute(block, 'seq', [(i, i ^ turn) for i in range(lax.axis_size('s...  8.66 us
    pallas_call x1, Pallas kernels, shards(): call(functools.partial(attention_kernel, cache_rows=cache_rows, scale=HD...  3.72 us
    unnamed x37, local copies, waits for them, and re-layouts  3.19 us
    ppermute x1, waiting for transfers between devices, ahead(): lax.ppermute(block, 'seq', [(i, (i + 1) % count) for i in range(count)])  2.68 us
    pallas_call x1, Pallas kernels, shards(): call(norm_kernel, (shape(RIM + tokens, 4 * width), shape(RIM + tokens, w_...  2.48 us
    pallas_call x1, Pallas kernels, shards(): call(steps_kernel, (shape(RIM + tokens, inner_width), shape(8, tokens, dt...  2.34 us
  transfers between devices with their start and end apart: 24, of which 9 were waited for; matrix products, arithmetic and copies ran while one was open for 7% of the time, Pallas kernels for 20%

profile of v5, /device:TPU:0, one launch (start us, length us, event | category | flops | bytes accessed | tf_op | source)
XLA Modules:
  0.0 72.1 jit_solution(5489178961779614029)
XLA Ops:
  0.6 3.0 %collective-permute-start = (bf16[256,768]{1,0:T(8,128)(2,1)}, bf16[256,768]{1,0:T(8,128)(2,1)S(1)}, u32[]{:S(2)}, u32[]{:S(2)}) collective-permute-start(bf16[256,768]{1,0:T(8,128)(2,1)} %bitcast.21), channel_id=1, source_target_pairs={{0,2},{2,0},{4,6},{6,4},{1,3},{3,1},{5,7},{7,5},{8,10},{10,8},{12,... | collective-permute-start | bytes 1179656 | tf_op jit(solution)/shard_map/ppermute | solution.py:45
  3.6 1.5 %collective-permute-start.1 = (bf16[256,768]{1,0:T(8,128)(2,1)}, bf16[256,768]{1,0:T(8,128)(2,1)S(1)}, u32[]{:S(2)}, u32[]{:S(2)}) collective-permute-start(bf16[256,768]{1,0:T(8,128)(2,1)} %bitcast.22), channel_id=1, source_target_pairs={{0,4},{2,6},{4,0},{6,2},{1,5},{3,7},{5,1},{7,3},{8,12},{10,14},{12... | collective-permute-start | bytes 1179656 | tf_op jit(solution)/shard_map/ppermute | solution.py:45
  5.9 1.6 %collective-permute-start.2 = (bf16[16,768]{1,0:T(8,128)(2,1)S(1)}, bf16[16,768]{1,0:T(8,128)(2,1)S(1)}, u32[]{:S(2)}, u32[]{:S(2)}) collective-permute-start(bf16[16,768]{1,0:T(8,128)(2,1)S(1)} %slice_bitcast_fusion), channel_id=1, source_target_pairs={{0,8},{8,16},{16,24},{24,0},{1,9},{9,17},{17,25},{25,1},{2,10},{10... | collective-permute-start | bytes 73736 | tf_op jit(solution)/shard_map/ppermute | solution.py:54
  8.9 2.7 %collective-permute-done.2.rim = bf16[16,768]{1,0:T(8,128)(2,1)S(1)} collective-permute-done((bf16[16,768]{1,0:T(8,128)(2,1)S(1)}, bf16[16,768]{1,0:T(8,128)(2,1)S(1)}, u32[]{:S(2)}, u32[]{:S(2)}) %collective-permute-start.2) | collective-permute-done | bytes 24608 | tf_op jit(solution)/shard_map/ppermute | solution.py:54
  13.0 1.5 %collective-permute-done.1.from_y = bf16[256,768]{1,0:T(8,128)(2,1)S(1)} collective-permute-done((bf16[256,768]{1,0:T(8,128)(2,1)}, bf16[256,768]{1,0:T(8,128)(2,1)S(1)}, u32[]{:S(2)}, u32[]{:S(2)}) %collective-permute-start.1) | collective-permute-done | bytes 393248 | tf_op jit(solution)/shard_map/ppermute | solution.py:45
  14.5 1.6 %collective-permute-start.3 = (bf16[144,768]{1,0:T(8,128)(2,1)S(1)}, bf16[144,768]{1,0:T(8,128)(2,1)S(1)}, u32[]{:S(2)}, u32[]{:S(2)}) collective-permute-start(bf16[144,768]{1,0:T(8,128)(2,1)S(1)} %get-tuple-element.29), channel_id=1, source_target_pairs={{0,4},{2,6},{4,0},{6,2},{1,5},{3,7},{5,1},{7,3},{8,12},{10,14},{12... | collective-permute-start | bytes 663560 | tf_op jit(solution)/shard_map/ppermute | solution.py:45
  16.6 1.4 %collective-permute-start.5 = (bf16[16,768]{1,0:T(8,128)(2,1)S(1)}, bf16[16,768]{1,0:T(8,128)(2,1)S(1)}, u32[]{:S(2)}, u32[]{:S(2)}) collective-permute-start(bf16[16,768]{1,0:T(8,128)(2,1)S(1)} %collective-permute-done.2.rim), channel_id=1, source_target_pairs={{0,6},{2,4},{4,2},{6,0},{1,7},{3,5},{5,3},{7,1},{8,14},{10,12},{12... | collective-permute-start | bytes 73736 | tf_op jit(solution)/shard_map/ppermute | solution.py:45
  18.2 3.1 %copy.25 = bf16[3072,2,384]{2,0,1:T(8,128)(2,1)S(1)} copy(bf16[3072,2,384]{2,1,0:T(2,128)(2,1)} %param.25) | data formatting | bytes 9437184 | tf_op args[5]
  22.3 2.5 %shard_map.212 = (bf16[272,3072]{1,0:T(8,128)(2,1)S(1)}, bf16[272,128]{1,0:T(8,128)(2,1)S(1)}, bf16[256,128]{1,0:T(8,128)(2,1)}, bf16[512,128]{1,0:T(8,128)(2,1)S(1)}) custom-call(s32[3]{0:T(128)S(1)} %pad_add_fusion.place, bf16[256,768]{1,0:T(8,128)(2,1)S(1)} %bitcast.23, bf16[256,768]{1,0:T(8,128)(2,1)S(1)} %collective-permute-done.from_x, ...), custom_call_target="tpu_custom_call" | custom-call | flops 3000000000 | tf_op jit(solution)/shard_map/pallas_call | solution.py:423
  25.5 1.4 %collective-permute-start.7 = (bf16[272,128]{1,0:T(8,128)(2,1)S(1)}, bf16[272,128]{1,0:T(8,128)(2,1)S(1)}, u32[]{:S(2)}, u32[]{:S(2)}) collective-permute-start(bf16[272,128]{1,0:T(8,128)(2,1)S(1)} %get-tuple-element.33.bc0), channel_id=1, source_target_pairs={{0,4},{2,6},{4,0},{6,2},{1,5},{3,7},{5,1},{7,3},{8,12},{10,14},{12... | collective-permute-start | bytes 208904 | tf_op jit(solution)/shard_map/ppermute | solution.py:45
  28.3 1.6 %collective-permute-start.9 = (bf16[512,128]{1,0:T(8,128)(2,1)S(1)}, bf16[512,128]{1,0:T(8,128)(2,1)S(1)}, u32[]{:S(2)}, u32[]{:S(2)}) collective-permute-start(bf16[512,128]{1,0:T(8,128)(2,1)S(1)} %get-tuple-element.38.refs_0_), channel_id=1, source_target_pairs={{0,8},{8,0},{16,24},{24,16},{1,9},{9,1},{17,25},{25,17},{2,10},{10... | collective-permute-start | bytes 393224 | tf_op jit(solution)/shard_map/ppermute | solution.py:49
  29.8 2.6 %collective-permute-start.10 = (bf16[512,128]{1,0:T(8,128)(2,1)S(1)}, bf16[512,128]{1,0:T(8,128)(2,1)S(1)}, u32[]{:S(2)}, u32[]{:S(2)}) collective-permute-start(bf16[512,128]{1,0:T(8,128)(2,1)S(1)} %get-tuple-element.38.refs_0_), channel_id=1, source_target_pairs={{0,16},{8,24},{16,0},{24,8},{1,17},{9,25},{17,1},{25,9},{2,18},{10... | collective-permute-start | bytes 393224 | tf_op jit(solution)/shard_map/ppermute | solution.py:49
  32.5 2.3 %shard_map.213 = (bf16[272,384]{1,0:T(8,128)(2,1)S(1)}, f32[8,256]{1,0:T(8,128)S(1)}, f32[8,256]{1,0:T(8,128)S(1)}) custom-call(f32[3]{0:T(128)S(1)} %copy-done.13, f32[3]{0:T(128)S(1)} %copy-done.14, bf16[272,3072]{1,0:T(8,128)(2,1)S(1)} %get-tuple-element.31.normed, bf16[2,3072,384]{2,1,0:T(8,128)(2,1)S(1)} %bitcast.19, bf16[3,3072]{1,0:T(4,128)(2,1)S(1)} %bitcast.27), custom_call_target="tpu_custom_call" | custom-call | flops 2000000000 | tf_op jit(solution)/shard_map/pallas_call | solution.py:442
  35.8 1.9 %shard_map.214 = (f32[384,256]{1,0:T(8,128)S(1)}, bf16[416,256]{1,0:T(8,128)(2,1)S(1)}, bf16[256,384]{1,0:T(8,128)(2,1)S(1)}, bf16[256,256]{1,0:T(8,128)(2,1)S(1)}, bf16[256,256]{1,0:T(8,128)(2,1)S(1)}) custom-call(s32[3]{0:T(128)S(1)} %pad_add_fusion.place, bf16[272,384]{1,0:T(8,128)(2,1)S(1)} %get-tuple-element.32.x_in, ...), custom_call_target="tpu_custom_call" | custom-call | flops 2000000000 | tf_op jit(solution)/shard_map/pallas_call | solution.py:460
  38.4 1.5 %shard_map.215 = (bf16[256,256]{1,0:T(8,128)(2,1)S(1)}, bf16[256,384]{1,0:T(8,128)(2,1)S(1)}) custom-call(bf16[272,3072]{1,0:T(8,128)(2,1)S(1)} %get-tuple-element.31.normed, bf16[3072,256]{1,0:T(8,128)(2,1)S(1)} %copy-done.2, bf16[2,3072,384]{2,1,0:T(8,128)(2,1)S(1)} %bitcast.20, f32[256,128]{1,0:T(8,128)S(1)} %get-tuple-element.56.cos, ...), custom_call_target="tpu_custom_call" | custom-call | flops 2000000000 | tf_op jit(solution)/shard_map/pallas_call | solution.py:501
  40.0 1.4 %collective-permute-start.13 = (bf16[512,128]{1,0:T(8,128)(2,1)S(1)}, bf16[512,128]{1,0:T(8,128)(2,1)S(1)}, u32[]{:S(2)}, u32[]{:S(2)}) collective-permute-start(bf16[512,128]{1,0:T(8,128)(2,1)S(1)} %collective-permute-done.9.refs_1_), channel_id=1, source_target_pairs={{0,2},{2,0},{4,6},{6,4},{1,3},{3,1},{5,7},{7,5},{8,10},{10,8},{12,... | collective-permute-start | bytes 393224 | tf_op jit(solution)/shard_map/ppermute | solution.py:45
  45.2 3.6 %collective-permute-start.17 = (bf16[416,256]{1,0:T(8,128)(2,1)S(1)}, bf16[416,256]{1,0:T(8,128)(2,1)S(1)}, u32[]{:S(2)}, u32[]{:S(2)}) collective-permute-start(bf16[416,256]{1,0:T(8,128)(2,1)S(1)} %shard_map.217), channel_id=1, source_target_pairs={{0,16},{8,24},{16,0},{24,8},{1,17},{9,25},{17,1},{25,9},{2,18},{10... | collective-permute-start | bytes 638984 | tf_op jit(solution)/shard_map/ppermute | solution.py:49
  48.8 3.7 %shard_map.216.attended = bf16[256,256]{1,0:T(8,128)(2,1)S(1)} custom-call(s32[3]{0:T(128)S(1)} %pad_add_fusion.place, s32[1]{0:T(128)} %copy.26.length, bf16[256,256]{1,0:T(8,128)(2,1)S(1)} %get-tuple-element.37.query, bf16[512,128]{1,0:T(8,128)(2,1)S(1)} %get-tuple-element.38.refs_0_, bf16[512,128]{1,0:T(8,128)(2,1)S(1)} %collective-permute-done.9.refs_1_, ...), custom_call_target="tpu_custom_call" | custom-call | flops 6000000000 | tf_op jit(solution)/shard_map/pallas_call | solution.py:514
  52.5 2.3 %collective-permute-done.17.far = bf16[416,256]{1,0:T(8,128)(2,1)S(1)} collective-permute-done((bf16[416,256]{1,0:T(8,128)(2,1)S(1)}, bf16[416,256]{1,0:T(8,128)(2,1)S(1)}, u32[]{:S(2)}, u32[]{:S(2)}) %collective-permute-start.17) | collective-permute-done | bytes 213024 | tf_op jit(solution)/shard_map/ppermute | solution.py:49
  54.8 1.7 %shard_map.219 = (f32[384,256]{1,0:T(8,128)S(1)}, bf16[256,384]{1,0:T(8,128)(2,1)S(1)}, bf16[128,768]{1,0:T(8,128)(2,1)S(1)}, bf16[128,768]{1,0:T(8,128)(2,1)S(1)}) custom-call(s32[3]{0:T(128)S(1)} %pad_add_fusion.1.place, bf16[416,256]{1,0:T(8,128)(2,1)S(1)} %collective-permute-done.16.second.near, bf16[416,256]{1,0:T(8,128)(2,1)S(1)} %collective-permute-done.17.far, ...), custom_call_target="tpu_custom_call" | custom-call | flops 3000000000 | tf_op jit(solution)/shard_map/pallas_call | solution.py:543
  56.6 1.6 %collective-permute-start.22 = (bf16[128,768]{1,0:T(8,128)(2,1)S(1)}, bf16[128,768]{1,0:T(8,128)(2,1)S(1)}, u32[]{:S(2)}, u32[]{:S(2)}) collective-permute-start(bf16[128,768]{1,0:T(8,128)(2,1)S(1)} %get-tuple-element.52), channel_id=1, source_target_pairs={{0,4},{2,6},{4,0},{6,2},{1,5},{3,7},{5,1},{7,3},{8,12},{10,14},{12... | collective-permute-start | bytes 589832 | tf_op jit(solution)/shard_map/ppermute | solution.py:45
  61.8 2.1 %shard_map.221 = (f32[256,768]{1,0:T(8,128)S(1)}, f32[128,768]{1,0:T(8,128)S(1)}, f32[128,768]{1,0:T(8,128)S(1)}, f32[1,1,3,128,256]{4,3,2,1,0:T(8,128)}) custom-call(s32[3]{0:T(128)S(1)} %pad_add_fusion.place, bf16[256,256]{1,0:T(8,128)(2,1)S(1)} %shard_map.216.attended, bf16[256,384]{1,0:T(8,128)(2,1)S(1)} %get-tuple-element.43.mixed, ...), custom_call_target="tpu_custom_call" | custom-call | flops 1000000000 | tf_op jit(solution)/shard_map/pallas_call | solution.py:564
  65.5 1.6 %collective-permute-start.20 = (bf16[128,768]{1,0:T(8,128)(2,1)S(1)}, bf16[128,768]{1,0:T(8,128)(2,1)S(1)}, u32[]{:S(2)}, u32[]{:S(2)}) collective-permute-start(bf16[128,768]{1,0:T(8,128)(2,1)S(1)} %add_convert_fusion.1), channel_id=1, source_target_pairs={{0,4},{2,6},{4,0},{6,2},{1,5},{3,7},{5,1},{7,3},{8,12},{10,14},{12... | collective-permute-start | bytes 589832 | tf_op jit(solution)/shard_map/ppermute | solution.py:45
  67.1 3.0 %collective-permute-done.23 = bf16[128,768]{1,0:T(8,128)(2,1)S(1)} collective-permute-done((bf16[128,768]{1,0:T(8,128)(2,1)S(1)}, bf16[128,768]{1,0:T(8,128)(2,1)S(1)}, u32[]{:S(2)}, u32[]{:S(2)}) %collective-permute-start.23) | collective-permute-done | bytes 196640 | tf_op jit(solution)/shard_map/ppermute | solution.py:45
  (87 shorter events, 19.2 us)
Async XLA Ops:
  0.6 12.3 %collective-permute-start = (bf16[256,768]{1,0:T(8,128)(2,1)}, bf16[256,768]{1,0:T(8,128)(2,1)S(1)}, u32[]{:S(2)}, u32[]{:S(2)}) collective-permute-start(bf16[256,768]{1,0:T(8,128)(2,1)} %bitcast.21), channel_id=1, source_target_pairs={{0,2},{2,0},{4,6},{6,4},{1,3},{3,1},{5,7},{7,5},{8,10},{10,8},{12,... | collective-permute-start | bytes 1179656 | tf_op jit(solution)/shard_map/ppermute | solution.py:45
  3.6 10.8 %collective-permute-start.1 = (bf16[256,768]{1,0:T(8,128)(2,1)}, bf16[256,768]{1,0:T(8,128)(2,1)S(1)}, u32[]{:S(2)}, u32[]{:S(2)}) collective-permute-start(bf16[256,768]{1,0:T(8,128)(2,1)} %bitcast.22), channel_id=1, source_target_pairs={{0,4},{2,6},{4,0},{6,2},{1,5},{3,7},{5,1},{7,3},{8,12},{10,14},{12... | collective-permute-start | bytes 1179656 | tf_op jit(solution)/shard_map/ppermute | solution.py:45
  5.9 5.6 %collective-permute-start.2 = (bf16[16,768]{1,0:T(8,128)(2,1)S(1)}, bf16[16,768]{1,0:T(8,128)(2,1)S(1)}, u32[]{:S(2)}, u32[]{:S(2)}) collective-permute-start(bf16[16,768]{1,0:T(8,128)(2,1)S(1)} %slice_bitcast_fusion), channel_id=1, source_target_pairs={{0,8},{8,16},{16,24},{24,0},{1,9},{9,17},{17,25},{25,1},{2,10},{10... | collective-permute-start | bytes 73736 | tf_op jit(solution)/shard_map/ppermute | solution.py:54
  14.5 7.8 %collective-permute-start.3 = (bf16[144,768]{1,0:T(8,128)(2,1)S(1)}, bf16[144,768]{1,0:T(8,128)(2,1)S(1)}, u32[]{:S(2)}, u32[]{:S(2)}) collective-permute-start(bf16[144,768]{1,0:T(8,128)(2,1)S(1)} %get-tuple-element.29), channel_id=1, source_target_pairs={{0,4},{2,6},{4,0},{6,2},{1,5},{3,7},{5,1},{7,3},{8,12},{10,14},{12... | collective-permute-start | bytes 663560 | tf_op jit(solution)/shard_map/ppermute | solution.py:45
  16.0 6.2 %collective-permute-start.4 = (bf16[144,768]{1,0:T(8,128)(2,1)S(1)}, bf16[144,768]{1,0:T(8,128)(2,1)S(1)}, u32[]{:S(2)}, u32[]{:S(2)}) collective-permute-start(bf16[144,768]{1,0:T(8,128)(2,1)S(1)} %get-tuple-element.30), channel_id=1, source_target_pairs={{0,2},{2,0},{4,6},{6,4},{1,3},{3,1},{5,7},{7,5},{8,10},{10,8},{12,... | collective-permute-start | bytes 663560 | tf_op jit(solution)/shard_map/ppermute | solution.py:45
  16.6 5.6 %collective-permute-start.5 = (bf16[16,768]{1,0:T(8,128)(2,1)S(1)}, bf16[16,768]{1,0:T(8,128)(2,1)S(1)}, u32[]{:S(2)}, u32[]{:S(2)}) collective-permute-start(bf16[16,768]{1,0:T(8,128)(2,1)S(1)} %collective-permute-done.2.rim), channel_id=1, source_target_pairs={{0,6},{2,4},{4,2},{6,0},{1,7},{3,5},{5,3},{7,1},{8,14},{10,12},{12... | collective-permute-start | bytes 73736 | tf_op jit(solution)/shard_map/ppermute | solution.py:45
  24.8 10.1 %collective-permute-start.6 = (bf16[272,128]{1,0:T(8,128)(2,1)S(1)}, bf16[272,128]{1,0:T(8,128)(2,1)S(1)}, u32[]{:S(2)}, u32[]{:S(2)}) collective-permute-start(bf16[272,128]{1,0:T(8,128)(2,1)S(1)} %get-tuple-element.33.bc0), channel_id=1, source_target_pairs={{0,2},{2,0},{4,6},{6,4},{1,3},{3,1},{5,7},{7,5},{8,10},{10,8},{12,... | collective-permute-start | bytes 208904 | tf_op jit(solution)/shard_map/ppermute | solution.py:45
  25.5 9.6 %collective-permute-start.7 = (bf16[272,128]{1,0:T(8,128)(2,1)S(1)}, bf16[272,128]{1,0:T(8,128)(2,1)S(1)}, u32[]{:S(2)}, u32[]{:S(2)}) collective-permute-start(bf16[272,128]{1,0:T(8,128)(2,1)S(1)} %get-tuple-element.33.bc0), channel_id=1, source_target_pairs={{0,4},{2,6},{4,0},{6,2},{1,5},{3,7},{5,1},{7,3},{8,12},{10,14},{12... | collective-permute-start | bytes 208904 | tf_op jit(solution)/shard_map/ppermute | solution.py:45
  26.9 8.9 %collective-permute-start.8 = (bf16[272,128]{1,0:T(8,128)(2,1)S(1)}, bf16[272,128]{1,0:T(8,128)(2,1)S(1)}, u32[]{:S(2)}, u32[]{:S(2)}) collective-permute-start(bf16[272,128]{1,0:T(8,128)(2,1)S(1)} %get-tuple-element.33.bc0), channel_id=1, source_target_pairs={{0,6},{2,4},{4,2},{6,0},{1,7},{3,5},{5,3},{7,1},{8,14},{10,12},{12... | collective-permute-start | bytes 208904 | tf_op jit(solution)/shard_map/ppermute | solution.py:45
  28.3 11.7 %collective-permute-start.9 = (bf16[512,128]{1,0:T(8,128)(2,1)S(1)}, bf16[512,128]{1,0:T(8,128)(2,1)S(1)}, u32[]{:S(2)}, u32[]{:S(2)}) collective-permute-start(bf16[512,128]{1,0:T(8,128)(2,1)S(1)} %get-tuple-element.38.refs_0_), channel_id=1, source_target_pairs={{0,8},{8,0},{16,24},{24,16},{1,9},{9,1},{17,25},{25,17},{2,10},{10... | collective-permute-start | bytes 393224 | tf_op jit(solution)/shard_map/ppermute | solution.py:49
  29.8 11.6 %collective-permute-start.10 = (bf16[512,128]{1,0:T(8,128)(2,1)S(1)}, bf16[512,128]{1,0:T(8,128)(2,1)S(1)}, u32[]{:S(2)}, u32[]{:S(2)}) collective-permute-start(bf16[512,128]{1,0:T(8,128)(2,1)S(1)} %get-tuple-element.38.refs_0_), channel_id=1, source_target_pairs={{0,16},{8,24},{16,0},{24,8},{1,17},{9,25},{17,1},{25,9},{2,18},{10... | collective-permute-start | bytes 393224 | tf_op jit(solution)/shard_map/ppermute | solution.py:49
  34.8 7.2 %collective-permute-start.11 = (bf16[512,128]{1,0:T(8,128)(2,1)S(1)}, bf16[512,128]{1,0:T(8,128)(2,1)S(1)}, u32[]{:S(2)}, u32[]{:S(2)}) collective-permute-start(bf16[512,128]{1,0:T(8,128)(2,1)S(1)} %get-tuple-element.38.refs_0_), channel_id=1, source_target_pairs={{0,24},{8,16},{16,8},{24,0},{1,25},{9,17},{17,9},{25,1},{2,26},{10... | collective-permute-start | bytes 393224 | tf_op jit(solution)/shard_map/ppermute | solution.py:49
  35.1 13.7 %collective-permute-start.12 = (bf16[512,128]{1,0:T(8,128)(2,1)S(1)}, bf16[512,128]{1,0:T(8,128)(2,1)S(1)}, u32[]{:S(2)}, u32[]{:S(2)}) collective-permute-start(bf16[512,128]{1,0:T(8,128)(2,1)S(1)} %get-tuple-element.38.refs_0_), channel_id=1, source_target_pairs={{0,2},{2,0},{4,6},{6,4},{1,3},{3,1},{5,7},{7,5},{8,10},{10,8},{12,... | collective-permute-start | bytes 393224 | tf_op jit(solution)/shard_map/ppermute | solution.py:45
  37.7 6.8 %collective-permute-start.16 = (bf16[416,256]{1,0:T(8,128)(2,1)S(1)}, bf16[416,256]{1,0:T(8,128)(2,1)S(1)}, u32[]{:S(2)}, u32[]{:S(2)}) collective-permute-start(bf16[416,256]{1,0:T(8,128)(2,1)S(1)} %get-tuple-element.39.first), channel_id=1, source_target_pairs={{0,8},{8,0},{16,24},{24,16},{1,9},{9,1},{17,25},{25,17},{2,10},{10... | collective-permute-start | bytes 638984 | tf_op jit(solution)/shard_map/ppermute | solution.py:49
  40.0 8.8 %collective-permute-start.13 = (bf16[512,128]{1,0:T(8,128)(2,1)S(1)}, bf16[512,128]{1,0:T(8,128)(2,1)S(1)}, u32[]{:S(2)}, u32[]{:S(2)}) collective-permute-start(bf16[512,128]{1,0:T(8,128)(2,1)S(1)} %collective-permute-done.9.refs_1_), channel_id=1, source_target_pairs={{0,2},{2,0},{4,6},{6,4},{1,3},{3,1},{5,7},{7,5},{8,10},{10,8},{12,... | collective-permute-start | bytes 393224 | tf_op jit(solution)/shard_map/ppermute | solution.py:45
  41.4 7.3 %collective-permute-start.14 = (bf16[512,128]{1,0:T(8,128)(2,1)S(1)}, bf16[512,128]{1,0:T(8,128)(2,1)S(1)}, u32[]{:S(2)}, u32[]{:S(2)}) collective-permute-start(bf16[512,128]{1,0:T(8,128)(2,1)S(1)} %collective-permute-done.10.refs_2_), channel_id=1, source_target_pairs={{0,2},{2,0},{4,6},{6,4},{1,3},{3,1},{5,7},{7,5},{8,10},{10,8},{12,... | collective-permute-start | bytes 393224 | tf_op jit(solution)/shard_map/ppermute | solution.py:45
  42.1 6.7 %collective-permute-start.15 = (bf16[512,128]{1,0:T(8,128)(2,1)S(1)}, bf16[512,128]{1,0:T(8,128)(2,1)S(1)}, u32[]{:S(2)}, u32[]{:S(2)}) collective-permute-start(bf16[512,128]{1,0:T(8,128)(2,1)S(1)} %collective-permute-done.11.refs_3_), channel_id=1, source_target_pairs={{0,2},{2,0},{4,6},{6,4},{1,3},{3,1},{5,7},{7,5},{8,10},{10,8},{12,... | collective-permute-start | bytes 393224 | tf_op jit(solution)/shard_map/ppermute | solution.py:45
  45.2 9.7 %collective-permute-start.17 = (bf16[416,256]{1,0:T(8,128)(2,1)S(1)}, bf16[416,256]{1,0:T(8,128)(2,1)S(1)}, u32[]{:S(2)}, u32[]{:S(2)}) collective-permute-start(bf16[416,256]{1,0:T(8,128)(2,1)S(1)} %shard_map.217), channel_id=1, source_target_pairs={{0,16},{8,24},{16,0},{24,8},{1,17},{9,25},{17,1},{25,9},{2,18},{10... | collective-permute-start | bytes 638984 | tf_op jit(solution)/shard_map/ppermute | solution.py:49
  56.6 7.8 %collective-permute-start.22 = (bf16[128,768]{1,0:T(8,128)(2,1)S(1)}, bf16[128,768]{1,0:T(8,128)(2,1)S(1)}, u32[]{:S(2)}, u32[]{:S(2)}) collective-permute-start(bf16[128,768]{1,0:T(8,128)(2,1)S(1)} %get-tuple-element.52), channel_id=1, source_target_pairs={{0,4},{2,6},{4,0},{6,2},{1,5},{3,7},{5,1},{7,3},{8,12},{10,14},{12... | collective-permute-start | bytes 589832 | tf_op jit(solution)/shard_map/ppermute | solution.py:45
  59.2 7.9 %collective-permute-start.21 = (bf16[128,768]{1,0:T(8,128)(2,1)S(1)}, bf16[128,768]{1,0:T(8,128)(2,1)S(1)}, u32[]{:S(2)}, u32[]{:S(2)}) collective-permute-start(bf16[128,768]{1,0:T(8,128)(2,1)S(1)} %get-tuple-element.50), channel_id=1, source_target_pairs={{0,4},{2,6},{4,0},{6,2},{1,5},{3,7},{5,1},{7,3},{8,12},{10,14},{12... | collective-permute-start | bytes 589832 | tf_op jit(solution)/shard_map/ppermute | solution.py:45
  59.8 5.7 %collective-permute-start.19 = (bf16[128,768]{1,0:T(8,128)(2,1)S(1)}, bf16[128,768]{1,0:T(8,128)(2,1)S(1)}, u32[]{:S(2)}, u32[]{:S(2)}) collective-permute-start(bf16[128,768]{1,0:T(8,128)(2,1)S(1)} %get-tuple-element.49), channel_id=1, source_target_pairs={{0,2},{2,0},{4,6},{6,4},{1,3},{3,1},{5,7},{7,5},{8,10},{10,8},{12,... | collective-permute-start | bytes 589832 | tf_op jit(solution)/shard_map/ppermute | solution.py:45
  60.5 9.7 %collective-permute-start.18 = (bf16[128,768]{1,0:T(8,128)(2,1)S(1)}, bf16[128,768]{1,0:T(8,128)(2,1)S(1)}, u32[]{:S(2)}, u32[]{:S(2)}) collective-permute-start(bf16[128,768]{1,0:T(8,128)(2,1)S(1)} %get-tuple-element.46.sent), channel_id=1, source_target_pairs={{0,2},{2,0},{4,6},{6,4},{1,3},{3,1},{5,7},{7,5},{8,10},{10,8},{12,... | collective-permute-start | bytes 589832 | tf_op jit(solution)/shard_map/ppermute | solution.py:45
  64.4 5.7 %collective-permute-start.23 = (bf16[128,768]{1,0:T(8,128)(2,1)S(1)}, bf16[128,768]{1,0:T(8,128)(2,1)S(1)}, u32[]{:S(2)}, u32[]{:S(2)}) collective-permute-start(bf16[128,768]{1,0:T(8,128)(2,1)S(1)} %add_convert_fusion), channel_id=1, source_target_pairs={{0,2},{2,0},{4,6},{6,4},{1,3},{3,1},{5,7},{7,5},{8,10},{10,8},{12,... | collective-permute-start | bytes 589832 | tf_op jit(solution)/shard_map/ppermute | solution.py:45
  65.5 5.7 %collective-permute-start.20 = (bf16[128,768]{1,0:T(8,128)(2,1)S(1)}, bf16[128,768]{1,0:T(8,128)(2,1)S(1)}, u32[]{:S(2)}, u32[]{:S(2)}) collective-permute-start(bf16[128,768]{1,0:T(8,128)(2,1)S(1)} %add_convert_fusion.1), channel_id=1, source_target_pairs={{0,4},{2,6},{4,0},{6,2},{1,5},{3,7},{5,1},{7,3},{8,12},{10,14},{12... | collective-permute-start | bytes 589832 | tf_op jit(solution)/shard_map/ppermute | solution.py:45
  (18 other events, 98.3 us)

commit v6 on v5

--- a/solution.py
+++ b/solution.py
@@ -74,7 +74,7 @@
     return v * cos + pltpu.roll(v, HD // 2, 1) * sin
 
 
-def pack_kernel(from_x, from_y, rim, *refs):
+def pack_kernel(from_y, from_x, rim, *refs):
     to_y, to_x = refs[-2:]
     half = to_y.shape[0] - RIM
     to_y[:half, :] = from_x[:half]
@@ -132,7 +132,10 @@
 
 def steps_kernel(dt_bias, a_log, normed, w_inner, w_dt, x_in, steps, cumulative):
     tokens = steps.shape[1]
-    x_in[...] = dot(normed[...], w_inner[1]).astype(bf16)
+    part = normed.shape[1] // 4
+    x_in[...] = sum(
+        dot(normed[:, at : at + part], w_inner[1, at : at + part]) for at in range(0, 4 * part, part)
+    ).astype(bf16)
     raw = jnp.concatenate([dot_nt(w_dt[...], normed[RIM:, :]), jnp.zeros((5, tokens), f32)], axis=0)
     head = lax.broadcasted_iota(jnp.int32, (8, tokens), 0)
     bias = jnp.zeros((8, tokens), f32)
@@ -414,7 +417,7 @@
 
     to_y, to_x = call(
         pack_kernel, (shape(half + RIM, width), shape(half + RIM, width)), 0, 3, 3
-    )(from_x, from_y, rim)
+    )(from_y, from_x, rim)
     by_y = swap(to_y, 2)
     by_x = swap(to_x, 1)
     diag_rim = swap(rim, 3)

time: 72.3 us -> 72.3 us (level)
  no operation moved by 1% of the time
where the time goes in v6:
time: 72.3 us; the launch traced here: 72.1 us
  starting transfers between devices  32.3 us (45%)
  Pallas kernels  18.6 us (26%)
  waiting for transfers between devices  13.9 us (19%)
  local copies, waits for them, and re-layouts  3.97 us (5%)
  other arithmetic  1.79 us (2%)
  between operations  1.67 us (2%)
    ppermute x18, starting transfers between devices, swap(): lax.ppermute(block, 'mp', [(i, i ^ turn) for i in range(lax.axis_size('mp...  22 us
    ppermute x18, waiting for transfers between devices, swap(): lax.ppermute(block, 'mp', [(i, i ^ turn) for i in range(lax.axis_size('mp...  8.87 us
    ppermute x5, starting transfers between devices, cross(): lax.ppermute(block, 'seq', [(i, i ^ turn) for i in range(lax.axis_size('s...  8.66 us
    pallas_call x1, Pallas kernels, shards(): call(functools.partial(attention_kernel, cache_rows=cache_rows, scale=HD...  3.72 us
    unnamed x37, local copies, waits for them, and re-layouts  3.19 us
    ppermute x1, waiting for transfers between devices, ahead(): lax.ppermute(block, 'seq', [(i, (i + 1) % count) for i in range(count)])  2.68 us
    pallas_call x1, Pallas kernels, shards(): call(norm_kernel, (shape(RIM + tokens, 4 * width), shape(RIM + tokens, w_...  2.48 us
    pallas_call x1, Pallas kernels, shards(): call(steps_kernel, (shape(RIM + tokens, inner_width), shape(8, tokens, dt...  2.35 us
  transfers between devices with their start and end apart: 24, of which 9 were waited for; matrix products, arithmetic and copies ran while one was open for 7% of the time, Pallas kernels for 20%

profile of v6, /device:TPU:0, one launch (start us, length us, event | category | flops | bytes accessed | tf_op | source)
XLA Modules:
  0.0 72.1 jit_solution(1800103847759200882)
XLA Ops:
  0.6 3.0 %collective-permute-start = (bf16[256,768]{1,0:T(8,128)(2,1)}, bf16[256,768]{1,0:T(8,128)(2,1)S(1)}, u32[]{:S(2)}, u32[]{:S(2)}) collective-permute-start(bf16[256,768]{1,0:T(8,128)(2,1)} %bitcast.21), channel_id=1, source_target_pairs={{0,2},{2,0},{4,6},{6,4},{1,3},{3,1},{5,7},{7,5},{8,10},{10,8},{12,... | collective-permute-start | bytes 1179656 | tf_op jit(solution)/shard_map/ppermute | solution.py:45
  3.6 1.5 %collective-permute-start.1 = (bf16[256,768]{1,0:T(8,128)(2,1)}, bf16[256,768]{1,0:T(8,128)(2,1)S(1)}, u32[]{:S(2)}, u32[]{:S(2)}) collective-permute-start(bf16[256,768]{1,0:T(8,128)(2,1)} %bitcast.22), channel_id=1, source_target_pairs={{0,4},{2,6},{4,0},{6,2},{1,5},{3,7},{5,1},{7,3},{8,12},{10,14},{12... | collective-permute-start | bytes 1179656 | tf_op jit(solution)/shard_map/ppermute | solution.py:45
  5.9 1.6 %collective-permute-start.2 = (bf16[16,768]{1,0:T(8,128)(2,1)S(1)}, bf16[16,768]{1,0:T(8,128)(2,1)S(1)}, u32[]{:S(2)}, u32[]{:S(2)}) collective-permute-start(bf16[16,768]{1,0:T(8,128)(2,1)S(1)} %slice_bitcast_fusion), channel_id=1, source_target_pairs={{0,8},{8,16},{16,24},{24,0},{1,9},{9,17},{17,25},{25,1},{2,10},{10... | collective-permute-start | bytes 73736 | tf_op jit(solution)/shard_map/ppermute | solution.py:54
  8.9 2.7 %collective-permute-done.2.rim = bf16[16,768]{1,0:T(8,128)(2,1)S(1)} collective-permute-done((bf16[16,768]{1,0:T(8,128)(2,1)S(1)}, bf16[16,768]{1,0:T(8,128)(2,1)S(1)}, u32[]{:S(2)}, u32[]{:S(2)}) %collective-permute-start.2) | collective-permute-done | bytes 24608 | tf_op jit(solution)/shard_map/ppermute | solution.py:54
  13.0 1.5 %collective-permute-done.1.from_y = bf16[256,768]{1,0:T(8,128)(2,1)S(1)} collective-permute-done((bf16[256,768]{1,0:T(8,128)(2,1)}, bf16[256,768]{1,0:T(8,128)(2,1)S(1)}, u32[]{:S(2)}, u32[]{:S(2)}) %collective-permute-start.1) | collective-permute-done | bytes 393248 | tf_op jit(solution)/shard_map/ppermute | solution.py:45
  14.5 1.6 %collective-permute-start.3 = (bf16[144,768]{1,0:T(8,128)(2,1)S(1)}, bf16[144,768]{1,0:T(8,128)(2,1)S(1)}, u32[]{:S(2)}, u32[]{:S(2)}) collective-permute-start(bf16[144,768]{1,0:T(8,128)(2,1)S(1)} %get-tuple-element.29), channel_id=1, source_target_pairs={{0,4},{2,6},{4,0},{6,2},{1,5},{3,7},{5,1},{7,3},{8,12},{10,14},{12... | collective-permute-start | bytes 663560 | tf_op jit(solution)/shard_map/ppermute | solution.py:45
  16.6 1.4 %collective-permute-start.5 = (bf16[16,768]{1,0:T(8,128)(2,1)S(1)}, bf16[16,768]{1,0:T(8,128)(2,1)S(1)}, u32[]{:S(2)}, u32[]{:S(2)}) collective-permute-start(bf16[16,768]{1,0:T(8,128)(2,1)S(1)} %collective-permute-done.2.rim), channel_id=1, source_target_pairs={{0,6},{2,4},{4,2},{6,0},{1,7},{3,5},{5,3},{7,1},{8,14},{10,12},{12... | collective-permute-start | bytes 73736 | tf_op jit(solution)/shard_map/ppermute | solution.py:45
  18.2 3.1 %copy.25 = bf16[3072,2,384]{2,0,1:T(8,128)(2,1)S(1)} copy(bf16[3072,2,384]{2,1,0:T(2,128)(2,1)} %param.25) | data formatting | bytes 9437184 | tf_op args[5]
  22.3 2.5 %shard_map.212 = (bf16[272,3072]{1,0:T(8,128)(2,1)S(1)}, bf16[272,128]{1,0:T(8,128)(2,1)S(1)}, bf16[256,128]{1,0:T(8,128)(2,1)}, bf16[512,128]{1,0:T(8,128)(2,1)S(1)}) custom-call(s32[3]{0:T(128)S(1)} %pad_add_fusion.place, bf16[256,768]{1,0:T(8,128)(2,1)S(1)} %bitcast.23, bf16[256,768]{1,0:T(8,128)(2,1)S(1)} %collective-permute-done.from_x, ...), custom_call_target="tpu_custom_call" | custom-call | flops 3000000000 | tf_op jit(solution)/shard_map/pallas_call | solution.py:426
  25.5 1.4 %collective-permute-start.7 = (bf16[272,128]{1,0:T(8,128)(2,1)S(1)}, bf16[272,128]{1,0:T(8,128)(2,1)S(1)}, u32[]{:S(2)}, u32[]{:S(2)}) collective-permute-start(bf16[272,128]{1,0:T(8,128)(2,1)S(1)} %get-tuple-element.33.bc0), channel_id=1, source_target_pairs={{0,4},{2,6},{4,0},{6,2},{1,5},{3,7},{5,1},{7,3},{8,12},{10,14},{12... | collective-permute-start | bytes 208904 | tf_op jit(solution)/shard_map/ppermute | solution.py:45
  28.3 1.6 %collective-permute-start.9 = (bf16[512,128]{1,0:T(8,128)(2,1)S(1)}, bf16[512,128]{1,0:T(8,128)(2,1)S(1)}, u32[]{:S(2)}, u32[]{:S(2)}) collective-permute-start(bf16[512,128]{1,0:T(8,128)(2,1)S(1)} %get-tuple-element.38.refs_0_), channel_id=1, source_target_pairs={{0,8},{8,0},{16,24},{24,16},{1,9},{9,1},{17,25},{25,17},{2,10},{10... | collective-permute-start | bytes 393224 | tf_op jit(solution)/shard_map/ppermute | solution.py:49
  29.8 2.6 %collective-permute-start.10 = (bf16[512,128]{1,0:T(8,128)(2,1)S(1)}, bf16[512,128]{1,0:T(8,128)(2,1)S(1)}, u32[]{:S(2)}, u32[]{:S(2)}) collective-permute-start(bf16[512,128]{1,0:T(8,128)(2,1)S(1)} %get-tuple-element.38.refs_0_), channel_id=1, source_target_pairs={{0,16},{8,24},{16,0},{24,8},{1,17},{9,25},{17,1},{25,9},{2,18},{10... | collective-permute-start | bytes 393224 | tf_op jit(solution)/shard_map/ppermute | solution.py:49
  32.5 2.3 %shard_map.213 = (bf16[272,384]{1,0:T(8,128)(2,1)S(1)}, f32[8,256]{1,0:T(8,128)S(1)}, f32[8,256]{1,0:T(8,128)S(1)}) custom-call(f32[3]{0:T(128)S(1)} %copy-done.13, f32[3]{0:T(128)S(1)} %copy-done.14, bf16[272,3072]{1,0:T(8,128)(2,1)S(1)} %get-tuple-element.31.normed, bf16[2,3072,384]{2,1,0:T(8,128)(2,1)S(1)} %bitcast.19, bf16[3,3072]{1,0:T(4,128)(2,1)S(1)} %bitcast.27), custom_call_target="tpu_custom_call" | custom-call | flops 2000000000 | tf_op jit(solution)/shard_map/pallas_call | solution.py:445
  35.8 1.9 %shard_map.214 = (f32[384,256]{1,0:T(8,128)S(1)}, bf16[416,256]{1,0:T(8,128)(2,1)S(1)}, bf16[256,384]{1,0:T(8,128)(2,1)S(1)}, bf16[256,256]{1,0:T(8,128)(2,1)S(1)}, bf16[256,256]{1,0:T(8,128)(2,1)S(1)}) custom-call(s32[3]{0:T(128)S(1)} %pad_add_fusion.place, bf16[272,384]{1,0:T(8,128)(2,1)S(1)} %get-tuple-element.32.x_in, ...), custom_call_target="tpu_custom_call" | custom-call | flops 2000000000 | tf_op jit(solution)/shard_map/pallas_call | solution.py:463
  38.4 1.5 %shard_map.215 = (bf16[256,256]{1,0:T(8,128)(2,1)S(1)}, bf16[256,384]{1,0:T(8,128)(2,1)S(1)}) custom-call(bf16[272,3072]{1,0:T(8,128)(2,1)S(1)} %get-tuple-element.31.normed, bf16[3072,256]{1,0:T(8,128)(2,1)S(1)} %copy-done.2, bf16[2,3072,384]{2,1,0:T(8,128)(2,1)S(1)} %bitcast.20, f32[256,128]{1,0:T(8,128)S(1)} %get-tuple-element.56.cos, ...), custom_call_target="tpu_custom_call" | custom-call | flops 2000000000 | tf_op jit(solution)/shard_map/pallas_call | solution.py:504
  40.0 1.4 %collective-permute-start.13 = (bf16[512,128]{1,0:T(8,128)(2,1)S(1)}, bf16[512,128]{1,0:T(8,128)(2,1)S(1)}, u32[]{:S(2)}, u32[]{:S(2)}) collective-permute-start(bf16[512,128]{1,0:T(8,128)(2,1)S(1)} %collective-permute-done.9.refs_1_), channel_id=1, source_target_pairs={{0,2},{2,0},{4,6},{6,4},{1,3},{3,1},{5,7},{7,5},{8,10},{10,8},{12,... | collective-permute-start | bytes 393224 | tf_op jit(solution)/shard_map/ppermute | solution.py:45
  45.2 3.6 %collective-permute-start.17 = (bf16[416,256]{1,0:T(8,128)(2,1)S(1)}, bf16[416,256]{1,0:T(8,128)(2,1)S(1)}, u32[]{:S(2)}, u32[]{:S(2)}) collective-permute-start(bf16[416,256]{1,0:T(8,128)(2,1)S(1)} %shard_map.217), channel_id=1, source_target_pairs={{0,16},{8,24},{16,0},{24,8},{1,17},{9,25},{17,1},{25,9},{2,18},{10... | collective-permute-start | bytes 638984 | tf_op jit(solution)/shard_map/ppermute | solution.py:49
  48.8 3.7 %shard_map.216.attended = bf16[256,256]{1,0:T(8,128)(2,1)S(1)} custom-call(s32[3]{0:T(128)S(1)} %pad_add_fusion.place, s32[1]{0:T(128)} %copy.26.length, bf16[256,256]{1,0:T(8,128)(2,1)S(1)} %get-tuple-element.37.query, bf16[512,128]{1,0:T(8,128)(2,1)S(1)} %get-tuple-element.38.refs_0_, bf16[512,128]{1,0:T(8,128)(2,1)S(1)} %collective-permute-done.9.refs_1_, ...), custom_call_target="tpu_custom_call" | custom-call | flops 6000000000 | tf_op jit(solution)/shard_map/pallas_call | solution.py:517
  52.5 2.3 %collective-permute-done.17.far = bf16[416,256]{1,0:T(8,128)(2,1)S(1)} collective-permute-done((bf16[416,256]{1,0:T(8,128)(2,1)S(1)}, bf16[416,256]{1,0:T(8,128)(2,1)S(1)}, u32[]{:S(2)}, u32[]{:S(2)}) %collective-permute-start.17) | collective-permute-done | bytes 213024 | tf_op jit(solution)/shard_map/ppermute | solution.py:49
  54.9 1.7 %shard_map.219 = (f32[384,256]{1,0:T(8,128)S(1)}, bf16[256,384]{1,0:T(8,128)(2,1)S(1)}, bf16[128,768]{1,0:T(8,128)(2,1)S(1)}, bf16[128,768]{1,0:T(8,128)(2,1)S(1)}) custom-call(s32[3]{0:T(128)S(1)} %pad_add_fusion.1.place, bf16[416,256]{1,0:T(8,128)(2,1)S(1)} %collective-permute-done.16.second.near, bf16[416,256]{1,0:T(8,128)(2,1)S(1)} %collective-permute-done.17.far, ...), custom_call_target="tpu_custom_call" | custom-call | flops 3000000000 | tf_op jit(solution)/shard_map/pallas_call | solution.py:546
  56.6 1.6 %collective-permute-start.22 = (bf16[128,768]{1,0:T(8,128)(2,1)S(1)}, bf16[128,768]{1,0:T(8,128)(2,1)S(1)}, u32[]{:S(2)}, u32[]{:S(2)}) collective-permute-start(bf16[128,768]{1,0:T(8,128)(2,1)S(1)} %get-tuple-element.52), channel_id=1, source_target_pairs={{0,4},{2,6},{4,0},{6,2},{1,5},{3,7},{5,1},{7,3},{8,12},{10,14},{12... | collective-permute-start | bytes 589832 | tf_op jit(solution)/shard_map/ppermute | solution.py:45
  61.8 2.1 %shard_map.221 = (f32[256,768]{1,0:T(8,128)S(1)}, f32[128,768]{1,0:T(8,128)S(1)}, f32[128,768]{1,0:T(8,128)S(1)}, f32[1,1,3,128,256]{4,3,2,1,0:T(8,128)}) custom-call(s32[3]{0:T(128)S(1)} %pad_add_fusion.place, bf16[256,256]{1,0:T(8,128)(2,1)S(1)} %shard_map.216.attended, bf16[256,384]{1,0:T(8,128)(2,1)S(1)} %get-tuple-element.43.mixed, ...), custom_call_target="tpu_custom_call" | custom-call | flops 1000000000 | tf_op jit(solution)/shard_map/pallas_call | solution.py:567
  65.5 1.6 %collective-permute-start.20 = (bf16[128,768]{1,0:T(8,128)(2,1)S(1)}, bf16[128,768]{1,0:T(8,128)(2,1)S(1)}, u32[]{:S(2)}, u32[]{:S(2)}) collective-permute-start(bf16[128,768]{1,0:T(8,128)(2,1)S(1)} %add_convert_fusion.1), channel_id=1, source_target_pairs={{0,4},{2,6},{4,0},{6,2},{1,5},{3,7},{5,1},{7,3},{8,12},{10,14},{12... | collective-permute-start | bytes 589832 | tf_op jit(solution)/shard_map/ppermute | solution.py:45
  67.1 3.0 %collective-permute-done.23 = bf16[128,768]{1,0:T(8,128)(2,1)S(1)} collective-permute-done((bf16[128,768]{1,0:T(8,128)(2,1)S(1)}, bf16[128,768]{1,0:T(8,128)(2,1)S(1)}, u32[]{:S(2)}, u32[]{:S(2)}) %collective-permute-start.23) | collective-permute-done | bytes 196640 | tf_op jit(solution)/shard_map/ppermute | solution.py:45
  (87 shorter events, 19.2 us)
Async XLA Ops:
  0.6 12.3 %collective-permute-start = (bf16[256,768]{1,0:T(8,128)(2,1)}, bf16[256,768]{1,0:T(8,128)(2,1)S(1)}, u32[]{:S(2)}, u32[]{:S(2)}) collective-permute-start(bf16[256,768]{1,0:T(8,128)(2,1)} %bitcast.21), channel_id=1, source_target_pairs={{0,2},{2,0},{4,6},{6,4},{1,3},{3,1},{5,7},{7,5},{8,10},{10,8},{12,... | collective-permute-start | bytes 1179656 | tf_op jit(solution)/shard_map/ppermute | solution.py:45
  3.6 10.8 %collective-permute-start.1 = (bf16[256,768]{1,0:T(8,128)(2,1)}, bf16[256,768]{1,0:T(8,128)(2,1)S(1)}, u32[]{:S(2)}, u32[]{:S(2)}) collective-permute-start(bf16[256,768]{1,0:T(8,128)(2,1)} %bitcast.22), channel_id=1, source_target_pairs={{0,4},{2,6},{4,0},{6,2},{1,5},{3,7},{5,1},{7,3},{8,12},{10,14},{12... | collective-permute-start | bytes 1179656 | tf_op jit(solution)/shard_map/ppermute | solution.py:45
  5.9 5.6 %collective-permute-start.2 = (bf16[16,768]{1,0:T(8,128)(2,1)S(1)}, bf16[16,768]{1,0:T(8,128)(2,1)S(1)}, u32[]{:S(2)}, u32[]{:S(2)}) collective-permute-start(bf16[16,768]{1,0:T(8,128)(2,1)S(1)} %slice_bitcast_fusion), channel_id=1, source_target_pairs={{0,8},{8,16},{16,24},{24,0},{1,9},{9,17},{17,25},{25,1},{2,10},{10... | collective-permute-start | bytes 73736 | tf_op jit(solution)/shard_map/ppermute | solution.py:54
  14.5 7.8 %collective-permute-start.3 = (bf16[144,768]{1,0:T(8,128)(2,1)S(1)}, bf16[144,768]{1,0:T(8,128)(2,1)S(1)}, u32[]{:S(2)}, u32[]{:S(2)}) collective-permute-start(bf16[144,768]{1,0:T(8,128)(2,1)S(1)} %get-tuple-element.29), channel_id=1, source_target_pairs={{0,4},{2,6},{4,0},{6,2},{1,5},{3,7},{5,1},{7,3},{8,12},{10,14},{12... | collective-permute-start | bytes 663560 | tf_op jit(solution)/shard_map/ppermute | solution.py:45
  16.0 6.2 %collective-permute-start.4 = (bf16[144,768]{1,0:T(8,128)(2,1)S(1)}, bf16[144,768]{1,0:T(8,128)(2,1)S(1)}, u32[]{:S(2)}, u32[]{:S(2)}) collective-permute-start(bf16[144,768]{1,0:T(8,128)(2,1)S(1)} %get-tuple-element.30), channel_id=1, source_target_pairs={{0,2},{2,0},{4,6},{6,4},{1,3},{3,1},{5,7},{7,5},{8,10},{10,8},{12,... | collective-permute-start | bytes 663560 | tf_op jit(solution)/shard_map/ppermute | solution.py:45
  16.6 5.6 %collective-permute-start.5 = (bf16[16,768]{1,0:T(8,128)(2,1)S(1)}, bf16[16,768]{1,0:T(8,128)(2,1)S(1)}, u32[]{:S(2)}, u32[]{:S(2)}) collective-permute-start(bf16[16,768]{1,0:T(8,128)(2,1)S(1)} %collective-permute-done.2.rim), channel_id=1, source_target_pairs={{0,6},{2,4},{4,2},{6,0},{1,7},{3,5},{5,3},{7,1},{8,14},{10,12},{12... | collective-permute-start | bytes 73736 | tf_op jit(solution)/shard_map/ppermute | solution.py:45
  24.8 10.1 %collective-permute-start.6 = (bf16[272,128]{1,0:T(8,128)(2,1)S(1)}, bf16[272,128]{1,0:T(8,128)(2,1)S(1)}, u32[]{:S(2)}, u32[]{:S(2)}) collective-permute-start(bf16[272,128]{1,0:T(8,128)(2,1)S(1)} %get-tuple-element.33.bc0), channel_id=1, source_target_pairs={{0,2},{2,0},{4,6},{6,4},{1,3},{3,1},{5,7},{7,5},{8,10},{10,8},{12,... | collective-permute-start | bytes 208904 | tf_op jit(solution)/shard_map/ppermute | solution.py:45
  25.5 9.6 %collective-permute-start.7 = (bf16[272,128]{1,0:T(8,128)(2,1)S(1)}, bf16[272,128]{1,0:T(8,128)(2,1)S(1)}, u32[]{:S(2)}, u32[]{:S(2)}) collective-permute-start(bf16[272,128]{1,0:T(8,128)(2,1)S(1)} %get-tuple-element.33.bc0), channel_id=1, source_target_pairs={{0,4},{2,6},{4,0},{6,2},{1,5},{3,7},{5,1},{7,3},{8,12},{10,14},{12... | collective-permute-start | bytes 208904 | tf_op jit(solution)/shard_map/ppermute | solution.py:45
  26.9 8.9 %collective-permute-start.8 = (bf16[272,128]{1,0:T(8,128)(2,1)S(1)}, bf16[272,128]{1,0:T(8,128)(2,1)S(1)}, u32[]{:S(2)}, u32[]{:S(2)}) collective-permute-start(bf16[272,128]{1,0:T(8,128)(2,1)S(1)} %get-tuple-element.33.bc0), channel_id=1, source_target_pairs={{0,6},{2,4},{4,2},{6,0},{1,7},{3,5},{5,3},{7,1},{8,14},{10,12},{12... | collective-permute-start | bytes 208904 | tf_op jit(solution)/shard_map/ppermute | solution.py:45
  28.3 11.7 %collective-permute-start.9 = (bf16[512,128]{1,0:T(8,128)(2,1)S(1)}, bf16[512,128]{1,0:T(8,128)(2,1)S(1)}, u32[]{:S(2)}, u32[]{:S(2)}) collective-permute-start(bf16[512,128]{1,0:T(8,128)(2,1)S(1)} %get-tuple-element.38.refs_0_), channel_id=1, source_target_pairs={{0,8},{8,0},{16,24},{24,16},{1,9},{9,1},{17,25},{25,17},{2,10},{10... | collective-permute-start | bytes 393224 | tf_op jit(solution)/shard_map/ppermute | solution.py:49
  29.8 11.6 %collective-permute-start.10 = (bf16[512,128]{1,0:T(8,128)(2,1)S(1)}, bf16[512,128]{1,0:T(8,128)(2,1)S(1)}, u32[]{:S(2)}, u32[]{:S(2)}) collective-permute-start(bf16[512,128]{1,0:T(8,128)(2,1)S(1)} %get-tuple-element.38.refs_0_), channel_id=1, source_target_pairs={{0,16},{8,24},{16,0},{24,8},{1,17},{9,25},{17,1},{25,9},{2,18},{10... | collective-permute-start | bytes 393224 | tf_op jit(solution)/shard_map/ppermute | solution.py:49
  34.8 7.2 %collective-permute-start.11 = (bf16[512,128]{1,0:T(8,128)(2,1)S(1)}, bf16[512,128]{1,0:T(8,128)(2,1)S(1)}, u32[]{:S(2)}, u32[]{:S(2)}) collective-permute-start(bf16[512,128]{1,0:T(8,128)(2,1)S(1)} %get-tuple-element.38.refs_0_), channel_id=1, source_target_pairs={{0,24},{8,16},{16,8},{24,0},{1,25},{9,17},{17,9},{25,1},{2,26},{10... | collective-permute-start | bytes 393224 | tf_op jit(solution)/shard_map/ppermute | solution.py:49
  35.1 13.7 %collective-permute-start.12 = (bf16[512,128]{1,0:T(8,128)(2,1)S(1)}, bf16[512,128]{1,0:T(8,128)(2,1)S(1)}, u32[]{:S(2)}, u32[]{:S(2)}) collective-permute-start(bf16[512,128]{1,0:T(8,128)(2,1)S(1)} %get-tuple-element.38.refs_0_), channel_id=1, source_target_pairs={{0,2},{2,0},{4,6},{6,4},{1,3},{3,1},{5,7},{7,5},{8,10},{10,8},{12,... | collective-permute-start | bytes 393224 | tf_op jit(solution)/shard_map/ppermute | solution.py:45
  37.7 6.8 %collective-permute-start.16 = (bf16[416,256]{1,0:T(8,128)(2,1)S(1)}, bf16[416,256]{1,0:T(8,128)(2,1)S(1)}, u32[]{:S(2)}, u32[]{:S(2)}) collective-permute-start(bf16[416,256]{1,0:T(8,128)(2,1)S(1)} %get-tuple-element.39.first), channel_id=1, source_target_pairs={{0,8},{8,0},{16,24},{24,16},{1,9},{9,1},{17,25},{25,17},{2,10},{10... | collective-permute-start | bytes 638984 | tf_op jit(solution)/shard_map/ppermute | solution.py:49
  40.0 8.8 %collective-permute-start.13 = (bf16[512,128]{1,0:T(8,128)(2,1)S(1)}, bf16[512,128]{1,0:T(8,128)(2,1)S(1)}, u32[]{:S(2)}, u32[]{:S(2)}) collective-permute-start(bf16[512,128]{1,0:T(8,128)(2,1)S(1)} %collective-permute-done.9.refs_1_), channel_id=1, source_target_pairs={{0,2},{2,0},{4,6},{6,4},{1,3},{3,1},{5,7},{7,5},{8,10},{10,8},{12,... | collective-permute-start | bytes 393224 | tf_op jit(solution)/shard_map/ppermute | solution.py:45
  41.4 7.3 %collective-permute-start.14 = (bf16[512,128]{1,0:T(8,128)(2,1)S(1)}, bf16[512,128]{1,0:T(8,128)(2,1)S(1)}, u32[]{:S(2)}, u32[]{:S(2)}) collective-permute-start(bf16[512,128]{1,0:T(8,128)(2,1)S(1)} %collective-permute-done.10.refs_2_), channel_id=1, source_target_pairs={{0,2},{2,0},{4,6},{6,4},{1,3},{3,1},{5,7},{7,5},{8,10},{10,8},{12,... | collective-permute-start | bytes 393224 | tf_op jit(solution)/shard_map/ppermute | solution.py:45
  42.1 6.7 %collective-permute-start.15 = (bf16[512,128]{1,0:T(8,128)(2,1)S(1)}, bf16[512,128]{1,0:T(8,128)(2,1)S(1)}, u32[]{:S(2)}, u32[]{:S(2)}) collective-permute-start(bf16[512,128]{1,0:T(8,128)(2,1)S(1)} %collective-permute-done.11.refs_3_), channel_id=1, source_target_pairs={{0,2},{2,0},{4,6},{6,4},{1,3},{3,1},{5,7},{7,5},{8,10},{10,8},{12,... | collective-permute-start | bytes 393224 | tf_op jit(solution)/shard_map/ppermute | solution.py:45
  45.2 9.7 %collective-permute-start.17 = (bf16[416,256]{1,0:T(8,128)(2,1)S(1)}, bf16[416,256]{1,0:T(8,128)(2,1)S(1)}, u32[]{:S(2)}, u32[]{:S(2)}) collective-permute-start(bf16[416,256]{1,0:T(8,128)(2,1)S(1)} %shard_map.217), channel_id=1, source_target_pairs={{0,16},{8,24},{16,0},{24,8},{1,17},{9,25},{17,1},{25,9},{2,18},{10... | collective-permute-start | bytes 638984 | tf_op jit(solution)/shard_map/ppermute | solution.py:49
  56.6 7.8 %collective-permute-start.22 = (bf16[128,768]{1,0:T(8,128)(2,1)S(1)}, bf16[128,768]{1,0:T(8,128)(2,1)S(1)}, u32[]{:S(2)}, u32[]{:S(2)}) collective-permute-start(bf16[128,768]{1,0:T(8,128)(2,1)S(1)} %get-tuple-element.52), channel_id=1, source_target_pairs={{0,4},{2,6},{4,0},{6,2},{1,5},{3,7},{5,1},{7,3},{8,12},{10,14},{12... | collective-permute-start | bytes 589832 | tf_op jit(solution)/shard_map/ppermute | solution.py:45
  59.2 7.9 %collective-permute-start.21 = (bf16[128,768]{1,0:T(8,128)(2,1)S(1)}, bf16[128,768]{1,0:T(8,128)(2,1)S(1)}, u32[]{:S(2)}, u32[]{:S(2)}) collective-permute-start(bf16[128,768]{1,0:T(8,128)(2,1)S(1)} %get-tuple-element.50), channel_id=1, source_target_pairs={{0,4},{2,6},{4,0},{6,2},{1,5},{3,7},{5,1},{7,3},{8,12},{10,14},{12... | collective-permute-start | bytes 589832 | tf_op jit(solution)/shard_map/ppermute | solution.py:45
  59.8 5.7 %collective-permute-start.19 = (bf16[128,768]{1,0:T(8,128)(2,1)S(1)}, bf16[128,768]{1,0:T(8,128)(2,1)S(1)}, u32[]{:S(2)}, u32[]{:S(2)}) collective-permute-start(bf16[128,768]{1,0:T(8,128)(2,1)S(1)} %get-tuple-element.49), channel_id=1, source_target_pairs={{0,2},{2,0},{4,6},{6,4},{1,3},{3,1},{5,7},{7,5},{8,10},{10,8},{12,... | collective-permute-start | bytes 589832 | tf_op jit(solution)/shard_map/ppermute | solution.py:45
  60.5 9.7 %collective-permute-start.18 = (bf16[128,768]{1,0:T(8,128)(2,1)S(1)}, bf16[128,768]{1,0:T(8,128)(2,1)S(1)}, u32[]{:S(2)}, u32[]{:S(2)}) collective-permute-start(bf16[128,768]{1,0:T(8,128)(2,1)S(1)} %get-tuple-element.46.sent), channel_id=1, source_target_pairs={{0,2},{2,0},{4,6},{6,4},{1,3},{3,1},{5,7},{7,5},{8,10},{10,8},{12,... | collective-permute-start | bytes 589832 | tf_op jit(solution)/shard_map/ppermute | solution.py:45
  64.4 5.7 %collective-permute-start.23 = (bf16[128,768]{1,0:T(8,128)(2,1)S(1)}, bf16[128,768]{1,0:T(8,128)(2,1)S(1)}, u32[]{:S(2)}, u32[]{:S(2)}) collective-permute-start(bf16[128,768]{1,0:T(8,128)(2,1)S(1)} %add_convert_fusion), channel_id=1, source_target_pairs={{0,2},{2,0},{4,6},{6,4},{1,3},{3,1},{5,7},{7,5},{8,10},{10,8},{12,... | collective-permute-start | bytes 589832 | tf_op jit(solution)/shard_map/ppermute | solution.py:45
  65.5 5.7 %collective-permute-start.20 = (bf16[128,768]{1,0:T(8,128)(2,1)S(1)}, bf16[128,768]{1,0:T(8,128)(2,1)S(1)}, u32[]{:S(2)}, u32[]{:S(2)}) collective-permute-start(bf16[128,768]{1,0:T(8,128)(2,1)S(1)} %add_convert_fusion.1), channel_id=1, source_target_pairs={{0,4},{2,6},{4,0},{6,2},{1,5},{3,7},{5,1},{7,3},{8,12},{10,14},{12... | collective-permute-start | bytes 589832 | tf_op jit(solution)/shard_map/ppermute | solution.py:45
  (18 other events, 98.3 us)
